TPU v7x, 32 devices: a whole 2x2x4 slice. The times are simulated.
32 devices in a mesh: grp: 4 (over x, core), row: 2 (over y), col: 4 (over z).
Axes of the slice: x: 2, y: 2, z: 4, core: 2. Of those that a mesh axis runs over, the one named last changes fastest.
Arguments:
- velocity: float32 [3, 4, 1024, 1024], P(None, 'col', ('grp', 'row')), may hold values from -8 to 8
- profile: int32 [4], P('col'), may hold values from 0 to 1
- x_filters: bfloat16 [2, 1024, 1024], replicated, may hold values from 0 to 1
- z_filter: bfloat16 [1024, 1024], replicated, may hold values from 0 to 1
Outputs:
- stress: float32 [6, 4, 1024, 1024], P(None, 'col', ('grp', 'row'))
All inputs are finite; a program needn't handle non-finite values.
Results may differ from a plain program's by a relative error of at most 0.0031.
Values may be sent and summed in bfloat16 or wider, within the bound.
No kernel may reach another device: no remote copies, remote signals or barrier semaphores. Data moves between devices by JAX's collectives and lax.ppermute only.
A program may use at most 64 MiB of HBM per device.

v0:
```python
import jax
import jax.numpy as jnp
from jax import lax
from jax.sharding import PartitionSpec as P

STEP_SIZE = 0.25
VISCOSITY = 0.8
PRODUCT_PAIRS = ((0, 0), (0, 1), (0, 2), (1, 1), (1, 2), (2, 2))


def extended(cells, sides, width):
    for axis, dim in sides:
        count = lax.axis_size(axis)
        head = lax.slice_in_dim(cells, 0, width, axis=dim)
        tail = lax.slice_in_dim(cells, cells.shape[dim] - width, cells.shape[dim], axis=dim)
        cells = jnp.concatenate(
            [
                lax.ppermute(tail, axis, [(i, (i + 1) % count) for i in range(count)]),
                cells,
                lax.ppermute(head, axis, [((i + 1) % count, i) for i in range(count)]),
            ],
            axis=dim,
        )
    return cells


def wall_zero(padded, extent, y_rows):
    height = padded.shape[1]
    all_rows = y_rows * lax.axis_size("col")
    row_index = lax.axis_index("col") * y_rows + jnp.arange(height, dtype=jnp.int32) - extent
    inside = (row_index >= 0) & (row_index < all_rows)
    return padded * inside.astype(padded.dtype)[None, :, None, None]


def shrink_rate(padded):
    center = padded[:, 1:-1, 1:-1]
    y_next = padded[:, 2:, 1:-1]
    y_prev = padded[:, :-2, 1:-1]
    z_next = padded[:, 1:-1, 2:]
    z_prev = padded[:, 1:-1, :-2]
    x_next = jnp.roll(center, -1, axis=3)
    x_prev = jnp.roll(center, 1, axis=3)
    advect = (
        center[0] * (0.5 * (x_next - x_prev))
        + center[1] * (0.5 * (y_next - y_prev))
        + center[2] * (0.5 * (z_next - z_prev))
    )
    laplace = x_next + x_prev + y_next + y_prev + z_next + z_prev - 6.0 * center
    return VISCOSITY * laplace - advect


def z_apply(received, z_filter):
    return jnp.einsum("fyos,rs->fyor", received, z_filter, preferred_element_type=jnp.float32)


def body(velocity, profile, x_filters, z_filter):
    y_rows = velocity.shape[1]

    def extend(current):
        padded = extended(current, ((("grp", "row"), 2), ("col", 1)), 1)
        return wall_zero(padded, 1, y_rows)

    section_one = velocity + STEP_SIZE * shrink_rate(extend(velocity))
    section_two = 0.75 * velocity + 0.25 * (
        section_one + STEP_SIZE * shrink_rate(extend(section_one))
    )
    advanced = velocity / 3.0 + 2.0 / 3.0 * (
        section_two + STEP_SIZE * shrink_rate(extend(section_two))
    )
    components = [advanced[0], advanced[1], advanced[2]] + [
        advanced[left_comp] * advanced[right_comp] for left_comp, right_comp in PRODUCT_PAIRS
    ]
    fields = jnp.stack(components).astype(jnp.bfloat16)
    matrices = jnp.take(x_filters, profile, axis=0)
    x_pass = jnp.einsum(
        "yox,fyzx->fyoz", matrices, fields, preferred_element_type=jnp.float32
    ).astype(jnp.bfloat16)
    filtered = z_apply(
        lax.all_to_all(x_pass, ("grp", "row"), split_axis=2, concat_axis=3, tiled=True), z_filter
    )
    stress = jnp.stack(
        [
            filtered[3 + number] - filtered[left_comp] * filtered[right_comp]
            for number, (left_comp, right_comp) in enumerate(PRODUCT_PAIRS)
        ]
    )
    return stress


def solution(mesh):
    placed = (P(None, "col", ("grp", "row"), None), P("col"), P(), P())
    return jax.shard_map(
        body,
        mesh=mesh,
        in_specs=placed,
        out_specs=P(None, "col", ("grp", "row"), None),
        check_vma=False,
    )
```

profile of v0, /device:TPU:0, one launch (start us, length us, event | category | flops | bytes accessed | tf_op | source)
XLA Modules:
  0.0 336.8 jit_solution(11020882150510423220)
XLA Ops:
  0.0 1.1 fusion.71
  1.1 3.0 collective-permute-start
  4.1 0.4 collective-permute-start.1
  4.6 1.4 collective-permute-done
  5.9 1.9 collective-permute-done.1
  7.8 1.6 pad_maximum_fusion
  9.5 2.8 copy.6
  12.2 1.6 collective-permute-start.2
  13.8 2.2 collective-permute-start.3
  16.1 36.2 %collective-permute-done.2 = f32[3,1,130,1024]{3,1,2,0:T(1,128)} collective-permute-done((f32[3,1,130,1024]{3,1,2,0:T(1,128)}, f32[3,1,130,1024]{3,1,2,0:T(1,128)}, u32[]{:S(2)}, u32[]{:S(2)}) %collective-permute-start.2) | collective-permute-done | bytes 1597472 | tf_op jit(solution)/shard_map/ppermute | solution.py:18
  52.3 1.8 copy.8
  54.0 29.8 %collective-permute-done.3 = f32[3,1,130,1024]{3,1,2,0:T(1,128)} collective-permute-done((f32[3,1,130,1024]{3,1,2,0:T(1,128)}, f32[3,1,130,1024]{3,1,2,0:T(1,128)}, u32[]{:S(2)}, u32[]{:S(2)}) %collective-permute-start.3) | collective-permute-done | bytes 1597472 | tf_op jit(solution)/shard_map/ppermute | solution.py:20
  83.8 1.8 copy.9
  85.6 1.2 maximum_multiply_fusion
  86.8 0.3 fusion.47
  87.1 0.6 fusion.67
  87.7 0.1 fusion.68
  87.8 1.7 fusion.25
  89.6 2.1 collective-permute-start.4
  91.7 0.6 collective-permute-start.5
  92.3 1.4 collective-permute-done.4
  93.7 1.7 collective-permute-done.5
  95.4 0.3 pad_maximum_fusion.1
  95.7 1.6 copy.10
  97.3 1.1 collective-permute-start.6
  98.4 2.8 collective-permute-start.7
  101.2 35.9 %collective-permute-done.6 = f32[3,1,130,1024]{3,1,2,0:T(1,128)S(1)} collective-permute-done((f32[3,1,130,1024]{3,1,2,0:T(1,128)S(1)}, f32[3,1,130,1024]{3,1,2,0:T(1,128)S(1)}, u32[]{:S(2)}, u32[]{:S(2)}) %collective-permute-start.6) | collective-permute-done | bytes 1597472 | tf_op jit(solution)/shard_map/ppermute | solution.py:18
  137.1 0.3 copy.12
  137.5 31.2 %collective-permute-done.7 = f32[3,1,130,1024]{3,1,2,0:T(1,128)S(1)} collective-permute-done((f32[3,1,130,1024]{3,1,2,0:T(1,128)S(1)}, f32[3,1,130,1024]{3,1,2,0:T(1,128)S(1)}, u32[]{:S(2)}, u32[]{:S(2)}) %collective-permute-start.7) | collective-permute-done | bytes 1597472 | tf_op jit(solution)/shard_map/ppermute | solution.py:20
  168.6 0.3 copy.13
  169.0 1.1 maximum_multiply_fusion.1
  170.1 0.7 fusion.65
  170.8 0.3 fusion.44
  171.1 0.1 fusion.66
  171.2 2.0 fusion.20
  173.2 1.0 collective-permute-start.8
  174.2 1.7 collective-permute-start.9
  175.9 1.4 collective-permute-done.8
  177.3 0.6 collective-permute-done.9
  177.9 0.3 pad_maximum_fusion.2
  178.2 1.6 copy.14
  179.9 2.2 collective-permute-start.10
  182.1 1.7 collective-permute-start.11
  184.4 35.2 %collective-permute-done.10 = f32[3,1,130,1024]{3,1,2,0:T(1,128)S(1)} collective-permute-done((f32[3,1,130,1024]{3,1,2,0:T(1,128)S(1)}, f32[3,1,130,1024]{3,1,2,0:T(1,128)S(1)}, u32[]{:S(2)}, u32[]{:S(2)}) %collective-permute-start.10) | collective-permute-done | bytes 1597472 | tf_op jit(solution)/shard_map/ppermute | solution.py:18
  219.6 0.3 copy.16
  219.9 31.6 %collective-permute-done.11 = f32[3,1,130,1024]{3,1,2,0:T(1,128)S(1)} collective-permute-done((f32[3,1,130,1024]{3,1,2,0:T(1,128)S(1)}, f32[3,1,130,1024]{3,1,2,0:T(1,128)S(1)}, u32[]{:S(2)}, u32[]{:S(2)}) %collective-permute-start.11) | collective-permute-done | bytes 1597472 | tf_op jit(solution)/shard_map/ppermute | solution.py:20
  251.5 0.3 copy.17
  251.9 1.1 maximum_multiply_fusion.2
  252.9 0.7 fusion.63
  253.6 0.3 fusion.41
  253.9 0.1 fusion.64
  254.1 2.0 bitcast_dynamic-update-slice_fusion
  256.4 2.0 copy-done.3
  258.4 3.9 %convert_bitcast_fusion = bf16[9,1,1024,128]{2,3,0,1:T(8,128)(2,1)} fusion(bf16[9,128,1024]{2,1,0:T(8,128)(2,1)S(1)} %fusion.59, bf16[2,1024,1024]{2,1,0:T(8,128)(2,1)S(1)} %copy-done.3, s32[]{:T(128)} %bitcast.17, pred[]{:T(512)} %bitcast.16), kind=kOutput, calls=%fused_computation.4 | convolution fusion | flops 2418147328 | bytes 6815749 | tf_op jit(solution)/shard_map/yox,fyzx->fyoz/dot_general | solution.py:75
  262.3 6.7 %copy.18 = bf16[9,1,1024,128]{3,0,1,2:T(8,128)(2,1)} copy(bf16[9,1,1024,128]{2,3,0,1:T(8,128)(2,1)} %convert_bitcast_fusion) | data formatting | bytes 4718592 | tf_op jit(solution)/shard_map/convert_element_type | solution.py:77
  269.0 52.5 %all_to_all.15 = bf16[9,1,1024,128]{3,0,1,2:T(8,128)(2,1)S(1)} all-to-all(bf16[9,1,1024,128]{3,0,1,2:T(8,128)(2,1)} %copy.18), channel_id=1, replica_groups=mesh['grp'=4,'row'=2,'col'=4] {'grp','row'}, dimensions={2} | all-to-all | bytes 4718592 | tf_op jit(solution)/shard_map/all_to_all | solution.py:79
  321.5 3.1 copy.21
  324.6 4.9 %reshape.472 = bf16[9,128,1024]{2,1,0:T(8,128)(2,1)} reshape(bf16[9,1,128,8,128]{4,3,2,0,1:T(8,128)(2,1)} %bitcast.94) | data formatting | bytes 4718592 | tf_op jit(solution)/shard_map/reshape.14
  329.5 4.3 %fusion = f32[9,128,1024]{2,1,0:T(8,128)S(1)} fusion(bf16[9,128,1024]{2,1,0:T(8,128)(2,1)} %reshape.472, bf16[1024,1024]{1,0:T(8,128)(2,1)S(1)} %copy-done), kind=kOutput, calls=%fused_computation.5 | convolution fusion | flops 2415919104 | bytes 9175040 | tf_op jit(solution)/shard_map/fyos,rs->fyor/dot_general | solution.py:53
  333.9 0.1 fusion.36
  334.0 0.1 fusion.34
  334.2 0.1 fusion.30
  334.3 1.7 copy-done.2
  335.9 0.9 fusion.28
  (17 shorter events, 0.5 us)
Async XLA Ops:
  0.0 329.5 %copy-start = (bf16[1024,1024]{1,0:T(8,128)(2,1)S(1)}, bf16[1024,1024]{1,0:T(8,128)(2,1)}, u32[]{:S(2)}) copy-start(bf16[1024,1024]{1,0:T(8,128)(2,1)} %param.7) | copy-start | bytes 6291460
  1.1 4.8 %collective-permute-start = (f32[3,1,1,1024]{3,2,1,0:T(1,128)S(1)}, f32[3,1,1,1024]{3,2,1,0:T(1,128)S(1)}, u32[]{:S(2)}, u32[]{:S(2)}) collective-permute-start(f32[3,1,1,1024]{3,2,1,0:T(1,128)S(1)} %get-tuple-element.43), channel_id=1, source_target_pairs={{0,4},{4,8},{8,12},{12,16},{16,20},{20,24},{24,28},{28,0},{1,5},{5... | collective-permute-start | bytes 36872 | tf_op jit(solution)/shard_map/ppermute | solution.py:18
  4.1 3.7 %collective-permute-start.1 = (f32[3,1,1,1024]{3,2,1,0:T(1,128)S(1)}, f32[3,1,1,1024]{3,2,1,0:T(1,128)S(1)}, u32[]{:S(2)}, u32[]{:S(2)}) collective-permute-start(f32[3,1,1,1024]{3,2,1,0:T(1,128)S(1)} %get-tuple-element.44), channel_id=1, source_target_pairs={{4,0},{8,4},{12,8},{16,12},{20,16},{24,20},{28,24},{0,28},{5,1},{9... | collective-permute-start | bytes 36872 | tf_op jit(solution)/shard_map/ppermute | solution.py:20
  12.2 40.0 %collective-permute-start.2 = (f32[3,1,130,1024]{3,1,2,0:T(1,128)}, f32[3,1,130,1024]{3,1,2,0:T(1,128)}, u32[]{:S(2)}, u32[]{:S(2)}) collective-permute-start(f32[3,1,130,1024]{3,1,2,0:T(1,128)} %copy.6), channel_id=1, source_target_pairs={{0,1},{1,2},{2,3},{3,0},{4,5},{5,6},{6,7},{7,4},{8,9},{9,10},{10,1... | collective-permute-start | bytes 4792328 | tf_op jit(solution)/shard_map/ppermute | solution.py:18
  13.8 70.0 %collective-permute-start.3 = (f32[3,1,130,1024]{3,1,2,0:T(1,128)}, f32[3,1,130,1024]{3,1,2,0:T(1,128)}, u32[]{:S(2)}, u32[]{:S(2)}) collective-permute-start(f32[3,1,130,1024]{3,1,2,0:T(1,128)} %copy.6), channel_id=1, source_target_pairs={{1,0},{2,1},{3,2},{0,3},{5,4},{6,5},{7,6},{4,7},{9,8},{10,9},{11,1... | collective-permute-start | bytes 4792328 | tf_op jit(solution)/shard_map/ppermute | solution.py:20
  54.0 31.6 %copy-start.1 = (f32[3,1,128,1024]{3,2,1,0:T(8,128)S(1)}, f32[3,1,128,1024]{3,2,1,0:T(8,128)}, u32[]{:S(2)}) copy-start(f32[3,1,128,1024]{3,2,1,0:T(8,128)} %param.4) | copy-start | bytes 4718596
  89.6 4.1 %collective-permute-start.4 = (f32[3,1,1,1024]{3,2,1,0:T(1,128)S(1)}, f32[3,1,1,1024]{3,2,1,0:T(1,128)S(1)}, u32[]{:S(2)}, u32[]{:S(2)}) collective-permute-start(f32[3,1,1,1024]{3,2,1,0:T(1,128)S(1)} %get-tuple-element.41), channel_id=1, source_target_pairs={{0,4},{4,8},{8,12},{12,16},{16,20},{20,24},{24,28},{28,0},{1,5},{5... | collective-permute-start | bytes 36872 | tf_op jit(solution)/shard_map/ppermute | solution.py:18
  91.7 3.7 %collective-permute-start.5 = (f32[3,1,1,1024]{3,2,1,0:T(1,128)S(1)}, f32[3,1,1,1024]{3,2,1,0:T(1,128)S(1)}, u32[]{:S(2)}, u32[]{:S(2)}) collective-permute-start(f32[3,1,1,1024]{3,2,1,0:T(1,128)S(1)} %get-tuple-element.42), channel_id=1, source_target_pairs={{4,0},{8,4},{12,8},{16,12},{20,16},{24,20},{28,24},{0,28},{5,1},{9... | collective-permute-start | bytes 36872 | tf_op jit(solution)/shard_map/ppermute | solution.py:20
  97.3 39.8 %collective-permute-start.6 = (f32[3,1,130,1024]{3,1,2,0:T(1,128)S(1)}, f32[3,1,130,1024]{3,1,2,0:T(1,128)S(1)}, u32[]{:S(2)}, u32[]{:S(2)}) collective-permute-start(f32[3,1,130,1024]{3,1,2,0:T(1,128)S(1)} %copy.10), channel_id=1, source_target_pairs={{0,1},{1,2},{2,3},{3,0},{4,5},{5,6},{6,7},{7,4},{8,9},{9,10},{10,1... | collective-permute-start | bytes 4792328 | tf_op jit(solution)/shard_map/ppermute | solution.py:18
  98.4 70.2 %collective-permute-start.7 = (f32[3,1,130,1024]{3,1,2,0:T(1,128)S(1)}, f32[3,1,130,1024]{3,1,2,0:T(1,128)S(1)}, u32[]{:S(2)}, u32[]{:S(2)}) collective-permute-start(f32[3,1,130,1024]{3,1,2,0:T(1,128)S(1)} %copy.10), channel_id=1, source_target_pairs={{1,0},{2,1},{3,2},{0,3},{5,4},{6,5},{7,6},{4,7},{9,8},{10,9},{11,1... | collective-permute-start | bytes 4792328 | tf_op jit(solution)/shard_map/ppermute | solution.py:20
  173.2 4.1 %collective-permute-start.8 = (f32[3,1,1,1024]{3,2,1,0:T(1,128)S(1)}, f32[3,1,1,1024]{3,2,1,0:T(1,128)S(1)}, u32[]{:S(2)}, u32[]{:S(2)}) collective-permute-start(f32[3,1,1,1024]{3,2,1,0:T(1,128)S(1)} %get-tuple-element.39), channel_id=1, source_target_pairs={{0,4},{4,8},{8,12},{12,16},{16,20},{20,24},{24,28},{28,0},{1,5},{5... | collective-permute-start | bytes 36872 | tf_op jit(solution)/shard_map/ppermute | solution.py:18
  174.2 3.7 %collective-permute-start.9 = (f32[3,1,1,1024]{3,2,1,0:T(1,128)S(1)}, f32[3,1,1,1024]{3,2,1,0:T(1,128)S(1)}, u32[]{:S(2)}, u32[]{:S(2)}) collective-permute-start(f32[3,1,1,1024]{3,2,1,0:T(1,128)S(1)} %get-tuple-element.40), channel_id=1, source_target_pairs={{4,0},{8,4},{12,8},{16,12},{20,16},{24,20},{28,24},{0,28},{5,1},{9... | collective-permute-start | bytes 36872 | tf_op jit(solution)/shard_map/ppermute | solution.py:20
  179.9 39.7 %collective-permute-start.10 = (f32[3,1,130,1024]{3,1,2,0:T(1,128)S(1)}, f32[3,1,130,1024]{3,1,2,0:T(1,128)S(1)}, u32[]{:S(2)}, u32[]{:S(2)}) collective-permute-start(f32[3,1,130,1024]{3,1,2,0:T(1,128)S(1)} %copy.14), channel_id=1, source_target_pairs={{0,1},{1,2},{2,3},{3,0},{4,5},{5,6},{6,7},{7,4},{8,9},{9,10},{10,1... | collective-permute-start | bytes 4792328 | tf_op jit(solution)/shard_map/ppermute | solution.py:18
  182.1 69.5 %collective-permute-start.11 = (f32[3,1,130,1024]{3,1,2,0:T(1,128)S(1)}, f32[3,1,130,1024]{3,1,2,0:T(1,128)S(1)}, u32[]{:S(2)}, u32[]{:S(2)}) collective-permute-start(f32[3,1,130,1024]{3,1,2,0:T(1,128)S(1)} %copy.14), channel_id=1, source_target_pairs={{1,0},{2,1},{3,2},{0,3},{5,4},{6,5},{7,6},{4,7},{9,8},{10,9},{11,1... | collective-permute-start | bytes 4792328 | tf_op jit(solution)/shard_map/ppermute | solution.py:20
  256.2 2.2 copy-start.3
  334.3 1.7 copy-start.2
where the time goes:
time: 337 us
  waiting for transfers between devices  208 us (62%)
  blocking collectives  52.5 us (16%)
  local copies, waits for them, and re-layouts  32.8 us (10%)
  starting transfers between devices  20.5 us (6%)
  other arithmetic  13.7 us (4%)
  matrix products  8.22 us (2%)
    ppermute x6, waiting for transfers between devices, extended(): lax.ppermute(tail, axis, [(i, (i + 1) % count) for i in range(count)])  111 us
    ppermute x6, waiting for transfers between devices, extended(): lax.ppermute(head, axis, [((i + 1) % count, i) for i in range(count)])  96.8 us
    all_to_all x1, blocking collectives, body(): lax.all_to_all(x_pass, ('grp', 'row'), split_axis=2, concat_axis=3, tiled...  52.5 us
    ppermute x6, starting transfers between devices, extended(): lax.ppermute(tail, axis, [(i, (i + 1) % count) for i in range(count)])  10.9 us
    ppermute x6, starting transfers between devices, extended(): lax.ppermute(head, axis, [((i + 1) % count, i) for i in range(count)])  9.52 us
  transfers between devices with their start and end apart: 12, of which 12 were waited for; matrix products, arithmetic and copies ran while one was open for 1% of the time, Pallas kernels for 0%

commit v1 on v0

--- a/solution.py
+++ b/solution.py
@@ -1,11 +1,287 @@
+import functools
+
 import jax
 import jax.numpy as jnp
 from jax import lax
+from jax.experimental import pallas as pl
+from jax.experimental.pallas import tpu as pltpu
 from jax.sharding import PartitionSpec as P
 
 STEP_SIZE = 0.25
 VISCOSITY = 0.8
 PRODUCT_PAIRS = ((0, 0), (0, 1), (0, 2), (1, 1), (1, 2), (2, 2))
+
+PLANE = ("grp", "row")
+WIRE = jnp.bfloat16
+CHUNKS = ((0,), (1,), (2,))
+CHIPS = (0, 1, 4, 5)
+HALO = 8
+VMEM_BYTES = 56 * 1024 * 1024
+NT = (((1,), (1,)), ((), ()))
+
+
+def exchange(value, axis, flip):
+    count = lax.axis_size(axis)
+    return lax.ppermute(value, axis, [(i, i ^ flip) for i in range(count)])
+
+
+def whole(memory=pltpu.VMEM):
+    return pl.BlockSpec(memory_space=memory)
+
+
+def step_kernel(slabs, q_ref, *refs):
+    mains, halos = refs[:4], refs[4:8]
+    outs, (start, one, two) = refs[8:-3], refs[-3:]
+    q = q_ref[0]
+    rows = mains[0].shape[-2]
+    width = mains[0].shape[-1]
+    for buffer in (start, one, two):
+        buffer[0] = jnp.zeros(buffer.shape[1:], buffer.dtype)
+        buffer[slabs + 1] = jnp.zeros(buffer.shape[1:], buffer.dtype)
+    for flip in range(slabs):
+        y = (q ^ flip) + 1
+        halo = halos[flip][...].astype(jnp.float32)
+        start[y, :, 0:HALO] = halo
+        start[y, :, HALO : HALO + rows] = mains[flip][...].reshape(3, rows, width).astype(jnp.float32)
+        start[y, :, HALO + rows :] = halo
+
+    last = HALO + rows
+
+    def rates(src, y, row):
+        above, below = (row, row) if row else (0, last)
+        here = [src[y, comp, row : row + HALO] for comp in range(3)]
+        half = [0.5 * value for value in here]
+        result = []
+        for comp in range(3):
+            center = here[comp]
+            y_next, y_prev = src[y + 1, comp, row : row + HALO], src[y - 1, comp, row : row + HALO]
+            z_next = src[y, comp, above + 1 : above + 1 + HALO]
+            z_prev = src[y, comp, below - 1 : below - 1 + HALO]
+            x_next = pltpu.roll(center, width - 1, 1)
+            x_prev = pltpu.roll(center, 1, 1)
+            advect = half[0] * (x_next - x_prev) + half[1] * (y_next - y_prev) + half[2] * (z_next - z_prev)
+            laplace = (x_next + x_prev) + (y_next + y_prev) + (z_next + z_prev) - 6.0 * center
+            result.append((center, VISCOSITY * laplace - advect))
+        return result
+
+    def put(buffer, y, comp, row, value):
+        buffer[y, comp, row : row + HALO] = value
+        if row == 0:
+            buffer[y, comp, last : last + HALO] = value
+
+    def section_one(number, carry):
+        y = number + 1
+        for row in range(0, last, HALO):
+            for comp, (center, rate) in enumerate(rates(start, y, row)):
+                put(one, y, comp, row, center + STEP_SIZE * rate)
+        return carry
+
+    def section_two(number, carry):
+        y = number + 1
+        for row in range(0, last, HALO):
+            for comp, (center, rate) in enumerate(rates(one, y, row)):
+                base = start[y, comp, row : row + HALO]
+                put(two, y, comp, row, 0.75 * base + 0.25 * (center + STEP_SIZE * rate))
+        return carry
+
+    lax.fori_loop(0, slabs, section_one, 0)
+    lax.fori_loop(0, slabs, section_two, 0)
+    for flip in range(slabs):
+        y = (q ^ flip) + 1
+        for row in range(HALO, last, 2 * HALO):
+            pair = [rates(two, y, row), rates(two, y, row + HALO)]
+            for number, comps in enumerate(CHUNKS):
+                out = outs[number * slabs + flip]
+                for place, comp in enumerate(comps):
+                    values = []
+                    for part in range(2):
+                        at = row + part * HALO
+                        center, rate = pair[part][comp]
+                        base = start[y, comp, at : at + HALO]
+                        values.append(base * (1.0 / 3.0) + (2.0 / 3.0) * (center + STEP_SIZE * rate))
+                    out[place, row - HALO : row + HALO] = jnp.concatenate(values, 0).astype(out.dtype)
+
+
+def advance(velocity, profile):
+    slabs = lax.axis_size("col")
+    q = lax.axis_index("col")
+    v = velocity[:, 0]
+    block, width = v.shape[1:]
+    rows = block // slabs
+    narrow = v.astype(WIRE)
+    plane = lax.axis_size(PLANE)
+    tail = lax.ppermute(narrow[:, block - HALO :], PLANE, [(i, (i + 1) % plane) for i in range(plane)])
+    head = lax.ppermute(narrow[:, :HALO], PLANE, [((i + 1) % plane, i) for i in range(plane)])
+    mains = [v]
+    for flip in range(1, slabs):
+        mains.append(exchange(lax.dynamic_slice_in_dim(narrow, rows * (q ^ flip), rows, 1), "col", flip))
+    framed = jnp.concatenate([tail, narrow, head], axis=1)
+    first = lax.broadcasted_iota(jnp.int32, (3, HALO, width), 1) < HALO // 2
+    halos = []
+    for flip in range(slabs):
+        at = rows * (q ^ flip)
+        before = lax.dynamic_slice_in_dim(framed, at, HALO, 1)
+        after = lax.dynamic_slice_in_dim(framed, at + rows + HALO, HALO, 1)
+        halo = jnp.where(first, after, before)
+        halos.append(exchange(halo, "col", flip) if flip else halo)
+
+    grid_spec = pltpu.PrefetchScalarGridSpec(
+        num_scalar_prefetch=1,
+        grid=(1,),
+        in_specs=[pl.BlockSpec((3, rows, width), lambda i, q_ref: (0, q_ref[0], 0))] + [whole()] * 7,
+        out_specs=[whole()] * (len(CHUNKS) * slabs),
+        scratch_shapes=[pltpu.VMEM((slabs + 2, 3, rows + 2 * HALO, width), jnp.float32)] * 3,
+    )
+    cells = 3 * slabs * rows * width
+    pieces = pl.pallas_call(
+        functools.partial(step_kernel, slabs),
+        out_shape=[
+            jax.ShapeDtypeStruct((len(comps), rows, width), WIRE) for comps in CHUNKS for _ in range(slabs)
+        ],
+        grid_spec=grid_spec,
+        compiler_params=pltpu.CompilerParams(vmem_limit_bytes=VMEM_BYTES),
+        cost_estimate=pl.CostEstimate(flops=75 * cells, bytes_accessed=6 * cells, transcendentals=0),
+        name="advance",
+    )(q.reshape(1).astype(jnp.int32), *mains, *halos)
+    chunks = []
+    for number in range(len(CHUNKS)):
+        mine = pieces[number * slabs : (number + 1) * slabs]
+        chunks.append([mine[0]] + [exchange(mine[flip], "col", flip) for flip in range(1, slabs)])
+    return chunks
+
+
+def fields_of(comps):
+    singles = list(comps)
+    pairs = [(a, b) for b in comps for a in range(b + 1)]
+    return singles, pairs
+
+
+def x_kernel(number, slabs, place_ref, matrices, *refs):
+    inputs = refs[: 2 * (number + 1)]
+    outs = refs[2 * (number + 1) : -4]
+    matrix, cells, fields, sem = refs[-4:]
+    q, me, prof = place_ref[0], place_ref[1], place_ref[2]
+    core = (me // 2) % 2
+    copies = []
+    for slot, flip in enumerate(CHIPS):
+        copies.append(
+            pltpu.make_async_copy(
+                matrices.at[prof, pl.ds(pl.multiple_of((me ^ flip) * 128, 128), 128)],
+                matrix.at[pl.ds(slot * 128, 128)],
+                sem.at[slot],
+            )
+        )
+        copies[-1].start()
+    for chunk in range(number + 1):
+        for other in range(2):
+            ref = inputs[2 * chunk + other]
+            rows = ref.shape[2]
+            base = 128 * (core ^ other)
+            for flip in range(slabs):
+                at = pl.multiple_of(base + rows * (q ^ flip), rows)
+                for place, comp in enumerate(CHUNKS[chunk]):
+                    cells[comp, pl.ds(at, rows)] = ref[flip, place]
+    singles, pairs = fields_of(CHUNKS[number])
+    for at, (a, b) in enumerate(pairs):
+        product = cells[a].astype(jnp.float32) * cells[b].astype(jnp.float32)
+        fields[at] = product.astype(jnp.bfloat16)
+    for copy in copies:
+        copy.wait()
+    for at in range(len(singles) + len(pairs)):
+        field = cells[singles[at]] if at < len(singles) else fields[at - len(singles)]
+        result = lax.dot_general(matrix[...], field, NT, preferred_element_type=jnp.float32)
+        for slot in range(len(CHIPS)):
+            outs[slot][at] = result[slot * 128 : (slot + 1) * 128].astype(jnp.bfloat16)
+
+
+def z_kernel(number, place_ref, z_filter, *refs):
+    singles, pairs = fields_of(CHUNKS[number])
+    count = len(singles) + len(pairs)
+    blocks = refs[: len(CHIPS)]
+    earlier = refs[len(CHIPS) : len(CHIPS) + number]
+    keep, stress, lines, passed, made, sem = refs[-6:]
+    me = place_ref[0]
+    for slot, flip in enumerate(CHIPS):
+        for core in range(2):
+            source = ((me ^ flip) & ~2) | (2 * core)
+            lane = pl.multiple_of(128 * source, 128)
+            for at in range(count):
+                lines[at * 128 : (at + 1) * 128, pl.ds(lane, 128)] = blocks[slot][at, :, 128 * core : 128 * core + 128]
+    passed[...] = lax.dot_general(lines[...], z_filter[...], NT, preferred_element_type=jnp.float32)
+    means = {}
+    for chunk in range(number):
+        for place, comp in enumerate(CHUNKS[chunk]):
+            means[comp] = earlier[chunk][place]
+    for place, comp in enumerate(singles):
+        means[comp] = passed[place * 128 : (place + 1) * 128]
+        keep[place] = means[comp]
+    copies = []
+    for at, pair in enumerate(pairs):
+        row = (len(singles) + at) * 128
+        made[at] = passed[row : row + 128] - means[pair[0]] * means[pair[1]]
+        copies.append(
+            pltpu.make_async_copy(made.at[at], stress.at[PRODUCT_PAIRS.index(pair), 0], sem.at[at])
+        )
+        copies[-1].start()
+    for copy in copies:
+        copy.wait()
+
+
+def fast_body(velocity, profile, x_filters, z_filter):
+    width = velocity.shape[3]
+    slabs = lax.axis_size("col")
+    q = lax.axis_index("col").astype(jnp.int32)
+    me = lax.axis_index(PLANE).astype(jnp.int32)
+    place = jnp.stack([q, me, profile[0]])
+    chunks = advance(velocity, profile)
+    gathered, means, stress = [], [], None
+    for number, pieces in enumerate(chunks):
+        mine = jnp.stack(pieces)
+        gathered += [mine, exchange(mine, "grp", 1)]
+        singles, pairs = fields_of(CHUNKS[number])
+        count = len(singles) + len(pairs)
+        blocks = pl.pallas_call(
+            functools.partial(x_kernel, number, slabs),
+            out_shape=[jax.ShapeDtypeStruct((count, 128, 256), jnp.bfloat16)] * len(CHIPS),
+            in_specs=[whole(pltpu.SMEM), whole(pl.ANY)] + [whole()] * len(gathered),
+            out_specs=[whole()] * len(CHIPS),
+            scratch_shapes=[
+                pltpu.VMEM((512, width), jnp.bfloat16),
+                pltpu.VMEM((3, 256, width), jnp.bfloat16),
+                pltpu.VMEM((len(pairs), 256, width), jnp.bfloat16),
+                pltpu.SemaphoreType.DMA((len(CHIPS),)),
+            ],
+            compiler_params=pltpu.CompilerParams(vmem_limit_bytes=VMEM_BYTES),
+            cost_estimate=pl.CostEstimate(
+                flops=2 * 512 * width * 256 * count, bytes_accessed=2 * 1024 * width, transcendentals=0
+            ),
+            name=f"x_filter_{number}",
+        )(place, x_filters, *gathered)
+        blocks = [blocks[0]] + [exchange(blocks[slot], PLANE, CHIPS[slot]) for slot in range(1, len(CHIPS))]
+        extra = [] if stress is None else [stress]
+        keep, stress = pl.pallas_call(
+            functools.partial(z_kernel, number),
+            out_shape=[
+                jax.ShapeDtypeStruct((len(singles), 128, width), jnp.float32),
+                jax.ShapeDtypeStruct((6, 1, 128, width), jnp.float32),
+            ],
+            in_specs=[whole(pltpu.SMEM)] + [whole()] * (1 + len(CHIPS) + len(means)) + [whole(pl.ANY)] * len(extra),
+            out_specs=[whole(), whole(pl.ANY)],
+            input_output_aliases={2 + len(CHIPS) + len(means): 1} if extra else {},
+            scratch_shapes=[
+                pltpu.VMEM((count * 128, width), jnp.bfloat16),
+                pltpu.VMEM((count * 128, width), jnp.float32),
+                pltpu.VMEM((len(pairs), 128, width), jnp.float32),
+                pltpu.SemaphoreType.DMA((len(pairs),)),
+            ],
+            compiler_params=pltpu.CompilerParams(vmem_limit_bytes=VMEM_BYTES),
+            cost_estimate=pl.CostEstimate(
+                flops=2 * 128 * count * width * width, bytes_accessed=4 * 1024 * width, transcendentals=0
+            ),
+            name=f"z_filter_{number}",
+        )(me.reshape(1), z_filter, *blocks, *means, *extra)
+        means.append(keep)
+    return stress
 
 
 def extended(cells, sides, width):
@@ -89,10 +365,21 @@
 
 def solution(mesh):
     placed = (P(None, "col", ("grp", "row"), None), P("col"), P(), P())
-    return jax.shard_map(
-        body,
-        mesh=mesh,
-        in_specs=placed,
-        out_specs=P(None, "col", ("grp", "row"), None),
-        check_vma=False,
-    )
+
+    def run(velocity, profile, x_filters, z_filter):
+        shape = dict(mesh.shape)
+        plane = shape["grp"] * shape["row"]
+        suits = (
+            (shape["grp"], shape["row"], shape["col"]) == (4, 2, 4)
+            and velocity.shape == (3, shape["col"], 128 * plane, 1024)
+            and x_filters.shape[1:] == z_filter.shape == (1024, 1024)
+        )
+        return jax.shard_map(
+            fast_body if suits else body,
+            mesh=mesh,
+            in_specs=placed,
+            out_specs=P(None, "col", ("grp", "row"), None),
+            check_vma=False,
+        )(velocity, profile, x_filters, z_filter)
+
+    return run

time: 337 us -> 113 us (0.34)
  waiting for transfers between devices: 208 us -> 21.5 us
  blocking collectives: 52.5 us -> 0 us
  Pallas kernels: 0 us -> 36.3 us
  local copies, waits for them, and re-layouts: 32.8 us -> 3.63 us
  starting transfers between devices: 20.5 us -> 44.7 us
  matrix products: 8.22 us -> 0 us
  other arithmetic: 13.7 us -> 5.52 us
    ppermute x12 -> x29, waiting for transfers between devices: 208 us -> 21.5 us  [the longest x27 21.5 us: exchange(): return lax.ppermute(value, axis, [(i, i ^ flip) for i in range(count)])]
    all_to_all x1 -> x0, blocking collectives: 52.5 us -> none  [body(): lax.all_to_all(x_pass, ('grp', 'row'), split_axis=2, concat_axis=3, tiled...]
    pallas_call x0 -> x7, Pallas kernels: none -> 36.3 us  [the longest x3 14.7 us: fast_body(): pl.pallas_call(functools.partial(z_kernel, number), out_shape=[jax.ShapeD...]
    ppermute x12 -> x29, starting transfers between devices: 20.5 us -> 44.7 us  [the longest x27 41.2 us: exchange(): return lax.ppermute(value, axis, [(i, i ^ flip) for i in range(count)])]
    dot_general x2 -> x0, matrix products: 8.22 us -> none  [the longest x1 4.32 us: z_apply(): jnp.einsum('fyos,rs->fyor', received, z_filter, preferred_element_type=jn...]
    convert_element_type x1 -> x0, local copies, waits for them, and re-layouts: 6.69 us -> none  [body(): x_pass = jnp.einsum('yox,fyzx->fyoz', matrices, fields, preferred_element...]
    concatenate x3 -> x0, local copies, waits for them, and re-layouts: 6.08 us -> none  [extended(): jnp.concatenate([lax.ppermute(tail, axis, [(i, (i + 1) % count) for i in...]
    another operation x1 -> x0, local copies, waits for them, and re-layouts: 4.94 us -> none
  transfers between devices with their start and end apart: 12 -> 29, of which waited for: 12 -> 6; matrix products, arithmetic and copies ran while one was open for 1% -> 4% of each run, Pallas kernels for 0% -> 19%
where the time goes in v1:
time: 113 us
  starting transfers between devices  44.7 us (40%)
  Pallas kernels  36.3 us (32%)
  waiting for transfers between devices  21.5 us (19%)
  other arithmetic  5.52 us (5%)
  local copies, waits for them, and re-layouts  3.63 us (3%)
    ppermute x27, starting transfers between devices, exchange(): return lax.ppermute(value, axis, [(i, i ^ flip) for i in range(count)])  41.2 us
    ppermute x27, waiting for transfers between devices, exchange(): return lax.ppermute(value, axis, [(i, i ^ flip) for i in range(count)])  21.5 us
    pallas_call x3, Pallas kernels, fast_body(): pl.pallas_call(functools.partial(z_kernel, number), out_shape=[jax.ShapeD...  14.7 us
    pallas_call x3, Pallas kernels, fast_body(): pl.pallas_call(functools.partial(x_kernel, number, slabs), out_shape=[jax...  12.7 us
    pallas_call x1, Pallas kernels, advance(): pl.pallas_call(functools.partial(step_kernel, slabs), out_shape=[jax.Shap...  8.89 us
    unnamed x46, local copies, waits for them, and re-layouts  3.59 us
    ppermute x1, starting transfers between devices, advance(): lax.ppermute(narrow[:, block - HALO:], PLANE, [(i, (i + 1) % plane) for i...  3.03 us
    another operation x3, other arithmetic, fast_body(): mine = jnp.stack(pieces)  2.62 us
  transfers between devices with their start and end apart: 29, of which 6 were waited for; matrix products, arithmetic and copies ran while one was open for 4% of the time, Pallas kernels for 19%

profile of v1, /device:TPU:0, one launch (start us, length us, event | category | flops | bytes accessed | tf_op | source)
XLA Modules:
  0.0 112.7 jit_solution(14084030254488997634)
XLA Ops:
  0.0 1.5 %bitcast_convert_fusion = bf16[3,128,1024]{2,1,0:T(8,128)(2,1)S(1)} fusion(f32[3,1,128,1024]{3,2,1,0:T(8,128)} %param.4), kind=kLoop, calls=%fused_computation.13 | loop fusion | flops 393216 | bytes 2359296 | tf_op jit(solution)/shard_map/convert_element_type | solution.py:111
  1.5 3.0 %collective-permute-start.3 = (bf16[3,8,1024]{2,1,0:T(8,128)(2,1)S(1)}, bf16[3,8,1024]{2,1,0:T(8,128)(2,1)S(1)}, u32[]{:S(2)}, u32[]{:S(2)}) collective-permute-start(bf16[3,8,1024]{2,1,0:T(8,128)(2,1)S(1)} %get-tuple-element.67), channel_id=1, source_target_pairs={{0,4},{4,8},{8,12},{12,16},{16,20},{20,24},{24,28},{28,0},{1,5},{5... | collective-permute-start | bytes 147464 | tf_op jit(solution)/shard_map/ppermute | solution.py:113
  4.6 0.4 collective-permute-start.4
  5.1 4.4 %collective-permute-start.2 = (bf16[3,32,1024]{2,1,0:T(8,128)(2,1)S(1)}, bf16[3,32,1024]{2,1,0:T(8,128)(2,1)S(1)}, u32[]{:S(2)}, u32[]{:S(2)}) collective-permute-start(bf16[3,32,1024]{2,1,0:T(8,128)(2,1)S(1)} %get-tuple-element.69), channel_id=1, source_target_pairs={{0,3},{1,2},{2,1},{3,0},{4,7},{5,6},{6,5},{7,4},{8,11},{9,10},{10,... | collective-permute-start | bytes 589832 | tf_op jit(solution)/shard_map/ppermute | solution.py:25
  9.4 0.6 collective-permute-start
  10.1 0.0 collective-permute-done.3
  10.1 0.0 collective-permute-done.4
  10.1 0.1 pad_maximum_fusion
  10.1 0.8 dynamic-slice_select_fusion
  10.9 3.7 %collective-permute-start.7 = (bf16[3,8,1024]{2,1,0:T(8,128)(2,1)S(1)}, bf16[3,8,1024]{2,1,0:T(8,128)(2,1)S(1)}, u32[]{:S(2)}, u32[]{:S(2)}) collective-permute-start(bf16[3,8,1024]{2,1,0:T(8,128)(2,1)S(1)} %get-tuple-element.63), channel_id=1, source_target_pairs={{0,3},{1,2},{2,1},{3,0},{4,7},{5,6},{6,5},{7,4},{8,11},{9,10},{10,... | collective-permute-start | bytes 147464 | tf_op jit(solution)/shard_map/ppermute | solution.py:25
  14.6 0.0 collective-permute-start.5
  14.6 9.1 %collective-permute-done.7.refs_7_ = bf16[3,8,1024]{2,1,0:T(8,128)(2,1)S(1)} collective-permute-done((bf16[3,8,1024]{2,1,0:T(8,128)(2,1)S(1)}, bf16[3,8,1024]{2,1,0:T(8,128)(2,1)S(1)}, u32[]{:S(2)}, u32[]{:S(2)}) %collective-permute-start.7) | collective-permute-done | bytes 49184 | tf_op jit(solution)/shard_map/ppermute | solution.py:25
  23.7 5.3 %collective-permute-start.6 = (bf16[3,8,1024]{2,1,0:T(8,128)(2,1)S(1)}, bf16[3,8,1024]{2,1,0:T(8,128)(2,1)S(1)}, u32[]{:S(2)}, u32[]{:S(2)}) collective-permute-start(bf16[3,8,1024]{2,1,0:T(8,128)(2,1)S(1)} %get-tuple-element.65), channel_id=1, source_target_pairs={{0,2},{1,3},{2,0},{3,1},{4,6},{5,7},{6,4},{7,5},{8,10},{9,11},{10,... | collective-permute-start | bytes 147464 | tf_op jit(solution)/shard_map/ppermute | solution.py:25
  29.0 2.1 %collective-permute-done.6.refs_6_ = bf16[3,8,1024]{2,1,0:T(8,128)(2,1)S(1)} collective-permute-done((bf16[3,8,1024]{2,1,0:T(8,128)(2,1)S(1)}, bf16[3,8,1024]{2,1,0:T(8,128)(2,1)S(1)}, u32[]{:S(2)}, u32[]{:S(2)}) %collective-permute-start.6) | collective-permute-done | bytes 49184 | tf_op jit(solution)/shard_map/ppermute | solution.py:25
  31.1 0.0 collective-permute-done.2.refs_3_
  31.1 0.0 collective-permute-done.refs_1_
  31.1 0.0 copy-start.11
  31.2 0.6 copy-done.20
  31.7 0.1 copy-done.9
  31.8 0.1 copy-done.10
  31.9 0.0 copy-done.11
  31.9 8.9 %advance.1 = (bf16[1,32,1024]{2,1,0:T(8,128)(2,1)}, bf16[1,32,1024]{2,1,0:T(8,128)(2,1)}, bf16[1,32,1024]{2,1,0:T(8,128)(2,1)}, bf16[1,32,1024]{2,1,0:T(8,128)(2...) custom-call(s32[1]{0:T(128)} %bitcast.1.q_ref, ...), custom_call_target="tpu_custom_call" | custom-call | flops 29491200 | bytes 2359296 | tf_op jit(solution)/shard_map/advance/pallas_call | solution.py:136
  40.8 1.9 %collective-permute-start.8 = (bf16[1,32,1024]{2,1,0:T(8,128)(2,1)}, bf16[1,32,1024]{2,1,0:T(8,128)(2,1)S(1)}, u32[]{:S(2)}, u32[]{:S(2)}) collective-permute-start(bf16[1,32,1024]{2,1,0:T(8,128)(2,1)} %get-tuple-element.35), channel_id=1, source_target_pairs={{0,1},{1,0},{2,3},{3,2},{4,5},{5,4},{6,7},{7,6},{8,9},{9,8},{10,11... | collective-permute-start | bytes 196616 | tf_op jit(solution)/shard_map/ppermute | solution.py:25
  42.8 1.1 collective-permute-start.9
  43.8 1.4 %collective-permute-start.10 = (bf16[1,32,1024]{2,1,0:T(8,128)(2,1)}, bf16[1,32,1024]{2,1,0:T(8,128)(2,1)S(1)}, u32[]{:S(2)}, u32[]{:S(2)}) collective-permute-start(bf16[1,32,1024]{2,1,0:T(8,128)(2,1)} %get-tuple-element.37), channel_id=1, source_target_pairs={{0,3},{1,2},{2,1},{3,0},{4,7},{5,6},{6,5},{7,4},{8,11},{9,10},{10,... | collective-permute-start | bytes 196616 | tf_op jit(solution)/shard_map/ppermute | solution.py:25
  45.9 1.1 collective-permute-start.12
  47.0 2.0 %collective-permute-start.13 = (bf16[1,32,1024]{2,1,0:T(8,128)(2,1)}, bf16[1,32,1024]{2,1,0:T(8,128)(2,1)S(1)}, u32[]{:S(2)}, u32[]{:S(2)}) collective-permute-start(bf16[1,32,1024]{2,1,0:T(8,128)(2,1)} %get-tuple-element.40), channel_id=1, source_target_pairs={{0,2},{1,3},{2,0},{3,1},{4,6},{5,7},{6,4},{7,5},{8,10},{9,11},{10,... | collective-permute-start | bytes 196616 | tf_op jit(solution)/shard_map/ppermute | solution.py:25
  49.0 0.0 collective-permute-done.8
  49.0 1.4 %collective-permute-start.14 = (bf16[1,32,1024]{2,1,0:T(8,128)(2,1)}, bf16[1,32,1024]{2,1,0:T(8,128)(2,1)S(1)}, u32[]{:S(2)}, u32[]{:S(2)}) collective-permute-start(bf16[1,32,1024]{2,1,0:T(8,128)(2,1)} %get-tuple-element.41), channel_id=1, source_target_pairs={{0,3},{1,2},{2,1},{3,0},{4,7},{5,6},{6,5},{7,4},{8,11},{9,10},{10,... | collective-permute-start | bytes 196616 | tf_op jit(solution)/shard_map/ppermute | solution.py:25
  50.3 1.6 %collective-permute-done.9 = bf16[1,32,1024]{2,1,0:T(8,128)(2,1)S(1)} collective-permute-done((bf16[1,32,1024]{2,1,0:T(8,128)(2,1)}, bf16[1,32,1024]{2,1,0:T(8,128)(2,1)S(1)}, u32[]{:S(2)}, u32[]{:S(2)}) %collective-permute-start.9) | collective-permute-done | bytes 65568 | tf_op jit(solution)/shard_map/ppermute | solution.py:25
  51.9 0.0 collective-permute-start.16
  51.9 0.0 collective-permute-done.10
  51.9 5.3 %collective-permute-start.17 = (bf16[1,32,1024]{2,1,0:T(8,128)(2,1)}, bf16[1,32,1024]{2,1,0:T(8,128)(2,1)S(1)}, u32[]{:S(2)}, u32[]{:S(2)}) collective-permute-start(bf16[1,32,1024]{2,1,0:T(8,128)(2,1)} %get-tuple-element.44), channel_id=1, source_target_pairs={{0,2},{1,3},{2,0},{3,1},{4,6},{5,7},{6,4},{7,5},{8,10},{9,11},{10,... | collective-permute-start | bytes 196616 | tf_op jit(solution)/shard_map/ppermute | solution.py:25
  57.3 0.9 pad_maximum_fusion.1.refs_0_
  58.1 0.0 copy-start
  58.2 1.6 %collective-permute-start.18 = (bf16[1,32,1024]{2,1,0:T(8,128)(2,1)}, bf16[1,32,1024]{2,1,0:T(8,128)(2,1)S(1)}, u32[]{:S(2)}, u32[]{:S(2)}) collective-permute-start(bf16[1,32,1024]{2,1,0:T(8,128)(2,1)} %get-tuple-element.45), channel_id=1, source_target_pairs={{0,3},{1,2},{2,1},{3,0},{4,7},{5,6},{6,5},{7,4},{8,11},{9,10},{10,... | collective-permute-start | bytes 196616 | tf_op jit(solution)/shard_map/ppermute | solution.py:25
  59.8 0.9 pad_maximum_fusion.2.refs_2_
  60.7 0.6 collective-permute-start.15
  61.2 0.0 collective-permute-done.16
  61.3 3.2 %collective-permute-done.18 = bf16[1,32,1024]{2,1,0:T(8,128)(2,1)S(1)} collective-permute-done((bf16[1,32,1024]{2,1,0:T(8,128)(2,1)}, bf16[1,32,1024]{2,1,0:T(8,128)(2,1)S(1)}, u32[]{:S(2)}, u32[]{:S(2)}) %collective-permute-start.18) | collective-permute-done | bytes 65568 | tf_op jit(solution)/shard_map/ppermute | solution.py:25
  64.5 0.9 pad_maximum_fusion.3.refs_4_
  65.4 0.1 collective-permute-start.19
  65.5 0.6 pad_add_fusion.place_ref
  66.0 0.7 copy-done.1
  66.7 3.7 %x_filter_0.1 = (bf16[2,128,256]{2,1,0:T(8,128)(2,1)}, bf16[2,128,256]{2,1,0:T(8,128)(2,1)}, bf16[2,128,256]{2,1,0:T(8,128)(2,1)}, bf16[2,128,256]{2,1,0:T(8,128)(2,1)}) custom-call(s32[3]{0:T(128)} %pad_add_fusion.place_ref, bf16[2,1024,1024]{2,1,0:T(8,128)(2,1)} %matrices.5, bf16[4,1,32,1024]{3,2,1,0:T(8,128)(2,1)} %copy-done, ...), custom_call_target="tpu_custom_call" | custom-call | flops 536870912 | bytes 2097152 | tf_op jit(solution)/shard_map/x_filter_0/pallas_call | solution.py:243
  70.5 1.5 %collective-permute-start.23 = (bf16[2,128,256]{2,1,0:T(8,128)(2,1)}, bf16[2,128,256]{2,1,0:T(8,128)(2,1)S(1)}, u32[]{:S(2)}, u32[]{:S(2)}) collective-permute-start(bf16[2,128,256]{2,1,0:T(8,128)(2,1)} %get-tuple-element.51), channel_id=1, source_target_pairs={{0,4},{4,0},{8,12},{12,8},{16,20},{20,16},{24,28},{28,24},{1,5},{5... | collective-permute-start | bytes 393224 | tf_op jit(solution)/shard_map/ppermute | solution.py:25
  72.0 0.7 copy-done.4
  72.7 4.2 %x_filter_1.1 = (bf16[3,128,256]{2,1,0:T(8,128)(2,1)}, bf16[3,128,256]{2,1,0:T(8,128)(2,1)}, bf16[3,128,256]{2,1,0:T(8,128)(2,1)}, bf16[3,128,256]{2,1,0:T(8,128)(2,1)}) custom-call(s32[3]{0:T(128)} %pad_add_fusion.place_ref, bf16[2,1024,1024]{2,1,0:T(8,128)(2,1)} %matrices.5, bf16[4,1,32,1024]{3,2,1,0:T(8,128)(2,1)} %copy-done, ...), custom_call_target="tpu_custom_call" | custom-call | flops 805306368 | bytes 2097152 | tf_op jit(solution)/shard_map/x_filter_1/pallas_call | solution.py:243
  77.0 0.6 collective-permute-start.26
  77.6 1.5 %collective-permute-start.24 = (bf16[2,128,256]{2,1,0:T(8,128)(2,1)S(1)}, bf16[2,128,256]{2,1,0:T(8,128)(2,1)S(1)}, u32[]{:S(2)}, u32[]{:S(2)}) collective-permute-start(bf16[2,128,256]{2,1,0:T(8,128)(2,1)S(1)} %copy-done.22), channel_id=1, source_target_pairs={{0,16},{4,20},{8,24},{12,28},{16,0},{20,4},{24,8},{28,12},{1,17},{... | collective-permute-start | bytes 393224 | tf_op jit(solution)/shard_map/ppermute | solution.py:25
  79.1 1.4 %collective-permute-start.25 = (bf16[2,128,256]{2,1,0:T(8,128)(2,1)S(1)}, bf16[2,128,256]{2,1,0:T(8,128)(2,1)S(1)}, u32[]{:S(2)}, u32[]{:S(2)}) collective-permute-start(bf16[2,128,256]{2,1,0:T(8,128)(2,1)S(1)} %copy-done.21), channel_id=1, source_target_pairs={{0,20},{4,16},{8,28},{12,24},{16,4},{20,0},{24,12},{28,8},{1,21},{... | collective-permute-start | bytes 393224 | tf_op jit(solution)/shard_map/ppermute | solution.py:25
  80.5 1.1 %collective-permute-start.27 = (bf16[3,128,256]{2,1,0:T(8,128)(2,1)}, bf16[3,128,256]{2,1,0:T(8,128)(2,1)S(1)}, u32[]{:S(2)}, u32[]{:S(2)}) collective-permute-start(bf16[3,128,256]{2,1,0:T(8,128)(2,1)} %get-tuple-element.57), channel_id=1, source_target_pairs={{0,16},{4,20},{8,24},{12,28},{16,0},{20,4},{24,8},{28,12},{1,17},{... | collective-permute-start | bytes 589832 | tf_op jit(solution)/shard_map/ppermute | solution.py:25
  81.7 0.9 collective-permute-start.28
  82.6 4.7 %x_filter_2.1 = (bf16[4,128,256]{2,1,0:T(8,128)(2,1)}, bf16[4,128,256]{2,1,0:T(8,128)(2,1)}, bf16[4,128,256]{2,1,0:T(8,128)(2,1)}, bf16[4,128,256]{2,1,0:T(8,128)(2,1)}) custom-call(s32[3]{0:T(128)} %pad_add_fusion.place_ref, bf16[2,1024,1024]{2,1,0:T(8,128)(2,1)} %matrices.5, bf16[4,1,32,1024]{3,2,1,0:T(8,128)(2,1)} %copy-done, ...), custom_call_target="tpu_custom_call" | custom-call | flops 1073741824 | bytes 2097152 | tf_op jit(solution)/shard_map/x_filter_2/pallas_call | solution.py:243
  87.4 1.5 %collective-permute-start.20 = (bf16[4,128,256]{2,1,0:T(8,128)(2,1)}, bf16[4,128,256]{2,1,0:T(8,128)(2,1)S(1)}, u32[]{:S(2)}, u32[]{:S(2)}) collective-permute-start(bf16[4,128,256]{2,1,0:T(8,128)(2,1)} %get-tuple-element.47), channel_id=1, source_target_pairs={{0,4},{4,0},{8,12},{12,8},{16,20},{20,16},{24,28},{28,24},{1,5},{5... | collective-permute-start | bytes 786440 | tf_op jit(solution)/shard_map/ppermute | solution.py:25
  88.9 1.1 %collective-permute-start.21 = (bf16[4,128,256]{2,1,0:T(8,128)(2,1)}, bf16[4,128,256]{2,1,0:T(8,128)(2,1)S(1)}, u32[]{:S(2)}, u32[]{:S(2)}) collective-permute-start(bf16[4,128,256]{2,1,0:T(8,128)(2,1)} %get-tuple-element.48), channel_id=1, source_target_pairs={{0,16},{4,20},{8,24},{12,28},{16,0},{20,4},{24,8},{28,12},{1,17},{... | collective-permute-start | bytes 786440 | tf_op jit(solution)/shard_map/ppermute | solution.py:25
  90.1 0.9 collective-permute-start.22
  90.9 4.2 %z_filter_0.1 = (f32[1,128,1024]{2,1,0:T(8,128)}, f32[6,1,128,1024]{3,2,1,0:T(8,128)}) custom-call(s32[1]{0:T(128)} %bitcast.place_ref, bf16[1024,1024]{1,0:T(8,128)(2,1)} %z_filter.5, bf16[2,128,256]{2,1,0:T(8,128)(2,1)} %get-tuple-element.50.refs_0_, bf16[2,128,256]{2,1,0:T(8,128)(2,1)} %copy-done.15, bf16[2,128,256]{2,1,0:T(8,128)(2,1)} %copy-done.16, ...), custom_call_target="tpu_custom_call" | custom-call | flops 536870912 | bytes 4194304 | tf_op jit(solution)/shard_map/z_filter_0/pallas_call | solution.py:262
  95.2 1.0 collective-permute-done.28.refs_3_
  96.2 0.7 copy-done.14
  96.8 4.9 %z_filter_1.1 = (f32[1,128,1024]{2,1,0:T(8,128)}, f32[6,1,128,1024]{3,2,1,0:T(8,128)}) custom-call(s32[1]{0:T(128)} %bitcast.place_ref, bf16[1024,1024]{1,0:T(8,128)(2,1)} %z_filter.5, bf16[3,128,256]{2,1,0:T(8,128)(2,1)} %get-tuple-element.55.refs_0_, bf16[3,128,256]{2,1,0:T(8,128)(2,1)} %copy-done.12, ...), custom_call_target="tpu_custom_call", output_to_operand_aliasing={{1}: (7, {})} | custom-call | flops 805306368 | bytes 4194304 | tf_op jit(solution)/shard_map/z_filter_1/pallas_call | solution.py:262
  101.8 4.6 %collective-permute-done.22.refs_3_ = bf16[4,128,256]{2,1,0:T(8,128)(2,1)S(1)} collective-permute-done((bf16[4,128,256]{2,1,0:T(8,128)(2,1)}, bf16[4,128,256]{2,1,0:T(8,128)(2,1)S(1)}, u32[]{:S(2)}, u32[]{:S(2)}) %collective-permute-start.22) | collective-permute-done | bytes 262176 | tf_op jit(solution)/shard_map/ppermute | solution.py:25
  106.4 0.7 copy-done.8
  107.1 5.6 %z_filter_2.1 = (f32[1,128,1024]{2,1,0:T(8,128)}, f32[6,1,128,1024]{3,2,1,0:T(8,128)}) custom-call(s32[1]{0:T(128)} %bitcast.place_ref, bf16[1024,1024]{1,0:T(8,128)(2,1)} %z_filter.5, bf16[4,128,256]{2,1,0:T(8,128)(2,1)} %get-tuple-element.46.refs_0_, bf16[4,128,256]{2,1,0:T(8,128)(2,1)} %copy-done.6, ...), custom_call_target="tpu_custom_call", output_to_operand_aliasing={{1}: (8, {})} | custom-call | flops 1073741824 | bytes 4194304 | tf_op jit(solution)/shard_map/z_filter_2/pallas_call | solution.py:262
  (57 shorter events, 0.2 us)
Async XLA Ops:
  1.5 8.5 %collective-permute-start.3 = (bf16[3,8,1024]{2,1,0:T(8,128)(2,1)S(1)}, bf16[3,8,1024]{2,1,0:T(8,128)(2,1)S(1)}, u32[]{:S(2)}, u32[]{:S(2)}) collective-permute-start(bf16[3,8,1024]{2,1,0:T(8,128)(2,1)S(1)} %get-tuple-element.67), channel_id=1, source_target_pairs={{0,4},{4,8},{8,12},{12,16},{16,20},{20,24},{24,28},{28,0},{1,5},{5... | collective-permute-start | bytes 147464 | tf_op jit(solution)/shard_map/ppermute | solution.py:113
  4.6 5.5 %collective-permute-start.4 = (bf16[3,8,1024]{2,1,0:T(8,128)(2,1)S(1)}, bf16[3,8,1024]{2,1,0:T(8,128)(2,1)S(1)}, u32[]{:S(2)}, u32[]{:S(2)}) collective-permute-start(bf16[3,8,1024]{2,1,0:T(8,128)(2,1)S(1)} %get-tuple-element.68), channel_id=1, source_target_pairs={{4,0},{8,4},{12,8},{16,12},{20,16},{24,20},{28,24},{0,28},{5,1},{9... | collective-permute-start | bytes 147464 | tf_op jit(solution)/shard_map/ppermute | solution.py:114
  5.1 26.0 %collective-permute-start.2 = (bf16[3,32,1024]{2,1,0:T(8,128)(2,1)S(1)}, bf16[3,32,1024]{2,1,0:T(8,128)(2,1)S(1)}, u32[]{:S(2)}, u32[]{:S(2)}) collective-permute-start(bf16[3,32,1024]{2,1,0:T(8,128)(2,1)S(1)} %get-tuple-element.69), channel_id=1, source_target_pairs={{0,3},{1,2},{2,1},{3,0},{4,7},{5,6},{6,5},{7,4},{8,11},{9,10},{10,... | collective-permute-start | bytes 589832 | tf_op jit(solution)/shard_map/ppermute | solution.py:25
  9.4 21.7 %collective-permute-start.1 = (bf16[3,32,1024]{2,1,0:T(8,128)(2,1)S(1)}, bf16[3,32,1024]{2,1,0:T(8,128)(2,1)S(1)}, u32[]{:S(2)}, u32[]{:S(2)}) collective-permute-start(bf16[3,32,1024]{2,1,0:T(8,128)(2,1)S(1)} %get-tuple-element.70), channel_id=1, source_target_pairs={{0,2},{1,3},{2,0},{3,1},{4,6},{5,7},{6,4},{7,5},{8,10},{9,11},{10,... | collective-permute-start | bytes 589832 | tf_op jit(solution)/shard_map/ppermute | solution.py:25
  9.4 21.7 %collective-permute-start = (bf16[3,32,1024]{2,1,0:T(8,128)(2,1)S(1)}, bf16[3,32,1024]{2,1,0:T(8,128)(2,1)S(1)}, u32[]{:S(2)}, u32[]{:S(2)}) collective-permute-start(bf16[3,32,1024]{2,1,0:T(8,128)(2,1)S(1)} %get-tuple-element.71), channel_id=1, source_target_pairs={{0,1},{1,0},{2,3},{3,2},{4,5},{5,4},{6,7},{7,6},{8,9},{9,8},{10,11... | collective-permute-start | bytes 589832 | tf_op jit(solution)/shard_map/ppermute | solution.py:25
  10.9 12.8 %collective-permute-start.7 = (bf16[3,8,1024]{2,1,0:T(8,128)(2,1)S(1)}, bf16[3,8,1024]{2,1,0:T(8,128)(2,1)S(1)}, u32[]{:S(2)}, u32[]{:S(2)}) collective-permute-start(bf16[3,8,1024]{2,1,0:T(8,128)(2,1)S(1)} %get-tuple-element.63), channel_id=1, source_target_pairs={{0,3},{1,2},{2,1},{3,0},{4,7},{5,6},{6,5},{7,4},{8,11},{9,10},{10,... | collective-permute-start | bytes 147464 | tf_op jit(solution)/shard_map/ppermute | solution.py:25
  14.6 14.4 %collective-permute-start.5 = (bf16[3,8,1024]{2,1,0:T(8,128)(2,1)S(1)}, bf16[3,8,1024]{2,1,0:T(8,128)(2,1)S(1)}, u32[]{:S(2)}, u32[]{:S(2)}) collective-permute-start(bf16[3,8,1024]{2,1,0:T(8,128)(2,1)S(1)} %get-tuple-element.64), channel_id=1, source_target_pairs={{0,1},{1,0},{2,3},{3,2},{4,5},{5,4},{6,7},{7,6},{8,9},{9,8},{10,11... | collective-permute-start | bytes 147464 | tf_op jit(solution)/shard_map/ppermute | solution.py:25
  23.7 7.4 %copy-start.18 = (bf16[3,8,1024]{2,1,0:T(8,128)(2,1)}, bf16[3,8,1024]{2,1,0:T(8,128)(2,1)S(1)}, u32[]{:S(2)}) copy-start(bf16[3,8,1024]{2,1,0:T(8,128)(2,1)S(1)} %collective-permute-done.7.refs_7_) | copy-start | bytes 147460
  23.7 7.4 %collective-permute-start.6 = (bf16[3,8,1024]{2,1,0:T(8,128)(2,1)S(1)}, bf16[3,8,1024]{2,1,0:T(8,128)(2,1)S(1)}, u32[]{:S(2)}, u32[]{:S(2)}) collective-permute-start(bf16[3,8,1024]{2,1,0:T(8,128)(2,1)S(1)} %get-tuple-element.65), channel_id=1, source_target_pairs={{0,2},{1,3},{2,0},{3,1},{4,6},{5,7},{6,4},{7,5},{8,10},{9,11},{10,... | collective-permute-start | bytes 147464 | tf_op jit(solution)/shard_map/ppermute | solution.py:25
  29.0 2.1 %copy-start.19 = (bf16[3,8,1024]{2,1,0:T(8,128)(2,1)}, bf16[3,8,1024]{2,1,0:T(8,128)(2,1)S(1)}, u32[]{:S(2)}) copy-start(bf16[3,8,1024]{2,1,0:T(8,128)(2,1)S(1)} %collective-permute-done.5.refs_5_) | copy-start | bytes 147460
  31.1 0.6 copy-start.20
  31.1 0.7 copy-start.9
  31.1 0.8 copy-start.10
  31.1 0.8 copy-start.11
  40.8 8.2 %collective-permute-start.8 = (bf16[1,32,1024]{2,1,0:T(8,128)(2,1)}, bf16[1,32,1024]{2,1,0:T(8,128)(2,1)S(1)}, u32[]{:S(2)}, u32[]{:S(2)}) collective-permute-start(bf16[1,32,1024]{2,1,0:T(8,128)(2,1)} %get-tuple-element.35), channel_id=1, source_target_pairs={{0,1},{1,0},{2,3},{3,2},{4,5},{5,4},{6,7},{7,6},{8,9},{9,8},{10,11... | collective-permute-start | bytes 196616 | tf_op jit(solution)/shard_map/ppermute | solution.py:25
  42.8 9.1 %collective-permute-start.9 = (bf16[1,32,1024]{2,1,0:T(8,128)(2,1)}, bf16[1,32,1024]{2,1,0:T(8,128)(2,1)S(1)}, u32[]{:S(2)}, u32[]{:S(2)}) collective-permute-start(bf16[1,32,1024]{2,1,0:T(8,128)(2,1)} %get-tuple-element.36), channel_id=1, source_target_pairs={{0,2},{1,3},{2,0},{3,1},{4,6},{5,7},{6,4},{7,5},{8,10},{9,11},{10,... | collective-permute-start | bytes 196616 | tf_op jit(solution)/shard_map/ppermute | solution.py:25
  43.8 8.1 %collective-permute-start.10 = (bf16[1,32,1024]{2,1,0:T(8,128)(2,1)}, bf16[1,32,1024]{2,1,0:T(8,128)(2,1)S(1)}, u32[]{:S(2)}, u32[]{:S(2)}) collective-permute-start(bf16[1,32,1024]{2,1,0:T(8,128)(2,1)} %get-tuple-element.37), channel_id=1, source_target_pairs={{0,3},{1,2},{2,1},{3,0},{4,7},{5,6},{6,5},{7,4},{8,11},{9,10},{10,... | collective-permute-start | bytes 196616 | tf_op jit(solution)/shard_map/ppermute | solution.py:25
  45.9 12.3 %collective-permute-start.12 = (bf16[1,32,1024]{2,1,0:T(8,128)(2,1)}, bf16[1,32,1024]{2,1,0:T(8,128)(2,1)S(1)}, u32[]{:S(2)}, u32[]{:S(2)}) collective-permute-start(bf16[1,32,1024]{2,1,0:T(8,128)(2,1)} %get-tuple-element.39), channel_id=1, source_target_pairs={{0,1},{1,0},{2,3},{3,2},{4,5},{5,4},{6,7},{7,6},{8,9},{9,8},{10,11... | collective-permute-start | bytes 196616 | tf_op jit(solution)/shard_map/ppermute | solution.py:25
  47.0 12.8 %collective-permute-start.13 = (bf16[1,32,1024]{2,1,0:T(8,128)(2,1)}, bf16[1,32,1024]{2,1,0:T(8,128)(2,1)S(1)}, u32[]{:S(2)}, u32[]{:S(2)}) collective-permute-start(bf16[1,32,1024]{2,1,0:T(8,128)(2,1)} %get-tuple-element.40), channel_id=1, source_target_pairs={{0,2},{1,3},{2,0},{3,1},{4,6},{5,7},{6,4},{7,5},{8,10},{9,11},{10,... | collective-permute-start | bytes 196616 | tf_op jit(solution)/shard_map/ppermute | solution.py:25
  49.0 10.8 %collective-permute-start.14 = (bf16[1,32,1024]{2,1,0:T(8,128)(2,1)}, bf16[1,32,1024]{2,1,0:T(8,128)(2,1)S(1)}, u32[]{:S(2)}, u32[]{:S(2)}) collective-permute-start(bf16[1,32,1024]{2,1,0:T(8,128)(2,1)} %get-tuple-element.41), channel_id=1, source_target_pairs={{0,3},{1,2},{2,1},{3,0},{4,7},{5,6},{6,5},{7,4},{8,11},{9,10},{10,... | collective-permute-start | bytes 196616 | tf_op jit(solution)/shard_map/ppermute | solution.py:25
  51.9 9.4 %collective-permute-start.16 = (bf16[1,32,1024]{2,1,0:T(8,128)(2,1)}, bf16[1,32,1024]{2,1,0:T(8,128)(2,1)S(1)}, u32[]{:S(2)}, u32[]{:S(2)}) collective-permute-start(bf16[1,32,1024]{2,1,0:T(8,128)(2,1)} %get-tuple-element.43), channel_id=1, source_target_pairs={{0,1},{1,0},{2,3},{3,2},{4,5},{5,4},{6,7},{7,6},{8,9},{9,8},{10,11... | collective-permute-start | bytes 196616 | tf_op jit(solution)/shard_map/ppermute | solution.py:25
  51.9 9.3 %collective-permute-start.17 = (bf16[1,32,1024]{2,1,0:T(8,128)(2,1)}, bf16[1,32,1024]{2,1,0:T(8,128)(2,1)S(1)}, u32[]{:S(2)}, u32[]{:S(2)}) collective-permute-start(bf16[1,32,1024]{2,1,0:T(8,128)(2,1)} %get-tuple-element.44), channel_id=1, source_target_pairs={{0,2},{1,3},{2,0},{3,1},{4,6},{5,7},{6,4},{7,5},{8,10},{9,11},{10,... | collective-permute-start | bytes 196616 | tf_op jit(solution)/shard_map/ppermute | solution.py:25
  58.1 7.9 %copy-start = (bf16[4,1,32,1024]{3,2,1,0:T(8,128)(2,1)}, bf16[4,1,32,1024]{3,2,1,0:T(8,128)(2,1)S(1)}, u32[]{:S(2)}) copy-start(bf16[4,1,32,1024]{3,2,1,0:T(8,128)(2,1)S(1)} %pad_maximum_fusion.1.refs_0_) | copy-start | bytes 786436
  58.2 6.3 %collective-permute-start.18 = (bf16[1,32,1024]{2,1,0:T(8,128)(2,1)}, bf16[1,32,1024]{2,1,0:T(8,128)(2,1)S(1)}, u32[]{:S(2)}, u32[]{:S(2)}) collective-permute-start(bf16[1,32,1024]{2,1,0:T(8,128)(2,1)} %get-tuple-element.45), channel_id=1, source_target_pairs={{0,3},{1,2},{2,1},{3,0},{4,7},{5,6},{6,5},{7,4},{8,11},{9,10},{10,... | collective-permute-start | bytes 196616 | tf_op jit(solution)/shard_map/ppermute | solution.py:25
  59.8 6.2 %collective-permute-start.11 = (bf16[4,1,32,1024]{3,2,1,0:T(8,128)(2,1)S(1)}, bf16[4,1,32,1024]{3,2,1,0:T(8,128)(2,1)S(1)}, u32[]{:S(2)}, u32[]{:S(2)}) collective-permute-start(bf16[4,1,32,1024]{3,2,1,0:T(8,128)(2,1)S(1)} %pad_maximum_fusion.1.refs_0_), channel_id=1, source_target_pairs={{0,8},{8,0},{16,24},{24,16},{1,9},{9,1},{17,25},{25,17},{2,10},{10... | collective-permute-start | bytes 786440 | tf_op jit(solution)/shard_map/ppermute | solution.py:25
  60.7 9.8 %copy-start.2 = (bf16[4,1,32,1024]{3,2,1,0:T(8,128)(2,1)}, bf16[4,1,32,1024]{3,2,1,0:T(8,128)(2,1)S(1)}, u32[]{:S(2)}) copy-start(bf16[4,1,32,1024]{3,2,1,0:T(8,128)(2,1)S(1)} %pad_maximum_fusion.2.refs_2_) | copy-start | bytes 786436
  60.7 11.3 %collective-permute-start.15 = (bf16[4,1,32,1024]{3,2,1,0:T(8,128)(2,1)S(1)}, bf16[4,1,32,1024]{3,2,1,0:T(8,128)(2,1)S(1)}, u32[]{:S(2)}, u32[]{:S(2)}) collective-permute-start(bf16[4,1,32,1024]{3,2,1,0:T(8,128)(2,1)S(1)} %pad_maximum_fusion.2.refs_2_), channel_id=1, source_target_pairs={{0,8},{8,0},{16,24},{24,16},{1,9},{9,1},{17,25},{25,17},{2,10},{10... | collective-permute-start | bytes 786440 | tf_op jit(solution)/shard_map/ppermute | solution.py:25
  65.4 17.2 %copy-start.3 = (bf16[4,1,32,1024]{3,2,1,0:T(8,128)(2,1)}, bf16[4,1,32,1024]{3,2,1,0:T(8,128)(2,1)S(1)}, u32[]{:S(2)}) copy-start(bf16[4,1,32,1024]{3,2,1,0:T(8,128)(2,1)S(1)} %pad_maximum_fusion.3.refs_4_) | copy-start | bytes 786436
  65.4 15.2 %collective-permute-start.19 = (bf16[4,1,32,1024]{3,2,1,0:T(8,128)(2,1)S(1)}, bf16[4,1,32,1024]{3,2,1,0:T(8,128)(2,1)S(1)}, u32[]{:S(2)}, u32[]{:S(2)}) collective-permute-start(bf16[4,1,32,1024]{3,2,1,0:T(8,128)(2,1)S(1)} %pad_maximum_fusion.3.refs_4_), channel_id=1, source_target_pairs={{0,8},{8,0},{16,24},{24,16},{1,9},{9,1},{17,25},{25,17},{2,10},{10... | collective-permute-start | bytes 786440 | tf_op jit(solution)/shard_map/ppermute | solution.py:25
  66.0 0.7 copy-start.1
  70.5 7.1 %copy-start.22 = (bf16[2,128,256]{2,1,0:T(8,128)(2,1)S(1)}, bf16[2,128,256]{2,1,0:T(8,128)(2,1)}, u32[]{:S(2)}) copy-start(bf16[2,128,256]{2,1,0:T(8,128)(2,1)} %get-tuple-element.52) | copy-start | bytes 393220
  70.5 8.6 %copy-start.21 = (bf16[2,128,256]{2,1,0:T(8,128)(2,1)S(1)}, bf16[2,128,256]{2,1,0:T(8,128)(2,1)}, u32[]{:S(2)}) copy-start(bf16[2,128,256]{2,1,0:T(8,128)(2,1)} %get-tuple-element.53) | copy-start | bytes 393220
  70.5 11.2 %collective-permute-start.23 = (bf16[2,128,256]{2,1,0:T(8,128)(2,1)}, bf16[2,128,256]{2,1,0:T(8,128)(2,1)S(1)}, u32[]{:S(2)}, u32[]{:S(2)}) collective-permute-start(bf16[2,128,256]{2,1,0:T(8,128)(2,1)} %get-tuple-element.51), channel_id=1, source_target_pairs={{0,4},{4,0},{8,12},{12,8},{16,20},{20,16},{24,28},{28,24},{1,5},{5... | collective-permute-start | bytes 393224 | tf_op jit(solution)/shard_map/ppermute | solution.py:25
  72.0 0.7 copy-start.4
  77.0 13.1 %collective-permute-start.26 = (bf16[3,128,256]{2,1,0:T(8,128)(2,1)}, bf16[3,128,256]{2,1,0:T(8,128)(2,1)S(1)}, u32[]{:S(2)}, u32[]{:S(2)}) collective-permute-start(bf16[3,128,256]{2,1,0:T(8,128)(2,1)} %get-tuple-element.56), channel_id=1, source_target_pairs={{0,4},{4,0},{8,12},{12,8},{16,20},{20,16},{24,28},{28,24},{1,5},{5... | collective-permute-start | bytes 589832 | tf_op jit(solution)/shard_map/ppermute | solution.py:25
  77.6 9.7 %collective-permute-start.24 = (bf16[2,128,256]{2,1,0:T(8,128)(2,1)S(1)}, bf16[2,128,256]{2,1,0:T(8,128)(2,1)S(1)}, u32[]{:S(2)}, u32[]{:S(2)}) collective-permute-start(bf16[2,128,256]{2,1,0:T(8,128)(2,1)S(1)} %copy-done.22), channel_id=1, source_target_pairs={{0,16},{4,20},{8,24},{12,28},{16,0},{20,4},{24,8},{28,12},{1,17},{... | collective-permute-start | bytes 393224 | tf_op jit(solution)/shard_map/ppermute | solution.py:25
  79.1 9.8 %collective-permute-start.25 = (bf16[2,128,256]{2,1,0:T(8,128)(2,1)S(1)}, bf16[2,128,256]{2,1,0:T(8,128)(2,1)S(1)}, u32[]{:S(2)}, u32[]{:S(2)}) collective-permute-start(bf16[2,128,256]{2,1,0:T(8,128)(2,1)S(1)} %copy-done.21), channel_id=1, source_target_pairs={{0,20},{4,16},{8,28},{12,24},{16,4},{20,0},{24,12},{28,8},{1,21},{... | collective-permute-start | bytes 393224 | tf_op jit(solution)/shard_map/ppermute | solution.py:25
  80.5 2.0 %copy-start.5 = (bf16[4,1,32,1024]{3,2,1,0:T(8,128)(2,1)}, bf16[4,1,32,1024]{3,2,1,0:T(8,128)(2,1)S(1)}, u32[]{:S(2)}) copy-start(bf16[4,1,32,1024]{3,2,1,0:T(8,128)(2,1)S(1)} %collective-permute-done.19.refs_5_) | copy-start | bytes 786436
  80.5 14.6 %collective-permute-start.27 = (bf16[3,128,256]{2,1,0:T(8,128)(2,1)}, bf16[3,128,256]{2,1,0:T(8,128)(2,1)S(1)}, u32[]{:S(2)}, u32[]{:S(2)}) collective-permute-start(bf16[3,128,256]{2,1,0:T(8,128)(2,1)} %get-tuple-element.57), channel_id=1, source_target_pairs={{0,16},{4,20},{8,24},{12,28},{16,0},{20,4},{24,8},{28,12},{1,17},{... | collective-permute-start | bytes 589832 | tf_op jit(solution)/shard_map/ppermute | solution.py:25
  81.7 5.7 %copy-start.15 = (bf16[2,128,256]{2,1,0:T(8,128)(2,1)}, bf16[2,128,256]{2,1,0:T(8,128)(2,1)S(1)}, u32[]{:S(2)}) copy-start(bf16[2,128,256]{2,1,0:T(8,128)(2,1)S(1)} %collective-permute-done.23.refs_1_) | copy-start | bytes 393220
  81.7 14.5 %collective-permute-start.28 = (bf16[3,128,256]{2,1,0:T(8,128)(2,1)}, bf16[3,128,256]{2,1,0:T(8,128)(2,1)S(1)}, u32[]{:S(2)}, u32[]{:S(2)}) collective-permute-start(bf16[3,128,256]{2,1,0:T(8,128)(2,1)} %get-tuple-element.58), channel_id=1, source_target_pairs={{0,20},{4,16},{8,28},{12,24},{16,4},{20,0},{24,12},{28,8},{1,21},{... | collective-permute-start | bytes 589832 | tf_op jit(solution)/shard_map/ppermute | solution.py:25
  87.4 3.6 %copy-start.16 = (bf16[2,128,256]{2,1,0:T(8,128)(2,1)}, bf16[2,128,256]{2,1,0:T(8,128)(2,1)S(1)}, u32[]{:S(2)}) copy-start(bf16[2,128,256]{2,1,0:T(8,128)(2,1)S(1)} %collective-permute-done.24.refs_2_) | copy-start | bytes 393220
  87.4 14.4 %collective-permute-start.20 = (bf16[4,128,256]{2,1,0:T(8,128)(2,1)}, bf16[4,128,256]{2,1,0:T(8,128)(2,1)S(1)}, u32[]{:S(2)}, u32[]{:S(2)}) collective-permute-start(bf16[4,128,256]{2,1,0:T(8,128)(2,1)} %get-tuple-element.47), channel_id=1, source_target_pairs={{0,4},{4,0},{8,12},{12,8},{16,20},{20,16},{24,28},{28,24},{1,5},{5... | collective-permute-start | bytes 786440 | tf_op jit(solution)/shard_map/ppermute | solution.py:25
  88.9 2.0 %copy-start.17 = (bf16[2,128,256]{2,1,0:T(8,128)(2,1)}, bf16[2,128,256]{2,1,0:T(8,128)(2,1)S(1)}, u32[]{:S(2)}) copy-start(bf16[2,128,256]{2,1,0:T(8,128)(2,1)S(1)} %collective-permute-done.25.refs_3_) | copy-start | bytes 393220
  88.9 12.9 %collective-permute-start.21 = (bf16[4,128,256]{2,1,0:T(8,128)(2,1)}, bf16[4,128,256]{2,1,0:T(8,128)(2,1)S(1)}, u32[]{:S(2)}, u32[]{:S(2)}) collective-permute-start(bf16[4,128,256]{2,1,0:T(8,128)(2,1)} %get-tuple-element.48), channel_id=1, source_target_pairs={{0,16},{4,20},{8,24},{12,28},{16,0},{20,4},{24,8},{28,12},{1,17},{... | collective-permute-start | bytes 786440 | tf_op jit(solution)/shard_map/ppermute | solution.py:25
  90.1 6.1 %copy-start.12 = (bf16[3,128,256]{2,1,0:T(8,128)(2,1)}, bf16[3,128,256]{2,1,0:T(8,128)(2,1)S(1)}, u32[]{:S(2)}) copy-start(bf16[3,128,256]{2,1,0:T(8,128)(2,1)S(1)} %collective-permute-done.26.refs_1_) | copy-start | bytes 589828
  90.1 16.3 %collective-permute-start.22 = (bf16[4,128,256]{2,1,0:T(8,128)(2,1)}, bf16[4,128,256]{2,1,0:T(8,128)(2,1)S(1)}, u32[]{:S(2)}, u32[]{:S(2)}) collective-permute-start(bf16[4,128,256]{2,1,0:T(8,128)(2,1)} %get-tuple-element.49), channel_id=1, source_target_pairs={{0,20},{4,16},{8,28},{12,24},{16,4},{20,0},{24,12},{28,8},{1,21},{... | collective-permute-start | bytes 786440 | tf_op jit(solution)/shard_map/ppermute | solution.py:25
  95.2 1.0 copy-start.13
  96.2 0.7 copy-start.14
  101.8 4.6 %copy-start.6 = (bf16[4,128,256]{2,1,0:T(8,128)(2,1)}, bf16[4,128,256]{2,1,0:T(8,128)(2,1)S(1)}, u32[]{:S(2)}) copy-start(bf16[4,128,256]{2,1,0:T(8,128)(2,1)S(1)} %collective-permute-done.20.refs_1_) | copy-start | bytes 786436
  101.8 4.6 %copy-start.7 = (bf16[4,128,256]{2,1,0:T(8,128)(2,1)}, bf16[4,128,256]{2,1,0:T(8,128)(2,1)S(1)}, u32[]{:S(2)}) copy-start(bf16[4,128,256]{2,1,0:T(8,128)(2,1)S(1)} %collective-permute-done.21.refs_2_) | copy-start | bytes 786436
  106.4 0.7 copy-start.8

commit v2 on v0

--- a/solution.py
+++ b/solution.py
@@ -1,11 +1,347 @@
+import functools
+
 import jax
 import jax.numpy as jnp
 from jax import lax
+from jax.experimental import pallas as pl
+from jax.experimental.pallas import tpu as pltpu
 from jax.sharding import PartitionSpec as P
 
 STEP_SIZE = 0.25
 VISCOSITY = 0.8
 PRODUCT_PAIRS = ((0, 0), (0, 1), (0, 2), (1, 1), (1, 2), (2, 2))
+FIELDS = 3 + len(PRODUCT_PAIRS)
+
+PLANE = ("grp", "row")
+WIRE = jnp.bfloat16
+CHUNKS = ((0,), (1, 2), (3,))
+CHIPS = (0, 1, 4, 5)
+HALO = 8
+REACH = 3
+VMEM_BYTES = 32 * 1024 * 1024
+NT = (((1,), (1,)), ((), ()))
+TN = (((0,), (0,)), ((), ()))
+TAIL_PARTS = 2
+WAITED = 3
+COSTS = dict(prepare=3.0, advance=5.0, x_filter_0=0.1, x_filter_1=0.1, x_filter_2=0.1, x_filter_3=0.1, z_filter_first=0.1, z_filter_last=0.1)
+
+
+def cost(name):
+    return pl.CostEstimate(flops=0, bytes_accessed=int(3.7e6 * COSTS[name]), transcendentals=0)
+
+
+def exchange(value, axis, flip):
+    count = lax.axis_size(axis)
+    return lax.ppermute(value, axis, [(i, i ^ flip) for i in range(count)])
+
+
+def delayed(value, *earlier):
+    return lax.optimization_barrier((value, earlier))[0]
+
+
+def whole(memory=pltpu.VMEM):
+    return pl.BlockSpec(memory_space=memory)
+
+
+def prepare_kernel(slabs, place_ref, x_filters, z_filter, rows_out, *refs):
+    lines_out, (sem,) = refs[: len(CHUNKS)], refs[len(CHUNKS) :]
+    q, me, prof = place_ref[0], place_ref[1], place_ref[2]
+    copies = []
+    for slot, flip in enumerate(CHIPS):
+        at = pl.multiple_of((me ^ flip) * 128, 128)
+        copies.append(
+            pltpu.make_async_copy(
+                x_filters.at[prof, pl.ds(at, 128)], rows_out.at[pl.ds(slot * 128, 128)], sem.at[slot]
+            )
+        )
+        copies[-1].start()
+    rows = 128 // slabs
+    picks = []
+    for flips in CHUNKS:
+        per_core = rows * len(flips)
+        target = lax.broadcasted_iota(jnp.int32, (2 * per_core, 256), 0)
+        source = lax.broadcasted_iota(jnp.int32, (2 * per_core, 256), 1)
+        core, inner = target // per_core, target % per_core
+        wanted = core * 128 + rows * (q ^ (flips[0] + inner // rows)) + inner % rows
+        picks.append((source == wanted).astype(jnp.bfloat16))
+    pick = jnp.concatenate(picks, axis=0)
+    for slot, flip in enumerate(CHIPS):
+        low = (me ^ flip) & ~2
+        pair = jnp.concatenate(
+            [z_filter[:, pl.ds(pl.multiple_of(128 * (low + 2 * core), 128), 128)] for core in range(2)], axis=1
+        )
+        picked = lax.dot_general(pick, pair, NT, preferred_element_type=jnp.float32).astype(jnp.bfloat16)
+        at = 0
+        for number, flips in enumerate(CHUNKS):
+            cells = 2 * rows * len(flips)
+            lines_out[number][slot * cells : (slot + 1) * cells] = picked[at : at + cells]
+            at += cells
+    for copy in copies:
+        copy.wait()
+
+
+def step_kernel(slabs, q_ref, *refs):
+    mains, halos = refs[:slabs], refs[slabs : 2 * slabs]
+    outs, (start, one, two, done) = refs[2 * slabs : -4], refs[-4:]
+    q = q_ref[0]
+    rows, width = outs[0].shape[-2:]
+    parts = width // 128
+    for buffer in (start, one, two):
+        buffer[0] = jnp.zeros(buffer.shape[1:], buffer.dtype)
+        buffer[slabs + 1] = jnp.zeros(buffer.shape[1:], buffer.dtype)
+    for flip in range(slabs):
+        y = (q ^ flip) + 1
+        for comp in range(3):
+            for row in range(0, rows, 16):
+                block = mains[flip][comp, row : row + 16].astype(jnp.float32)
+                for half in range(2):
+                    for part in range(parts):
+                        at = (REACH + row + 8 * half) * 8 + part
+                        start[y, comp, pl.ds(at, 8, stride=8)] = block[
+                            8 * half : 8 * half + 8, 128 * part : 128 * part + 128
+                        ]
+            halo = halos[flip][comp].astype(jnp.float32)
+            for part in range(parts):
+                lanes = halo[:, 128 * part : 128 * part + 128]
+                start[y, comp, pl.ds((REACH + rows) * 8 + part, REACH, stride=8)] = lanes[:REACH]
+                start[y, comp, pl.ds(part, REACH, stride=8)] = lanes[HALO - REACH :]
+
+    lane = lax.broadcasted_iota(jnp.int32, (8, 128), 1)
+    at_end, at_start = lane == 127, lane == 0
+
+    def sweep(src, y, first, count, emit):
+        behind = [src[y, comp, 8 * first - 8 : 8 * first] for comp in range(3)]
+        here = [src[y, comp, 8 * first : 8 * first + 8] for comp in range(3)]
+        for row in range(first, first + count):
+            ahead = [src[y, comp, 8 * row + 8 : 8 * row + 16] for comp in range(3)]
+            lower, upper = [], []
+            for comp in range(3):
+                drift = (0.5 * STEP_SIZE) * here[comp]
+                upper.append(STEP_SIZE * VISCOSITY - drift)
+                lower.append(STEP_SIZE * VISCOSITY + drift)
+            for comp in range(3):
+                center = here[comp]
+                next_lane = pltpu.roll(center, 127, 1)
+                x_next = jnp.where(at_end, pltpu.roll(next_lane, 7, 0), next_lane)
+                prev_lane = pltpu.roll(center, 1, 1)
+                x_prev = jnp.where(at_start, pltpu.roll(prev_lane, 1, 0), prev_lane)
+                y_next = src[y + 1, comp, 8 * row : 8 * row + 8]
+                y_prev = src[y - 1, comp, 8 * row : 8 * row + 8]
+                along_x = upper[0] * x_next + lower[0] * x_prev
+                along_y = upper[1] * y_next + lower[1] * y_prev
+                along_z = upper[2] * ahead[comp] + lower[2] * behind[comp]
+                rest = (1.0 - 6.0 * STEP_SIZE * VISCOSITY) * center
+                emit(row, comp, (along_x + along_y) + (along_z + rest))
+            behind, here = here, ahead
+
+    def section_one(number, carry):
+        y = number + 1
+
+        def emit(row, comp, moved):
+            one[y, comp, 8 * row : 8 * row + 8] = moved
+
+        sweep(start, y, 1, rows + 2 * REACH - 2, emit)
+        return carry
+
+    def section_two(number, carry):
+        y = number + 1
+
+        def emit(row, comp, moved):
+            at = slice(8 * row, 8 * row + 8)
+            two[y, comp, at] = 0.75 * start[y, comp, at] + 0.25 * moved
+
+        sweep(one, y, 2, rows + 2 * REACH - 4, emit)
+        return carry
+
+    def section_three(number, carry):
+        y = number + 1
+
+        def emit(row, comp, moved):
+            at = slice(8 * row, 8 * row + 8)
+            to = slice(8 * (row - REACH), 8 * (row - REACH) + 8)
+            done[number, comp, to] = (1.0 / 3.0) * start[y, comp, at] + (2.0 / 3.0) * moved
+
+        sweep(two, y, REACH, rows, emit)
+        return carry
+
+    lax.fori_loop(0, slabs, section_one, 0)
+    lax.fori_loop(0, slabs, section_two, 0)
+    lax.fori_loop(0, slabs, section_three, 0)
+    for flip in range(slabs):
+        for comp in range(3):
+            for row in range(0, rows, 16):
+                for part in range(parts):
+                    pair = [done[q ^ flip, comp, pl.ds((row + at) * 8 + part, 8, stride=8)] for at in (0, 8)]
+                    outs[flip][comp, row : row + 16, 128 * part : 128 * part + 128] = jnp.concatenate(
+                        pair, axis=0
+                    ).astype(outs[flip].dtype)
+
+
+def advance(velocity, filters):
+    slabs, plane = lax.axis_size("col"), lax.axis_size(PLANE)
+    q = lax.axis_index("col").astype(jnp.int32)
+    v = velocity[:, 0]
+    block, width = v.shape[1:]
+    rows = block // slabs
+    narrow = v.astype(WIRE)
+    tail = lax.ppermute(narrow[:, block - HALO :], PLANE, [(j, (j + 1) % plane) for j in range(plane)])
+    head = lax.ppermute(narrow[:, :HALO], PLANE, [((j + 1) % plane, j) for j in range(plane)])
+    mains = [lax.dynamic_slice_in_dim(v, rows * q, rows, 1)]
+    for flip in range(1, slabs):
+        mains.append(exchange(lax.dynamic_slice_in_dim(narrow, rows * (q ^ flip), rows, 1), "col", flip))
+    low = lax.broadcasted_iota(jnp.int32, (3, HALO, width), 1) < HALO // 2
+    halos = []
+    for flip in range(slabs):
+        at = rows * (q ^ flip)
+        before = lax.dynamic_slice_in_dim(narrow, jnp.maximum(at - HALO, 0), HALO, 1)
+        after = lax.dynamic_slice_in_dim(narrow, jnp.minimum(at + rows, block - HALO), HALO, 1)
+        before = jnp.where(at == 0, tail, before)
+        after = jnp.where(at == block - rows, head, after)
+        halos.append(jnp.where(low, after, before))
+    halos[1], mains[1] = lax.optimization_barrier((halos[1], mains[1]))
+    for flip in (3, 2, 1):
+        halos[flip] = exchange(halos[flip], "col", flip)
+    mains, halos, filters = lax.optimization_barrier((mains, halos, filters))
+
+    lines = 8 * (rows + 2 * REACH)
+    pieces = pl.pallas_call(
+        functools.partial(step_kernel, slabs),
+        out_shape=[jax.ShapeDtypeStruct((3, rows, width), WIRE)] * slabs,
+        in_specs=[whole(pltpu.SMEM)] + [whole()] * (2 * slabs),
+        out_specs=[whole()] * slabs,
+        scratch_shapes=[pltpu.VMEM((slabs + 2, 3, lines, 128), jnp.float32)] * 3
+        + [pltpu.VMEM((slabs, 3, 8 * rows, 128), jnp.float32)],
+        compiler_params=pltpu.CompilerParams(vmem_limit_bytes=VMEM_BYTES),
+        cost_estimate=cost("advance"),
+        name="advance",
+    )(q.reshape(1), *mains, *halos)
+    pieces = list(pieces)
+    pieces[1], pieces[2] = exchange(pieces[1], "col", 1), exchange(pieces[2], "col", 2)
+    pieces[3] = exchange(pieces[3], "col", 3)
+    return pieces, filters
+
+
+def x_kernel(place_ref, matrix, *refs):
+    inputs, outs, (fields,) = refs[: -len(CHIPS) - 1], refs[-len(CHIPS) - 1 : -1], refs[-1:]
+    core = (place_ref[1] // 2) % 2
+    half = len(inputs) // 2
+    for other in range(2):
+        for piece in range(half):
+            ref = inputs[other * half + piece]
+            rows = ref.shape[1]
+            at = pl.multiple_of(rows * (half * (core ^ other) + piece), rows)
+            for comp in range(3):
+                fields[comp, pl.ds(at, rows)] = ref[comp]
+            for number, (a, b) in enumerate(PRODUCT_PAIRS):
+                product = ref[a].astype(jnp.float32) * ref[b].astype(jnp.float32)
+                fields[3 + number, pl.ds(at, rows)] = product.astype(jnp.bfloat16)
+    cells = fields.shape[1]
+    group = fields[...].reshape(FIELDS * cells, fields.shape[2])
+    result = lax.dot_general(group, matrix[...], NT, preferred_element_type=jnp.float32)
+    for number in range(FIELDS):
+        for slot in range(len(CHIPS)):
+            part = result[number * cells : (number + 1) * cells, slot * 128 : (slot + 1) * 128]
+            outs[slot][number] = part.astype(jnp.bfloat16)
+
+
+def z_sum(lines, blocks, columns):
+    left = jnp.concatenate(
+        [jnp.concatenate([block[number] for number in range(FIELDS)], axis=1) for block in blocks], axis=0
+    )
+    right = jnp.concatenate([line[:, columns] for line in lines], axis=0)
+    return lax.dot_general(left, right, TN, preferred_element_type=jnp.float32)
+
+
+def z_first_kernel(*refs):
+    count = (len(refs) - 1) // (1 + len(CHIPS))
+    lines, blocks, passed = refs[:count], refs[count:-1], refs[-1]
+    passed[...] = z_sum(lines, blocks, slice(None)).reshape(passed.shape)
+
+
+def z_last_kernel(passed, lines, *refs):
+    blocks, (stress, made, sem) = refs[: len(CHIPS)], refs[len(CHIPS) :]
+    copies = []
+    width = passed.shape[2] // TAIL_PARTS
+    for part in range(TAIL_PARTS):
+        columns = slice(part * width, (part + 1) * width)
+        result = z_sum([lines], blocks, columns)
+        total = [passed[at, :, columns] + result[at * 128 : (at + 1) * 128] for at in range(FIELDS)]
+        for at, (a, b) in enumerate(PRODUCT_PAIRS):
+            made[at, :, columns] = total[3 + at] - total[a] * total[b]
+        copies.append(pltpu.make_async_copy(made.at[:, :, columns], stress.at[:, 0, :, columns], sem.at[part]))
+        copies[-1].start()
+    for copy in copies:
+        copy.wait()
+
+
+def fast_body(velocity, profile, x_filters, z_filter):
+    width = velocity.shape[3]
+    slabs = lax.axis_size("col")
+    q = lax.axis_index("col").astype(jnp.int32)
+    me = lax.axis_index(PLANE).astype(jnp.int32)
+    place = jnp.stack([q, me, profile[0]])
+    params = pltpu.CompilerParams(vmem_limit_bytes=VMEM_BYTES)
+    sizes = [2 * len(flips) * 128 // slabs for flips in CHUNKS]
+    matrix, *lines = pl.pallas_call(
+        functools.partial(prepare_kernel, slabs),
+        out_shape=[jax.ShapeDtypeStruct((128 * len(CHIPS), width), jnp.bfloat16)]
+        + [jax.ShapeDtypeStruct((len(CHIPS) * cells, z_filter.shape[0]), jnp.bfloat16) for cells in sizes],
+        in_specs=[whole(pltpu.SMEM), whole(pl.ANY), whole()],
+        out_specs=[whole()] * (1 + len(CHUNKS)),
+        scratch_shapes=[pltpu.SemaphoreType.DMA((len(CHIPS),))],
+        compiler_params=params,
+        cost_estimate=cost("prepare"),
+        name="prepare",
+    )(place, x_filters, z_filter)
+
+    pieces, (matrix, *lines) = advance(velocity, (matrix, *lines))
+    blocks = []
+    for number, flips in enumerate(CHUNKS):
+        mine = [pieces[flip] for flip in flips]
+        theirs = [exchange(piece, "grp", 1) for piece in mine]
+        cells = sizes[number]
+        made = pl.pallas_call(
+            x_kernel,
+            out_shape=[jax.ShapeDtypeStruct((FIELDS, cells, 128), jnp.bfloat16)] * len(CHIPS),
+            in_specs=[whole(pltpu.SMEM)] + [whole()] * (1 + 2 * len(flips)),
+            out_specs=[whole()] * len(CHIPS),
+            scratch_shapes=[pltpu.VMEM((FIELDS, cells, width), jnp.bfloat16)],
+            compiler_params=params,
+            cost_estimate=cost(f"x_filter_{number}"),
+            name=f"x_filter_{number}",
+        )(place, matrix, *mine, *theirs)
+        made = list(made)
+        if number == len(CHUNKS) - 1:
+            made = delayed(made, *blocks[-1][1:WAITED])
+        if number == 1:
+            made[3] = delayed(made[3], pieces[3])
+        blocks.append([made[0]] + [exchange(made[slot], PLANE, CHIPS[slot]) for slot in range(1, len(CHIPS))])
+        if number == 0:
+            for flip in CHUNKS[1]:
+                pieces[flip] = delayed(pieces[flip], *blocks[0][1:])
+    early = len(CHUNKS) - 1
+    passed = pl.pallas_call(
+        z_first_kernel,
+        out_shape=jax.ShapeDtypeStruct((FIELDS, 128, width), jnp.float32),
+        in_specs=[whole()] * (early * (1 + len(CHIPS))),
+        out_specs=whole(),
+        compiler_params=params,
+        cost_estimate=cost("z_filter_first"),
+        name="z_filter_first",
+    )(*lines[:early], *[block for sent in blocks[:early] for block in sent])
+    return pl.pallas_call(
+        z_last_kernel,
+        out_shape=jax.ShapeDtypeStruct((len(PRODUCT_PAIRS), 1, 128, width), jnp.float32),
+        in_specs=[whole()] * (2 + len(CHIPS)),
+        out_specs=whole(pl.ANY),
+        scratch_shapes=[
+            pltpu.VMEM((len(PRODUCT_PAIRS), 128, width), jnp.float32),
+            pltpu.SemaphoreType.DMA((TAIL_PARTS,)),
+        ],
+        compiler_params=params,
+        cost_estimate=cost("z_filter_last"),
+        name="z_filter_last",
+    )(passed, lines[-1], *blocks[-1])
 
 
 def extended(cells, sides, width):
@@ -89,10 +425,21 @@
 
 def solution(mesh):
     placed = (P(None, "col", ("grp", "row"), None), P("col"), P(), P())
-    return jax.shard_map(
-        body,
-        mesh=mesh,
-        in_specs=placed,
-        out_specs=P(None, "col", ("grp", "row"), None),
-        check_vma=False,
-    )
+
+    def run(velocity, profile, x_filters, z_filter):
+        shape = dict(mesh.shape)
+        plane = shape["grp"] * shape["row"]
+        suits = (
+            (shape["grp"], shape["row"], shape["col"]) == (4, 2, 4)
+            and velocity.shape == (3, shape["col"], 128 * plane, 1024)
+            and x_filters.shape[1:] == z_filter.shape == (1024, 1024)
+        )
+        return jax.shard_map(
+            fast_body if suits else body,
+            mesh=mesh,
+            in_specs=placed,
+            out_specs=P(None, "col", ("grp", "row"), None),
+            check_vma=False,
+        )(velocity, profile, x_filters, z_filter)
+
+    return run

time: 337 us -> 77.6 us (0.23)
  waiting for transfers between devices: 208 us -> 20.6 us
  blocking collectives: 52.5 us -> 0 us
  local copies, waits for them, and re-layouts: 32.8 us -> 4.78 us
  Pallas kernels: 0 us -> 15.7 us
  starting transfers between devices: 20.5 us -> 29.8 us
  matrix products: 8.22 us -> 0 us
  other arithmetic: 13.7 us -> 5.48 us
    ppermute x12 -> x24, waiting for transfers between devices: 208 us -> 20.6 us  [the longest x22 18.2 us: exchange(): return lax.ppermute(value, axis, [(i, i ^ flip) for i in range(count)])]
    all_to_all x1 -> x0, blocking collectives: 52.5 us -> none  [body(): lax.all_to_all(x_pass, ('grp', 'row'), split_axis=2, concat_axis=3, tiled...]
    pallas_call x0 -> x7, Pallas kernels: none -> 15.7 us  [the longest x3 5.25 us: fast_body(): pl.pallas_call(x_kernel, out_shape=[jax.ShapeDtypeStruct((FIELDS, cells,...]
    ppermute x12 -> x24, starting transfers between devices: 20.5 us -> 29.8 us  [the longest x22 27.8 us: exchange(): return lax.ppermute(value, axis, [(i, i ^ flip) for i in range(count)])]
    dot_general x2 -> x0, matrix products: 8.22 us -> none  [the longest x1 4.32 us: z_apply(): jnp.einsum('fyos,rs->fyor', received, z_filter, preferred_element_type=jn...]
    convert_element_type x1 -> x0, local copies, waits for them, and re-layouts: 6.69 us -> none  [body(): x_pass = jnp.einsum('yox,fyzx->fyoz', matrices, fields, preferred_element...]
    concatenate x3 -> x0, local copies, waits for them, and re-layouts: 6.08 us -> none  [extended(): jnp.concatenate([lax.ppermute(tail, axis, [(i, (i + 1) % count) for i in...]
    another operation x1 -> x0, local copies, waits for them, and re-layouts: 4.94 us -> none
  transfers between devices with their start and end apart: 12 -> 24, of which waited for: 12 -> 12; matrix products, arithmetic and copies ran while one was open for 1% -> 7% of each run, Pallas kernels for 0% -> 11%
where the time goes in v2:
time: 77.6 us; the launch traced here: 77.3 us
  starting transfers between devices  29.8 us (38%)
  waiting for transfers between devices  20.6 us (27%)
  Pallas kernels  15.7 us (20%)
  other arithmetic  5.48 us (7%)
  local copies, waits for them, and re-layouts  4.78 us (6%)
  between operations  0.86 us (1%)
    ppermute x22, starting transfers between devices, exchange(): return lax.ppermute(value, axis, [(i, i ^ flip) for i in range(count)])  27.8 us
    ppermute x22, waiting for transfers between devices, exchange(): return lax.ppermute(value, axis, [(i, i ^ flip) for i in range(count)])  18.2 us
    pallas_call x3, Pallas kernels, fast_body(): pl.pallas_call(x_kernel, out_shape=[jax.ShapeDtypeStruct((FIELDS, cells,...  5.25 us
    pallas_call x1, Pallas kernels, advance(): pl.pallas_call(functools.partial(step_kernel, slabs), out_shape=[jax.Shap...  4.71 us
    convert_element_type x2, other arithmetic, advance(): narrow = v.astype(WIRE)  3.1 us
    pallas_call x1, Pallas kernels, fast_body(): pl.pallas_call(z_last_kernel, out_shape=jax.ShapeDtypeStruct((len(PRODUCT...  2.31 us
    select_n x2, other arithmetic, advance(): halos.append(jnp.where(low, after, before))  2.3 us
    unnamed x6, local copies, waits for them, and re-layouts  2.29 us
  transfers between devices with their start and end apart: 24, of which 12 were waited for; matrix products, arithmetic and copies ran while one was open for 7% of the time, Pallas kernels for 11%

profile of v2, /device:TPU:0, one launch (start us, length us, event | category | flops | bytes accessed | tf_op | source)
XLA Modules:
  0.0 77.3 jit_solution(4108074449194162623)
XLA Ops:
  0.0 1.5 %bitcast_convert_fusion = bf16[3,1,128,1024]{3,2,0,1:T(8,128)(2,1)S(1)} fusion(f32[3,1,128,1024]{3,2,1,0:T(8,128)} %param.4), kind=kLoop, calls=%fused_computation | loop fusion | flops 393216 | bytes 2359296 | tf_op jit(solution)/shard_map/convert_element_type | solution.py:186
  1.5 0.0 copy-start.2
  1.6 0.8 %dynamic-slice_bitcast_fusion.1 = (bf16[3,32,1024]{2,1,0:T(8,128)(2,1)S(1)}, bf16[3,32,1024]{2,1,0:T(8,128)(2,1)S(1)}, bf16[3,32,1024]{2,1,0:T(8,128)(2,1)}) fusion(bf16[3,1,128,1024]{3,2,0,1:T(8,128)(2,1)S(1)} %bitcast_convert_fusion, s32[]{:T(128)S(6)} %select_n.100, s32[]{:T(128)S(6)} %select_n.99, s32[]{:T(128)S(6)} %select_n.98), kind=kLoop, calls=%fused_computation.2 | loop fusion | bytes 1179660 | tf_op jit(solution)/shard_map/dynamic_slice | solution.py:191
  2.4 0.1 copy-done.2
  2.5 5.0 %collective-permute-start.4 = (bf16[3,32,1024]{2,1,0:T(8,128)(2,1)S(1)}, bf16[3,32,1024]{2,1,0:T(8,128)(2,1)S(1)}, u32[]{:S(2)}, u32[]{:S(2)}) collective-permute-start(bf16[3,32,1024]{2,1,0:T(8,128)(2,1)S(1)} %get-tuple-element.90), channel_id=1, source_target_pairs={{0,3},{1,2},{2,1},{3,0},{4,7},{5,6},{6,5},{7,4},{8,11},{9,10},{10,... | collective-permute-start | bytes 589832 | tf_op jit(solution)/shard_map/ppermute | solution.py:35
  7.5 0.0 collective-permute-start.3
  7.5 0.6 collective-permute-start.2
  8.1 1.6 %fusion.5 = bf16[3,128,1024]{2,1,0:T(8,128)(2,1)S(1)} fusion(f32[3,1,128,1024]{3,2,1,0:T(8,128)} %param.4), kind=kLoop, calls=%fused_computation.20 | loop fusion | flops 393216 | bytes 2359296 | tf_op jit(solution)/shard_map/convert_element_type | solution.py:186
  9.7 0.6 fusion.4
  10.3 1.4 %collective-permute-start = (bf16[3,8,1024]{2,1,0:T(8,128)(2,1)}, bf16[3,8,1024]{2,1,0:T(8,128)(2,1)S(1)}, u32[]{:S(2)}, u32[]{:S(2)}) collective-permute-start(bf16[3,8,1024]{2,1,0:T(8,128)(2,1)} %get-tuple-element.93), channel_id=1, source_target_pairs={{4,0},{8,4},{12,8},{16,12},{20,16},{24,20},{28,24},{0,28},{5,1},{9... | collective-permute-start | bytes 147464 | tf_op jit(solution)/shard_map/ppermute | solution.py:188
  11.7 0.6 collective-permute-start.1
  12.4 1.0 %dynamic-slice_bitcast_fusion.refs_0_ = f32[3,32,1024]{2,1,0:T(8,128)S(1)} fusion(f32[3,1,128,1024]{3,2,1,0:T(8,128)} %param.4, s32[]{:T(128)S(6)} %select_n.91), kind=kLoop, calls=%fused_computation.1 | loop fusion | bytes 786436 | tf_op jit(solution)/shard_map/dynamic_slice | solution.py:189
  14.1 0.5 collective-permute-done
  14.6 1.9 %collective-permute-done.1 = bf16[3,8,1024]{2,1,0:T(8,128)(2,1)} collective-permute-done((bf16[3,8,1024]{2,1,0:T(8,128)(2,1)}, bf16[3,8,1024]{2,1,0:T(8,128)(2,1)}, u32[]{:S(2)}, u32[]{:S(2)}) %collective-permute-start.1) | collective-permute-done | bytes 49184 | tf_op jit(solution)/shard_map/ppermute | solution.py:187
  16.6 1.3 %fusion = (bf16[3,8,1024]{2,1,0:T(8,128)(2,1)S(1)}, bf16[3,8,1024]{2,1,0:T(8,128)(2,1)S(1)}, bf16[3,8,1024]{2,1,0:T(8,128)(2,1)S(1)}) fusion(bf16[3,8,1024]{2,1,0:T(8,128)(2,1)} %collective-permute-done.1, bf16[3,8,1024]{2,1,0:T(8,128)(2,1)S(1)} %collective-permute-done, bf16[3,1,128,1024]{3,2,0,1:T(8,128)(2,1)} %copy-done.2, s32[]{:T(128)S(6)} %max.15, ...), kind=kLoop, calls=%fused_computation.6 | loop fusion | flops 221184 | bytes 540710 | tf_op jit(solution)/shard_map/jit(_where)/select_n | solution.py:200
  17.9 3.5 %collective-permute-start.7 = (bf16[3,8,1024]{2,1,0:T(8,128)(2,1)S(1)}, bf16[3,8,1024]{2,1,0:T(8,128)(2,1)S(1)}, u32[]{:S(2)}, u32[]{:S(2)}) collective-permute-start(bf16[3,8,1024]{2,1,0:T(8,128)(2,1)S(1)} %get-tuple-element.87), channel_id=1, source_target_pairs={{0,3},{1,2},{2,1},{3,0},{4,7},{5,6},{6,5},{7,4},{8,11},{9,10},{10,... | collective-permute-start | bytes 147464 | tf_op jit(solution)/shard_map/ppermute | solution.py:35
  21.3 0.0 collective-permute-start.6
  21.3 1.0 %fusion.3 = bf16[3,8,1024]{2,1,0:T(8,128)(2,1)S(1)} fusion(bf16[3,8,1024]{2,1,0:T(8,128)(2,1)} %collective-permute-done.1, bf16[3,8,1024]{2,1,0:T(8,128)(2,1)S(1)} %collective-permute-done, bf16[3,1,128,1024]{3,2,0,1:T(8,128)(2,1)} %copy-done.2, s32[]{:T(128)S(6)} %max.12, s32[]{:T(128)S(6)} %select_n.93, pred[8]{0:T(512)(128)(4,1)S(1)} %iota_compare_fusion, ...), kind=kLoop, calls=%fused_computation.15 | loop fusion | flops 73728 | bytes 245778 | tf_op jit(solution)/shard_map/jit(_where)/select_n | solution.py:200
  22.3 0.0 collective-permute-done.2.refs_1_
  22.3 1.1 %collective-permute-start.5 = (bf16[3,8,1024]{2,1,0:T(8,128)(2,1)S(1)}, bf16[3,8,1024]{2,1,0:T(8,128)(2,1)S(1)}, u32[]{:S(2)}, u32[]{:S(2)}) collective-permute-start(bf16[3,8,1024]{2,1,0:T(8,128)(2,1)S(1)} %fusion.3), channel_id=1, source_target_pairs={{0,1},{1,0},{2,3},{3,2},{4,5},{5,4},{6,7},{7,6},{8,9},{9,8},{10,11... | collective-permute-start | bytes 147464 | tf_op jit(solution)/shard_map/ppermute | solution.py:35
  23.4 0.1 pad_add_fusion.place_ref
  23.5 2.2 %copy-done = bf16[2,1024,1024]{2,1,0:T(8,128)(2,1)S(1)} copy-done((bf16[2,1024,1024]{2,1,0:T(8,128)(2,1)S(1)}, bf16[2,1024,1024]{2,1,0:T(8,128)(2,1)}, u32[]{:S(2)}) %copy-start) | copy-done | bytes 4194328
  25.7 1.4 %prepare.1 = (bf16[512,1024]{1,0:T(8,128)(2,1)S(1)}, bf16[256,1024]{1,0:T(8,128)(2,1)S(1)}, bf16[512,1024]{1,0:T(8,128)(2,1)S(1)}, bf16[256,1024]{1,0:T(8,128)(2,1)S(1)}) custom-call(s32[3]{0:T(128)S(1)} %pad_add_fusion.place_ref, bf16[2,1024,1024]{2,1,0:T(8,128)(2,1)S(1)} %copy-done, bf16[1024,1024]{1,0:T(8,128)(2,1)S(1)} %copy-done.1), custom_call_target="tpu_custom_call" | custom-call | bytes 11100000 | tf_op jit(solution)/shard_map/prepare/pallas_call | solution.py:285
  27.1 0.0 collective-permute-done.7.refs_7_
  27.1 1.3 %collective-permute-done.6.refs_6_ = bf16[3,8,1024]{2,1,0:T(8,128)(2,1)S(1)} collective-permute-done((bf16[3,8,1024]{2,1,0:T(8,128)(2,1)S(1)}, bf16[3,8,1024]{2,1,0:T(8,128)(2,1)S(1)}, u32[]{:S(2)}, u32[]{:S(2)}) %collective-permute-start.6) | collective-permute-done | bytes 49184 | tf_op jit(solution)/shard_map/ppermute | solution.py:35
  28.4 0.0 collective-permute-done.4.refs_3_
  28.4 0.0 collective-permute-done.3.refs_2_
  28.4 0.0 collective-permute-done.5.refs_5_
  28.4 4.7 %advance.1 = (bf16[3,32,1024]{2,1,0:T(8,128)(2,1)S(1)}, bf16[3,32,1024]{2,1,0:T(8,128)(2,1)S(1)}, bf16[3,32,1024]{2,1,0:T(8,128)(2,1)S(1)}, bf16[3,32,1024]{2,1,0:T(8,128)(2,1)S(1)}) custom-call(s32[1]{0:T(128)} %bitcast.14.q_ref, f32[3,32,1024]{2,1,0:T(8,128)S(1)} %dynamic-slice_bitcast_fusion.refs_0_, ...), custom_call_target="tpu_custom_call" | custom-call | bytes 18500000 | tf_op jit(solution)/shard_map/advance/pallas_call | solution.py:207
  33.2 0.1 collective-permute-start.8
  33.2 1.1 %collective-permute-start.13 = (bf16[3,32,1024]{2,1,0:T(8,128)(2,1)S(1)}, bf16[3,32,1024]{2,1,0:T(8,128)(2,1)S(1)}, u32[]{:S(2)}, u32[]{:S(2)}) collective-permute-start(bf16[3,32,1024]{2,1,0:T(8,128)(2,1)S(1)} %get-tuple-element.70), channel_id=1, source_target_pairs={{0,2},{1,3},{2,0},{3,1},{4,6},{5,7},{6,4},{7,5},{8,10},{9,11},{10,... | collective-permute-start | bytes 589832 | tf_op jit(solution)/shard_map/ppermute | solution.py:35
  34.4 2.0 %collective-permute-start.12 = (bf16[3,32,1024]{2,1,0:T(8,128)(2,1)S(1)}, bf16[3,32,1024]{2,1,0:T(8,128)(2,1)S(1)}, u32[]{:S(2)}, u32[]{:S(2)}) collective-permute-start(bf16[3,32,1024]{2,1,0:T(8,128)(2,1)S(1)} %get-tuple-element.68), channel_id=1, source_target_pairs={{0,1},{1,0},{2,3},{3,2},{4,5},{5,4},{6,7},{7,6},{8,9},{9,8},{10,11... | collective-permute-start | bytes 589832 | tf_op jit(solution)/shard_map/ppermute | solution.py:35
  36.3 0.0 collective-permute-done.8.refs_1_
  36.3 1.5 %x_filter_0.1 = (bf16[9,64,128]{2,1,0:T(8,128)(2,1)S(1)}, bf16[9,64,128]{2,1,0:T(8,128)(2,1)S(1)}, bf16[9,64,128]{2,1,0:T(8,128)(2,1)S(1)}, bf16[9,64,128]{2,1,0:T(8,128)(2,1)S(1)}) custom-call(s32[3]{0:T(128)S(1)} %pad_add_fusion.place_ref, bf16[512,1024]{1,0:T(8,128)(2,1)S(1)} %get-tuple-element.54.matrix, ...), custom_call_target="tpu_custom_call" | custom-call | bytes 370000 | tf_op jit(solution)/shard_map/x_filter_0/pallas_call | solution.py:303
  37.8 1.6 %collective-permute-start.9 = (bf16[9,64,128]{2,1,0:T(8,128)(2,1)S(1)}, bf16[9,64,128]{2,1,0:T(8,128)(2,1)S(1)}, u32[]{:S(2)}, u32[]{:S(2)}) collective-permute-start(bf16[9,64,128]{2,1,0:T(8,128)(2,1)S(1)} %get-tuple-element.65), channel_id=1, source_target_pairs={{0,4},{4,0},{8,12},{12,8},{16,20},{20,16},{24,28},{28,24},{1,5},{5... | collective-permute-start | bytes 442376 | tf_op jit(solution)/shard_map/ppermute | solution.py:35
  39.4 1.5 %collective-permute-start.10 = (bf16[9,64,128]{2,1,0:T(8,128)(2,1)S(1)}, bf16[9,64,128]{2,1,0:T(8,128)(2,1)S(1)}, u32[]{:S(2)}, u32[]{:S(2)}) collective-permute-start(bf16[9,64,128]{2,1,0:T(8,128)(2,1)S(1)} %get-tuple-element.66), channel_id=1, source_target_pairs={{0,16},{4,20},{8,24},{12,28},{16,0},{20,4},{24,8},{28,12},{1,17},{... | collective-permute-start | bytes 442376 | tf_op jit(solution)/shard_map/ppermute | solution.py:35
  40.9 0.5 collective-permute-start.11
  41.4 4.2 %collective-permute-done.13.refs_1_ = bf16[3,32,1024]{2,1,0:T(8,128)(2,1)S(1)} collective-permute-done((bf16[3,32,1024]{2,1,0:T(8,128)(2,1)S(1)}, bf16[3,32,1024]{2,1,0:T(8,128)(2,1)S(1)}, u32[]{:S(2)}, u32[]{:S(2)}) %collective-permute-start.13) | collective-permute-done | bytes 196640 | tf_op jit(solution)/shard_map/ppermute | solution.py:35
  45.6 0.6 collective-permute-done.10.refs_4_
  46.2 1.7 %collective-permute-done.11.refs_5_ = bf16[9,64,128]{2,1,0:T(8,128)(2,1)S(1)} collective-permute-done((bf16[9,64,128]{2,1,0:T(8,128)(2,1)S(1)}, bf16[9,64,128]{2,1,0:T(8,128)(2,1)S(1)}, u32[]{:S(2)}, u32[]{:S(2)}) %collective-permute-start.11) | collective-permute-done | bytes 147488 | tf_op jit(solution)/shard_map/ppermute | solution.py:35
  47.9 0.0 collective-permute-done.12.refs_0_
  47.9 0.0 collective-permute-start.14
  47.9 0.5 collective-permute-start.15
  48.4 1.3 %collective-permute-start.18 = (bf16[3,32,1024]{2,1,0:T(8,128)(2,1)S(1)}, bf16[3,32,1024]{2,1,0:T(8,128)(2,1)S(1)}, u32[]{:S(2)}, u32[]{:S(2)}) collective-permute-start(bf16[3,32,1024]{2,1,0:T(8,128)(2,1)S(1)} %get-tuple-element.76), channel_id=1, source_target_pairs={{0,3},{1,2},{2,1},{3,0},{4,7},{5,6},{6,5},{7,4},{8,11},{9,10},{10,... | collective-permute-start | bytes 589832 | tf_op jit(solution)/shard_map/ppermute | solution.py:35
  49.7 0.0 collective-permute-done.14.refs_2_
  49.7 0.0 collective-permute-done.15.refs_3_
  49.7 2.3 %x_filter_1.1 = (bf16[9,128,128]{2,1,0:T(8,128)(2,1)S(1)}, bf16[9,128,128]{2,1,0:T(8,128)(2,1)S(1)}, bf16[9,128,128]{2,1,0:T(8,128)(2,1)S(1)}, bf16[9,128,128]{2,1,0:T(8,128)(2,1)S(1)}) custom-call(s32[3]{0:T(128)S(1)} %pad_add_fusion.place_ref, bf16[512,1024]{1,0:T(8,128)(2,1)S(1)} %get-tuple-element.54.matrix, ...), custom_call_target="tpu_custom_call" | custom-call | bytes 370000 | tf_op jit(solution)/shard_map/x_filter_1/pallas_call | solution.py:303
  52.0 1.6 %collective-permute-start.16 = (bf16[9,128,128]{2,1,0:T(8,128)(2,1)S(1)}, bf16[9,128,128]{2,1,0:T(8,128)(2,1)S(1)}, u32[]{:S(2)}, u32[]{:S(2)}) collective-permute-start(bf16[9,128,128]{2,1,0:T(8,128)(2,1)S(1)} %get-tuple-element.73), channel_id=1, source_target_pairs={{0,4},{4,0},{8,12},{12,8},{16,20},{20,16},{24,28},{28,24},{1,5},{5... | collective-permute-start | bytes 884744 | tf_op jit(solution)/shard_map/ppermute | solution.py:35
  53.6 1.5 %collective-permute-start.17 = (bf16[9,128,128]{2,1,0:T(8,128)(2,1)S(1)}, bf16[9,128,128]{2,1,0:T(8,128)(2,1)S(1)}, u32[]{:S(2)}, u32[]{:S(2)}) collective-permute-start(bf16[9,128,128]{2,1,0:T(8,128)(2,1)S(1)} %get-tuple-element.74), channel_id=1, source_target_pairs={{0,16},{4,20},{8,24},{12,28},{16,0},{20,4},{24,8},{28,12},{1,17},{... | collective-permute-start | bytes 884744 | tf_op jit(solution)/shard_map/ppermute | solution.py:35
  55.1 2.0 %collective-permute-done.18.refs_0_ = bf16[3,32,1024]{2,1,0:T(8,128)(2,1)S(1)} collective-permute-done((bf16[3,32,1024]{2,1,0:T(8,128)(2,1)S(1)}, bf16[3,32,1024]{2,1,0:T(8,128)(2,1)S(1)}, u32[]{:S(2)}, u32[]{:S(2)}) %collective-permute-start.18) | collective-permute-done | bytes 196640 | tf_op jit(solution)/shard_map/ppermute | solution.py:35
  57.1 2.4 %collective-permute-start.19 = (bf16[9,128,128]{2,1,0:T(8,128)(2,1)S(1)}, bf16[9,128,128]{2,1,0:T(8,128)(2,1)S(1)}, u32[]{:S(2)}, u32[]{:S(2)}) collective-permute-start(bf16[9,128,128]{2,1,0:T(8,128)(2,1)S(1)} %get-tuple-element.77), channel_id=1, source_target_pairs={{0,20},{4,16},{8,28},{12,24},{16,4},{20,0},{24,12},{28,8},{1,21},{... | collective-permute-start | bytes 884744 | tf_op jit(solution)/shard_map/ppermute | solution.py:35
  59.6 0.0 collective-permute-done.20.refs_1_
  59.6 1.5 %x_filter_2.1 = (bf16[9,64,128]{2,1,0:T(8,128)(2,1)S(1)}, bf16[9,64,128]{2,1,0:T(8,128)(2,1)S(1)}, bf16[9,64,128]{2,1,0:T(8,128)(2,1)S(1)}, bf16[9,64,128]{2,1,0:T(8,128)(2,1)S(1)}) custom-call(s32[3]{0:T(128)S(1)} %pad_add_fusion.place_ref, bf16[512,1024]{1,0:T(8,128)(2,1)S(1)} %get-tuple-element.54.matrix, ...), custom_call_target="tpu_custom_call" | custom-call | bytes 370000 | tf_op jit(solution)/shard_map/x_filter_2/pallas_call | solution.py:303
  61.1 0.0 collective-permute-done.16.refs_7_
  61.1 2.3 %collective-permute-done.17.refs_8_ = bf16[9,128,128]{2,1,0:T(8,128)(2,1)S(1)} collective-permute-done((bf16[9,128,128]{2,1,0:T(8,128)(2,1)S(1)}, bf16[9,128,128]{2,1,0:T(8,128)(2,1)S(1)}, u32[]{:S(2)}, u32[]{:S(2)}) %collective-permute-start.17) | collective-permute-done | bytes 294944 | tf_op jit(solution)/shard_map/ppermute | solution.py:35
  63.4 0.5 collective-permute-start.21
  63.9 1.5 %collective-permute-start.22 = (bf16[9,64,128]{2,1,0:T(8,128)(2,1)S(1)}, bf16[9,64,128]{2,1,0:T(8,128)(2,1)S(1)}, u32[]{:S(2)}, u32[]{:S(2)}) collective-permute-start(bf16[9,64,128]{2,1,0:T(8,128)(2,1)S(1)} %get-tuple-element.85), channel_id=1, source_target_pairs={{0,16},{4,20},{8,24},{12,28},{16,0},{20,4},{24,8},{28,12},{1,17},{... | collective-permute-start | bytes 442376 | tf_op jit(solution)/shard_map/ppermute | solution.py:35
  65.4 1.5 %collective-permute-start.23 = (bf16[9,64,128]{2,1,0:T(8,128)(2,1)S(1)}, bf16[9,64,128]{2,1,0:T(8,128)(2,1)S(1)}, u32[]{:S(2)}, u32[]{:S(2)}) collective-permute-start(bf16[9,64,128]{2,1,0:T(8,128)(2,1)S(1)} %get-tuple-element.86), channel_id=1, source_target_pairs={{0,20},{4,16},{8,28},{12,24},{16,4},{20,0},{24,12},{28,8},{1,21},{... | collective-permute-start | bytes 442376 | tf_op jit(solution)/shard_map/ppermute | solution.py:35
  66.9 2.8 %collective-permute-done.19.refs_9_ = bf16[9,128,128]{2,1,0:T(8,128)(2,1)S(1)} collective-permute-done((bf16[9,128,128]{2,1,0:T(8,128)(2,1)S(1)}, bf16[9,128,128]{2,1,0:T(8,128)(2,1)S(1)}, u32[]{:S(2)}, u32[]{:S(2)}) %collective-permute-start.19) | collective-permute-done | bytes 294944 | tf_op jit(solution)/shard_map/ppermute | solution.py:35
  69.7 2.0 %z_filter_first.1.passed = f32[9,128,1024]{2,1,0:T(8,128)S(1)} custom-call(bf16[256,1024]{1,0:T(8,128)(2,1)S(1)} %get-tuple-element.52.refs_0_, bf16[512,1024]{1,0:T(8,128)(2,1)S(1)} %get-tuple-element.53.refs_1_, bf16[9,64,128]{2,1,0:T(8,128)(2,1)S(1)} %get-tuple-element.64.refs_2_, bf16[9,64,128]{2,1,0:T(8,128)(2,1)S(1)} %collective-permute-done.9.refs_3_, ...), custom_call_target="tpu_custom_call" | custom-call | bytes 370000 | tf_op jit(solution)/shard_map/z_filter_first/pallas_call | solution.py:323
  71.8 1.0 %collective-permute-done.21.refs_1_ = bf16[9,64,128]{2,1,0:T(8,128)(2,1)S(1)} collective-permute-done((bf16[9,64,128]{2,1,0:T(8,128)(2,1)S(1)}, bf16[9,64,128]{2,1,0:T(8,128)(2,1)S(1)}, u32[]{:S(2)}, u32[]{:S(2)}) %collective-permute-start.21) | collective-permute-done | bytes 147488 | tf_op jit(solution)/shard_map/ppermute | solution.py:35
  72.8 0.1 collective-permute-done.22.refs_2_
  73.0 2.0 %collective-permute-done.23.refs_3_ = bf16[9,64,128]{2,1,0:T(8,128)(2,1)S(1)} collective-permute-done((bf16[9,64,128]{2,1,0:T(8,128)(2,1)S(1)}, bf16[9,64,128]{2,1,0:T(8,128)(2,1)S(1)}, u32[]{:S(2)}, u32[]{:S(2)}) %collective-permute-start.23) | collective-permute-done | bytes 147488 | tf_op jit(solution)/shard_map/ppermute | solution.py:35
  75.0 2.3 %z_filter_last.1 = f32[6,1,128,1024]{3,2,1,0:T(8,128)} custom-call(f32[9,128,1024]{2,1,0:T(8,128)S(1)} %z_filter_first.1.passed, bf16[256,1024]{1,0:T(8,128)(2,1)S(1)} %get-tuple-element.78.lines, bf16[9,64,128]{2,1,0:T(8,128)(2,1)S(1)} %get-tuple-element.83.refs_0_, bf16[9,64,128]{2,1,0:T(8,128)(2,1)S(1)} %collective-permute-done.21.refs_1_, ...), custom_call_target="tpu_custom_call" | custom-call | bytes 370000 | tf_op jit(solution)/shard_map/z_filter_last/pallas_call | solution.py:332
  (6 shorter events, 0.0 us)
Async XLA Ops:
  1.5 0.9 %copy-start.2 = (bf16[3,1,128,1024]{3,2,0,1:T(8,128)(2,1)}, bf16[3,1,128,1024]{3,2,0,1:T(8,128)(2,1)S(1)}, u32[]{:S(2)}) copy-start(bf16[3,1,128,1024]{3,2,0,1:T(8,128)(2,1)S(1)} %bitcast_convert_fusion) | copy-start | bytes 2359300
  2.5 26.0 %collective-permute-start.4 = (bf16[3,32,1024]{2,1,0:T(8,128)(2,1)S(1)}, bf16[3,32,1024]{2,1,0:T(8,128)(2,1)S(1)}, u32[]{:S(2)}, u32[]{:S(2)}) collective-permute-start(bf16[3,32,1024]{2,1,0:T(8,128)(2,1)S(1)} %get-tuple-element.90), channel_id=1, source_target_pairs={{0,3},{1,2},{2,1},{3,0},{4,7},{5,6},{6,5},{7,4},{8,11},{9,10},{10,... | collective-permute-start | bytes 589832 | tf_op jit(solution)/shard_map/ppermute | solution.py:35
  7.5 20.9 %collective-permute-start.3 = (bf16[3,32,1024]{2,1,0:T(8,128)(2,1)S(1)}, bf16[3,32,1024]{2,1,0:T(8,128)(2,1)S(1)}, u32[]{:S(2)}, u32[]{:S(2)}) collective-permute-start(bf16[3,32,1024]{2,1,0:T(8,128)(2,1)S(1)} %get-tuple-element.91), channel_id=1, source_target_pairs={{0,2},{1,3},{2,0},{3,1},{4,6},{5,7},{6,4},{7,5},{8,10},{9,11},{10,... | collective-permute-start | bytes 589832 | tf_op jit(solution)/shard_map/ppermute | solution.py:35
  7.5 16.0 %copy-start.1 = (bf16[1024,1024]{1,0:T(8,128)(2,1)S(1)}, bf16[1024,1024]{1,0:T(8,128)(2,1)}, u32[]{:S(2)}) copy-start(bf16[1024,1024]{1,0:T(8,128)(2,1)} %z_filter.1) | copy-start | bytes 6291460
  7.5 14.8 %collective-permute-start.2 = (bf16[3,32,1024]{2,1,0:T(8,128)(2,1)}, bf16[3,32,1024]{2,1,0:T(8,128)(2,1)S(1)}, u32[]{:S(2)}, u32[]{:S(2)}) collective-permute-start(bf16[3,32,1024]{2,1,0:T(8,128)(2,1)} %get-tuple-element.92), channel_id=1, source_target_pairs={{0,1},{1,0},{2,3},{3,2},{4,5},{5,4},{6,7},{7,6},{8,9},{9,8},{10,11... | collective-permute-start | bytes 589832 | tf_op jit(solution)/shard_map/ppermute | solution.py:35
  10.3 4.3 %collective-permute-start = (bf16[3,8,1024]{2,1,0:T(8,128)(2,1)}, bf16[3,8,1024]{2,1,0:T(8,128)(2,1)S(1)}, u32[]{:S(2)}, u32[]{:S(2)}) collective-permute-start(bf16[3,8,1024]{2,1,0:T(8,128)(2,1)} %get-tuple-element.93), channel_id=1, source_target_pairs={{4,0},{8,4},{12,8},{16,12},{20,16},{24,20},{28,24},{0,28},{5,1},{9... | collective-permute-start | bytes 147464 | tf_op jit(solution)/shard_map/ppermute | solution.py:188
  11.7 4.8 %collective-permute-start.1 = (bf16[3,8,1024]{2,1,0:T(8,128)(2,1)}, bf16[3,8,1024]{2,1,0:T(8,128)(2,1)}, u32[]{:S(2)}, u32[]{:S(2)}) collective-permute-start(bf16[3,8,1024]{2,1,0:T(8,128)(2,1)} %get-tuple-element.94), channel_id=1, source_target_pairs={{0,4},{4,8},{8,12},{12,16},{16,20},{20,24},{24,28},{28,0},{1,5},{5... | collective-permute-start | bytes 147464 | tf_op jit(solution)/shard_map/ppermute | solution.py:187
  17.9 9.3 %collective-permute-start.7 = (bf16[3,8,1024]{2,1,0:T(8,128)(2,1)S(1)}, bf16[3,8,1024]{2,1,0:T(8,128)(2,1)S(1)}, u32[]{:S(2)}, u32[]{:S(2)}) collective-permute-start(bf16[3,8,1024]{2,1,0:T(8,128)(2,1)S(1)} %get-tuple-element.87), channel_id=1, source_target_pairs={{0,3},{1,2},{2,1},{3,0},{4,7},{5,6},{6,5},{7,4},{8,11},{9,10},{10,... | collective-permute-start | bytes 147464 | tf_op jit(solution)/shard_map/ppermute | solution.py:35
  21.3 7.1 %collective-permute-start.6 = (bf16[3,8,1024]{2,1,0:T(8,128)(2,1)S(1)}, bf16[3,8,1024]{2,1,0:T(8,128)(2,1)S(1)}, u32[]{:S(2)}, u32[]{:S(2)}) collective-permute-start(bf16[3,8,1024]{2,1,0:T(8,128)(2,1)S(1)} %get-tuple-element.88), channel_id=1, source_target_pairs={{0,2},{1,3},{2,0},{3,1},{4,6},{5,7},{6,4},{7,5},{8,10},{9,11},{10,... | collective-permute-start | bytes 147464 | tf_op jit(solution)/shard_map/ppermute | solution.py:35
  22.3 6.1 %collective-permute-start.5 = (bf16[3,8,1024]{2,1,0:T(8,128)(2,1)S(1)}, bf16[3,8,1024]{2,1,0:T(8,128)(2,1)S(1)}, u32[]{:S(2)}, u32[]{:S(2)}) collective-permute-start(bf16[3,8,1024]{2,1,0:T(8,128)(2,1)S(1)} %fusion.3), channel_id=1, source_target_pairs={{0,1},{1,0},{2,3},{3,2},{4,5},{5,4},{6,7},{7,6},{8,9},{9,8},{10,11... | collective-permute-start | bytes 147464 | tf_op jit(solution)/shard_map/ppermute | solution.py:35
  23.5 2.2 %copy-start = (bf16[2,1024,1024]{2,1,0:T(8,128)(2,1)S(1)}, bf16[2,1024,1024]{2,1,0:T(8,128)(2,1)}, u32[]{:S(2)}) copy-start(bf16[2,1024,1024]{2,1,0:T(8,128)(2,1)} %x_filters.1) | copy-start | bytes 12582916
  33.2 3.2 %collective-permute-start.8 = (bf16[3,32,1024]{2,1,0:T(8,128)(2,1)S(1)}, bf16[3,32,1024]{2,1,0:T(8,128)(2,1)S(1)}, u32[]{:S(2)}, u32[]{:S(2)}) collective-permute-start(bf16[3,32,1024]{2,1,0:T(8,128)(2,1)S(1)} %get-tuple-element.63.refs_0_), channel_id=1, source_target_pairs={{0,8},{8,0},{16,24},{24,16},{1,9},{9,1},{17,25},{25,17},{2,10},{10... | collective-permute-start | bytes 589832 | tf_op jit(solution)/shard_map/ppermute | solution.py:35
  33.2 12.4 %collective-permute-start.13 = (bf16[3,32,1024]{2,1,0:T(8,128)(2,1)S(1)}, bf16[3,32,1024]{2,1,0:T(8,128)(2,1)S(1)}, u32[]{:S(2)}, u32[]{:S(2)}) collective-permute-start(bf16[3,32,1024]{2,1,0:T(8,128)(2,1)S(1)} %get-tuple-element.70), channel_id=1, source_target_pairs={{0,2},{1,3},{2,0},{3,1},{4,6},{5,7},{6,4},{7,5},{8,10},{9,11},{10,... | collective-permute-start | bytes 589832 | tf_op jit(solution)/shard_map/ppermute | solution.py:35
  34.4 13.5 %collective-permute-start.12 = (bf16[3,32,1024]{2,1,0:T(8,128)(2,1)S(1)}, bf16[3,32,1024]{2,1,0:T(8,128)(2,1)S(1)}, u32[]{:S(2)}, u32[]{:S(2)}) collective-permute-start(bf16[3,32,1024]{2,1,0:T(8,128)(2,1)S(1)} %get-tuple-element.68), channel_id=1, source_target_pairs={{0,1},{1,0},{2,3},{3,2},{4,5},{5,4},{6,7},{7,6},{8,9},{9,8},{10,11... | collective-permute-start | bytes 589832 | tf_op jit(solution)/shard_map/ppermute | solution.py:35
  37.8 7.8 %collective-permute-start.9 = (bf16[9,64,128]{2,1,0:T(8,128)(2,1)S(1)}, bf16[9,64,128]{2,1,0:T(8,128)(2,1)S(1)}, u32[]{:S(2)}, u32[]{:S(2)}) collective-permute-start(bf16[9,64,128]{2,1,0:T(8,128)(2,1)S(1)} %get-tuple-element.65), channel_id=1, source_target_pairs={{0,4},{4,0},{8,12},{12,8},{16,20},{20,16},{24,28},{28,24},{1,5},{5... | collective-permute-start | bytes 442376 | tf_op jit(solution)/shard_map/ppermute | solution.py:35
  39.4 6.8 %collective-permute-start.10 = (bf16[9,64,128]{2,1,0:T(8,128)(2,1)S(1)}, bf16[9,64,128]{2,1,0:T(8,128)(2,1)S(1)}, u32[]{:S(2)}, u32[]{:S(2)}) collective-permute-start(bf16[9,64,128]{2,1,0:T(8,128)(2,1)S(1)} %get-tuple-element.66), channel_id=1, source_target_pairs={{0,16},{4,20},{8,24},{12,28},{16,0},{20,4},{24,8},{28,12},{1,17},{... | collective-permute-start | bytes 442376 | tf_op jit(solution)/shard_map/ppermute | solution.py:35
  40.9 7.0 %collective-permute-start.11 = (bf16[9,64,128]{2,1,0:T(8,128)(2,1)S(1)}, bf16[9,64,128]{2,1,0:T(8,128)(2,1)S(1)}, u32[]{:S(2)}, u32[]{:S(2)}) collective-permute-start(bf16[9,64,128]{2,1,0:T(8,128)(2,1)S(1)} %get-tuple-element.67), channel_id=1, source_target_pairs={{0,20},{4,16},{8,28},{12,24},{16,4},{20,0},{24,12},{28,8},{1,21},{... | collective-permute-start | bytes 442376 | tf_op jit(solution)/shard_map/ppermute | solution.py:35
  47.9 1.9 %collective-permute-start.14 = (bf16[3,32,1024]{2,1,0:T(8,128)(2,1)S(1)}, bf16[3,32,1024]{2,1,0:T(8,128)(2,1)S(1)}, u32[]{:S(2)}, u32[]{:S(2)}) collective-permute-start(bf16[3,32,1024]{2,1,0:T(8,128)(2,1)S(1)} %collective-permute-done.12.refs_0_), channel_id=1, source_target_pairs={{0,8},{8,0},{16,24},{24,16},{1,9},{9,1},{17,25},{25,17},{2,10},{10... | collective-permute-start | bytes 589832 | tf_op jit(solution)/shard_map/ppermute | solution.py:35
  47.9 1.9 %collective-permute-start.15 = (bf16[3,32,1024]{2,1,0:T(8,128)(2,1)S(1)}, bf16[3,32,1024]{2,1,0:T(8,128)(2,1)S(1)}, u32[]{:S(2)}, u32[]{:S(2)}) collective-permute-start(bf16[3,32,1024]{2,1,0:T(8,128)(2,1)S(1)} %collective-permute-done.13.refs_1_), channel_id=1, source_target_pairs={{0,8},{8,0},{16,24},{24,16},{1,9},{9,1},{17,25},{25,17},{2,10},{10... | collective-permute-start | bytes 589832 | tf_op jit(solution)/shard_map/ppermute | solution.py:35
  48.4 8.7 %collective-permute-start.18 = (bf16[3,32,1024]{2,1,0:T(8,128)(2,1)S(1)}, bf16[3,32,1024]{2,1,0:T(8,128)(2,1)S(1)}, u32[]{:S(2)}, u32[]{:S(2)}) collective-permute-start(bf16[3,32,1024]{2,1,0:T(8,128)(2,1)S(1)} %get-tuple-element.76), channel_id=1, source_target_pairs={{0,3},{1,2},{2,1},{3,0},{4,7},{5,6},{6,5},{7,4},{8,11},{9,10},{10,... | collective-permute-start | bytes 589832 | tf_op jit(solution)/shard_map/ppermute | solution.py:35
  52.0 9.1 %collective-permute-start.16 = (bf16[9,128,128]{2,1,0:T(8,128)(2,1)S(1)}, bf16[9,128,128]{2,1,0:T(8,128)(2,1)S(1)}, u32[]{:S(2)}, u32[]{:S(2)}) collective-permute-start(bf16[9,128,128]{2,1,0:T(8,128)(2,1)S(1)} %get-tuple-element.73), channel_id=1, source_target_pairs={{0,4},{4,0},{8,12},{12,8},{16,20},{20,16},{24,28},{28,24},{1,5},{5... | collective-permute-start | bytes 884744 | tf_op jit(solution)/shard_map/ppermute | solution.py:35
  53.6 9.8 %collective-permute-start.17 = (bf16[9,128,128]{2,1,0:T(8,128)(2,1)S(1)}, bf16[9,128,128]{2,1,0:T(8,128)(2,1)S(1)}, u32[]{:S(2)}, u32[]{:S(2)}) collective-permute-start(bf16[9,128,128]{2,1,0:T(8,128)(2,1)S(1)} %get-tuple-element.74), channel_id=1, source_target_pairs={{0,16},{4,20},{8,24},{12,28},{16,0},{20,4},{24,8},{28,12},{1,17},{... | collective-permute-start | bytes 884744 | tf_op jit(solution)/shard_map/ppermute | solution.py:35
  57.1 2.5 %collective-permute-start.20 = (bf16[3,32,1024]{2,1,0:T(8,128)(2,1)S(1)}, bf16[3,32,1024]{2,1,0:T(8,128)(2,1)S(1)}, u32[]{:S(2)}, u32[]{:S(2)}) collective-permute-start(bf16[3,32,1024]{2,1,0:T(8,128)(2,1)S(1)} %collective-permute-done.18.refs_0_), channel_id=1, source_target_pairs={{0,8},{8,0},{16,24},{24,16},{1,9},{9,1},{17,25},{25,17},{2,10},{10... | collective-permute-start | bytes 589832 | tf_op jit(solution)/shard_map/ppermute | solution.py:35
  57.1 12.6 %collective-permute-start.19 = (bf16[9,128,128]{2,1,0:T(8,128)(2,1)S(1)}, bf16[9,128,128]{2,1,0:T(8,128)(2,1)S(1)}, u32[]{:S(2)}, u32[]{:S(2)}) collective-permute-start(bf16[9,128,128]{2,1,0:T(8,128)(2,1)S(1)} %get-tuple-element.77), channel_id=1, source_target_pairs={{0,20},{4,16},{8,28},{12,24},{16,4},{20,0},{24,12},{28,8},{1,21},{... | collective-permute-start | bytes 884744 | tf_op jit(solution)/shard_map/ppermute | solution.py:35
  63.4 9.4 %collective-permute-start.21 = (bf16[9,64,128]{2,1,0:T(8,128)(2,1)S(1)}, bf16[9,64,128]{2,1,0:T(8,128)(2,1)S(1)}, u32[]{:S(2)}, u32[]{:S(2)}) collective-permute-start(bf16[9,64,128]{2,1,0:T(8,128)(2,1)S(1)} %get-tuple-element.84), channel_id=1, source_target_pairs={{0,4},{4,0},{8,12},{12,8},{16,20},{20,16},{24,28},{28,24},{1,5},{5... | collective-permute-start | bytes 442376 | tf_op jit(solution)/shard_map/ppermute | solution.py:35
  63.9 9.0 %collective-permute-start.22 = (bf16[9,64,128]{2,1,0:T(8,128)(2,1)S(1)}, bf16[9,64,128]{2,1,0:T(8,128)(2,1)S(1)}, u32[]{:S(2)}, u32[]{:S(2)}) collective-permute-start(bf16[9,64,128]{2,1,0:T(8,128)(2,1)S(1)} %get-tuple-element.85), channel_id=1, source_target_pairs={{0,16},{4,20},{8,24},{12,28},{16,0},{20,4},{24,8},{28,12},{1,17},{... | collective-permute-start | bytes 442376 | tf_op jit(solution)/shard_map/ppermute | solution.py:35
  65.4 9.5 %collective-permute-start.23 = (bf16[9,64,128]{2,1,0:T(8,128)(2,1)S(1)}, bf16[9,64,128]{2,1,0:T(8,128)(2,1)S(1)}, u32[]{:S(2)}, u32[]{:S(2)}) collective-permute-start(bf16[9,64,128]{2,1,0:T(8,128)(2,1)S(1)} %get-tuple-element.86), channel_id=1, source_target_pairs={{0,20},{4,16},{8,28},{12,24},{16,4},{20,0},{24,12},{28,8},{1,21},{... | collective-permute-start | bytes 442376 | tf_op jit(solution)/shard_map/ppermute | solution.py:35

commit v3 on v2

--- a/solution.py
+++ b/solution.py
@@ -47,35 +47,32 @@
     lines_out, (sem,) = refs[: len(CHUNKS)], refs[len(CHUNKS) :]
     q, me, prof = place_ref[0], place_ref[1], place_ref[2]
     copies = []
+    for core in range(2):
+        for slot, flip in enumerate(CHIPS):
+            at = pl.multiple_of((me ^ flip ^ (2 * core)) * 128, 128)
+            to = (core * len(CHIPS) + slot) * 128
+            copies.append(
+                pltpu.make_async_copy(
+                    x_filters.at[prof, pl.ds(at, 128)], rows_out.at[pl.ds(to, 128)], sem.at[core * len(CHIPS) + slot]
+                )
+            )
+            copies[-1].start()
+    rows = 128 // slabs
+    target = lax.broadcasted_iota(jnp.int32, (128, 128), 0)
+    source = lax.broadcasted_iota(jnp.int32, (128, 128), 1)
+    pick = (source == rows * (q ^ (target // rows)) + target % rows).astype(jnp.bfloat16)
     for slot, flip in enumerate(CHIPS):
-        at = pl.multiple_of((me ^ flip) * 128, 128)
-        copies.append(
-            pltpu.make_async_copy(
-                x_filters.at[prof, pl.ds(at, 128)], rows_out.at[pl.ds(slot * 128, 128)], sem.at[slot]
-            )
-        )
-        copies[-1].start()
-    rows = 128 // slabs
-    picks = []
-    for flips in CHUNKS:
-        per_core = rows * len(flips)
-        target = lax.broadcasted_iota(jnp.int32, (2 * per_core, 256), 0)
-        source = lax.broadcasted_iota(jnp.int32, (2 * per_core, 256), 1)
-        core, inner = target // per_core, target % per_core
-        wanted = core * 128 + rows * (q ^ (flips[0] + inner // rows)) + inner % rows
-        picks.append((source == wanted).astype(jnp.bfloat16))
-    pick = jnp.concatenate(picks, axis=0)
-    for slot, flip in enumerate(CHIPS):
-        low = (me ^ flip) & ~2
-        pair = jnp.concatenate(
-            [z_filter[:, pl.ds(pl.multiple_of(128 * (low + 2 * core), 128), 128)] for core in range(2)], axis=1
-        )
-        picked = lax.dot_general(pick, pair, NT, preferred_element_type=jnp.float32).astype(jnp.bfloat16)
-        at = 0
-        for number, flips in enumerate(CHUNKS):
-            cells = 2 * rows * len(flips)
-            lines_out[number][slot * cells : (slot + 1) * cells] = picked[at : at + cells]
-            at += cells
+        for core in range(2):
+            lanes = pl.ds(pl.multiple_of(128 * (me ^ flip ^ (2 * core)), 128), 128)
+            picked = lax.dot_general(pick, z_filter[:, lanes], NT, preferred_element_type=jnp.float32)
+            for number, flips in enumerate(CHUNKS):
+                cells = rows * len(flips)
+                part = picked[rows * flips[0] : rows * flips[0] + cells].astype(jnp.bfloat16)
+                if number < len(CHUNKS) - 1:
+                    at = (core * len(CHIPS) + slot) * cells
+                else:
+                    at = (slot * 2 + core) * cells
+                lines_out[number][at : at + cells] = part
     for copy in copies:
         copy.wait()
 
@@ -183,18 +180,17 @@
     v = velocity[:, 0]
     block, width = v.shape[1:]
     rows = block // slabs
-    narrow = v.astype(WIRE)
-    tail = lax.ppermute(narrow[:, block - HALO :], PLANE, [(j, (j + 1) % plane) for j in range(plane)])
-    head = lax.ppermute(narrow[:, :HALO], PLANE, [((j + 1) % plane, j) for j in range(plane)])
+    tail = lax.ppermute(v[:, block - HALO :].astype(WIRE), PLANE, [(j, (j + 1) % plane) for j in range(plane)])
+    head = lax.ppermute(v[:, :HALO].astype(WIRE), PLANE, [((j + 1) % plane, j) for j in range(plane)])
     mains = [lax.dynamic_slice_in_dim(v, rows * q, rows, 1)]
     for flip in range(1, slabs):
-        mains.append(exchange(lax.dynamic_slice_in_dim(narrow, rows * (q ^ flip), rows, 1), "col", flip))
+        mains.append(exchange(lax.dynamic_slice_in_dim(v, rows * (q ^ flip), rows, 1).astype(WIRE), "col", flip))
     low = lax.broadcasted_iota(jnp.int32, (3, HALO, width), 1) < HALO // 2
     halos = []
     for flip in range(slabs):
         at = rows * (q ^ flip)
-        before = lax.dynamic_slice_in_dim(narrow, jnp.maximum(at - HALO, 0), HALO, 1)
-        after = lax.dynamic_slice_in_dim(narrow, jnp.minimum(at + rows, block - HALO), HALO, 1)
+        before = lax.dynamic_slice_in_dim(v, jnp.maximum(at - HALO, 0), HALO, 1).astype(WIRE)
+        after = lax.dynamic_slice_in_dim(v, jnp.minimum(at + rows, block - HALO), HALO, 1).astype(WIRE)
         before = jnp.where(at == 0, tail, before)
         after = jnp.where(at == block - rows, head, after)
         halos.append(jnp.where(low, after, before))
@@ -221,50 +217,58 @@
     return pieces, filters
 
 
-def x_kernel(place_ref, matrix, *refs):
+def x_kernel(cores, matrix, *refs):
     inputs, outs, (fields,) = refs[: -len(CHIPS) - 1], refs[-len(CHIPS) - 1 : -1], refs[-1:]
-    core = (place_ref[1] // 2) % 2
-    half = len(inputs) // 2
-    for other in range(2):
-        for piece in range(half):
-            ref = inputs[other * half + piece]
-            rows = ref.shape[1]
-            at = pl.multiple_of(rows * (half * (core ^ other) + piece), rows)
-            for comp in range(3):
-                fields[comp, pl.ds(at, rows)] = ref[comp]
-            for number, (a, b) in enumerate(PRODUCT_PAIRS):
-                product = ref[a].astype(jnp.float32) * ref[b].astype(jnp.float32)
-                fields[3 + number, pl.ds(at, rows)] = product.astype(jnp.bfloat16)
     cells = fields.shape[1]
+    rows = cells // len(inputs)
+    for piece, ref in enumerate(inputs):
+        at = slice(rows * piece, rows * piece + rows)
+        for comp in range(3):
+            fields[comp, at] = ref[comp]
+        for number, (a, b) in enumerate(PRODUCT_PAIRS):
+            product = ref[a].astype(jnp.float32) * ref[b].astype(jnp.float32)
+            fields[3 + number, at] = product.astype(jnp.bfloat16)
     group = fields[...].reshape(FIELDS * cells, fields.shape[2])
-    result = lax.dot_general(group, matrix[...], NT, preferred_element_type=jnp.float32)
+    result = lax.dot_general(
+        group, matrix[: cores * len(CHIPS) * 128], NT, preferred_element_type=jnp.float32
+    ).astype(jnp.bfloat16)
     for number in range(FIELDS):
-        for slot in range(len(CHIPS)):
-            part = result[number * cells : (number + 1) * cells, slot * 128 : (slot + 1) * 128]
-            outs[slot][number] = part.astype(jnp.bfloat16)
+        for core in range(cores):
+            for slot in range(len(CHIPS)):
+                at = (core * len(CHIPS) + slot) * 128
+                outs[slot][core, number] = result[number * cells : (number + 1) * cells, at : at + 128]
+
+
+def side_by_side(block):
+    return jnp.concatenate([block[number] for number in range(FIELDS)], axis=1)
 
 
 def z_sum(lines, blocks, columns):
-    left = jnp.concatenate(
-        [jnp.concatenate([block[number] for number in range(FIELDS)], axis=1) for block in blocks], axis=0
-    )
+    left = jnp.concatenate(blocks, axis=0)
     right = jnp.concatenate([line[:, columns] for line in lines], axis=0)
     return lax.dot_general(left, right, TN, preferred_element_type=jnp.float32)
 
 
 def z_first_kernel(*refs):
-    count = (len(refs) - 1) // (1 + len(CHIPS))
-    lines, blocks, passed = refs[:count], refs[count:-1], refs[-1]
-    passed[...] = z_sum(lines, blocks, slice(None)).reshape(passed.shape)
-
-
-def z_last_kernel(passed, lines, *refs):
-    blocks, (stress, made, sem) = refs[: len(CHIPS)], refs[len(CHIPS) :]
+    lines, first, others, second, passed = refs[:2], refs[2:6], refs[6], refs[7:11], refs[11]
+    blocks = [side_by_side(ref[0]) for ref in first]
+    blocks += [side_by_side(others[slot]) for slot in range(len(CHIPS))]
+    blocks += [side_by_side(ref[0]) for ref in second]
+    half = lines[1].shape[0] // 2
+    passed[...] = z_sum([lines[0], lines[1].at[:half]], blocks, slice(None)).reshape(passed.shape)
+
+
+def z_last_kernel(passed, line_second, line_last, others, *refs):
+    blocks = [side_by_side(others[slot]) for slot in range(len(CHIPS))]
+    blocks += [side_by_side(ref[0]) for ref in refs[: len(CHIPS)]]
+    half = line_second.shape[0] // 2
+    lines = [line_second.at[half:], line_last]
+    stress, made, sem = refs[len(CHIPS) :]
     copies = []
     width = passed.shape[2] // TAIL_PARTS
     for part in range(TAIL_PARTS):
         columns = slice(part * width, (part + 1) * width)
-        result = z_sum([lines], blocks, columns)
+        result = z_sum(lines, blocks, columns)
         total = [passed[at, :, columns] + result[at * 128 : (at + 1) * 128] for at in range(FIELDS)]
         for at, (a, b) in enumerate(PRODUCT_PAIRS):
             made[at, :, columns] = total[3 + at] - total[a] * total[b]
@@ -281,58 +285,66 @@
     me = lax.axis_index(PLANE).astype(jnp.int32)
     place = jnp.stack([q, me, profile[0]])
     params = pltpu.CompilerParams(vmem_limit_bytes=VMEM_BYTES)
-    sizes = [2 * len(flips) * 128 // slabs for flips in CHUNKS]
+    sizes = [len(flips) * 128 // slabs for flips in CHUNKS]
     matrix, *lines = pl.pallas_call(
         functools.partial(prepare_kernel, slabs),
-        out_shape=[jax.ShapeDtypeStruct((128 * len(CHIPS), width), jnp.bfloat16)]
-        + [jax.ShapeDtypeStruct((len(CHIPS) * cells, z_filter.shape[0]), jnp.bfloat16) for cells in sizes],
+        out_shape=[jax.ShapeDtypeStruct((256 * len(CHIPS), width), jnp.bfloat16)]
+        + [jax.ShapeDtypeStruct((2 * len(CHIPS) * cells, z_filter.shape[0]), jnp.bfloat16) for cells in sizes],
         in_specs=[whole(pltpu.SMEM), whole(pl.ANY), whole()],
         out_specs=[whole()] * (1 + len(CHUNKS)),
-        scratch_shapes=[pltpu.SemaphoreType.DMA((len(CHIPS),))],
+        scratch_shapes=[pltpu.SemaphoreType.DMA((2 * len(CHIPS),))],
         compiler_params=params,
         cost_estimate=cost("prepare"),
         name="prepare",
     )(place, x_filters, z_filter)
 
     pieces, (matrix, *lines) = advance(velocity, (matrix, *lines))
+
+    def x_filter(number, cores, inputs):
+        cells = sum(piece.shape[1] for piece in inputs)
+        return list(
+            pl.pallas_call(
+                functools.partial(x_kernel, cores),
+                out_shape=[jax.ShapeDtypeStruct((cores, FIELDS, cells, 128), jnp.bfloat16)] * len(CHIPS),
+                in_specs=[whole()] * (1 + len(inputs)),
+                out_specs=[whole()] * len(CHIPS),
+                scratch_shapes=[pltpu.VMEM((FIELDS, cells, width), jnp.bfloat16)],
+                compiler_params=params,
+                cost_estimate=cost(f"x_filter_{number}"),
+                name=f"x_filter_{number}",
+            )(matrix, *inputs)
+        )
+
+    def to_chips(made):
+        return [made[0]] + [exchange(made[slot], PLANE, CHIPS[slot]) for slot in range(1, len(CHIPS))]
+
     blocks = []
-    for number, flips in enumerate(CHUNKS):
-        mine = [pieces[flip] for flip in flips]
-        theirs = [exchange(piece, "grp", 1) for piece in mine]
-        cells = sizes[number]
-        made = pl.pallas_call(
-            x_kernel,
-            out_shape=[jax.ShapeDtypeStruct((FIELDS, cells, 128), jnp.bfloat16)] * len(CHIPS),
-            in_specs=[whole(pltpu.SMEM)] + [whole()] * (1 + 2 * len(flips)),
-            out_specs=[whole()] * len(CHIPS),
-            scratch_shapes=[pltpu.VMEM((FIELDS, cells, width), jnp.bfloat16)],
-            compiler_params=params,
-            cost_estimate=cost(f"x_filter_{number}"),
-            name=f"x_filter_{number}",
-        )(place, matrix, *mine, *theirs)
-        made = list(made)
-        if number == len(CHUNKS) - 1:
-            made = delayed(made, *blocks[-1][1:WAITED])
-        if number == 1:
-            made[3] = delayed(made[3], pieces[3])
-        blocks.append([made[0]] + [exchange(made[slot], PLANE, CHIPS[slot]) for slot in range(1, len(CHIPS))])
-        if number == 0:
-            for flip in CHUNKS[1]:
-                pieces[flip] = delayed(pieces[flip], *blocks[0][1:])
-    early = len(CHUNKS) - 1
+    for number, flips in enumerate(CHUNKS[:-1]):
+        made = x_filter(number, 2, [pieces[flip] for flip in flips])
+        if blocks:
+            made = delayed(made, *blocks[-1][1 : len(CHIPS)])
+        sent = to_chips(made)
+        blocks.append(sent)
+    mine = [pieces[flip] for flip in CHUNKS[-1]]
+    made = x_filter(len(CHUNKS) - 1, 1, mine + [exchange(piece, "grp", 1) for piece in mine])
+    made[3] = delayed(made[3], blocks[-1][1])
+    last = to_chips(made)
+    first, second = blocks
+    first_others = exchange(jnp.stack([block[1] for block in first]), "grp", 1)
     passed = pl.pallas_call(
         z_first_kernel,
         out_shape=jax.ShapeDtypeStruct((FIELDS, 128, width), jnp.float32),
-        in_specs=[whole()] * (early * (1 + len(CHIPS))),
+        in_specs=[whole()] * (3 + 2 * len(CHIPS)),
         out_specs=whole(),
         compiler_params=params,
         cost_estimate=cost("z_filter_first"),
         name="z_filter_first",
-    )(*lines[:early], *[block for sent in blocks[:early] for block in sent])
+    )(*lines[:2], *first, first_others, *second)
+    second_others = exchange(delayed(jnp.stack([block[1] for block in second]), passed, *last[1:]), "grp", 1)
     return pl.pallas_call(
         z_last_kernel,
         out_shape=jax.ShapeDtypeStruct((len(PRODUCT_PAIRS), 1, 128, width), jnp.float32),
-        in_specs=[whole()] * (2 + len(CHIPS)),
+        in_specs=[whole()] * (4 + len(CHIPS)),
         out_specs=whole(pl.ANY),
         scratch_shapes=[
             pltpu.VMEM((len(PRODUCT_PAIRS), 128, width), jnp.float32),
@@ -341,7 +353,7 @@
         compiler_params=params,
         cost_estimate=cost("z_filter_last"),
         name="z_filter_last",
-    )(passed, lines[-1], *blocks[-1])
+    )(passed, lines[1], lines[2], second_others, *last)
 
 
 def extended(cells, sides, width):

time: 77.6 us -> 72.8 us (0.938)
  waiting for transfers between devices: 20.6 us -> 16.8 us
  Pallas kernels: 15.7 us -> 13.4 us
  starting transfers between devices: 29.8 us -> 31.3 us
  other arithmetic: 5.48 us -> 4.32 us
  local copies, waits for them, and re-layouts: 4.78 us -> 5.92 us
    ppermute x22 -> x21, waiting for transfers between devices: 18.2 us -> 15.1 us  [exchange(): return lax.ppermute(value, axis, [(i, i ^ flip) for i in range(count)])]
    convert_element_type x2 -> x0, other arithmetic: 3.1 us -> none  [advance(): narrow = v.astype(WIRE)]
    pallas_call x3, Pallas kernels: 5.25 us -> 3.05 us  [x_filter(): pl.pallas_call(functools.partial(x_kernel, cores), out_shape=[jax.ShapeDt...]
    convert_element_type x0 -> x1, local copies, waits for them, and re-layouts: none -> 2 us  [advance(): lax.dynamic_slice_in_dim(v, rows * (q ^ flip), rows, 1).astype(WIRE)]
    another operation x0 -> x3, other arithmetic: none -> 1.7 us  [the longest x1 1.58 us: run(): jax.shard_map(fast_body if suits else body, mesh=mesh, in_specs=placed, o...]
    ppermute x22 -> x21, starting transfers between devices: 27.8 us -> 28.6 us  [exchange(): return lax.ppermute(value, axis, [(i, i ^ flip) for i in range(count)])]
    dynamic_slice x1 -> x0, local copies, waits for them, and re-layouts: 0.82 us -> none  [advance(): lax.dynamic_slice_in_dim(narrow, rows * (q ^ flip), rows, 1)]
    ppermute x2, waiting for transfers between devices: 2.46 us -> 1.69 us  [the longest x1 1.42 us: advance(): lax.ppermute(v[:, :HALO].astype(WIRE), PLANE, [((j + 1) % plane, j) for j...]
  transfers between devices with their start and end apart: 24 -> 23, of which waited for: 12 -> 12; matrix products, arithmetic and copies ran while one was open for 7% -> 8% of each run, Pallas kernels for 11% -> 8%
where the time goes in v3:
time: 72.8 us; the launch traced here: 72.6 us
  starting transfers between devices  31.3 us (43%)
  waiting for transfers between devices  16.8 us (23%)
  Pallas kernels  13.4 us (18%)
  local copies, waits for them, and re-layouts  5.92 us (8%)
  other arithmetic  4.32 us (6%)
  between operations  0.89 us (1%)
    ppermute x21, starting transfers between devices, exchange(): return lax.ppermute(value, axis, [(i, i ^ flip) for i in range(count)])  28.6 us
    ppermute x21, waiting for transfers between devices, exchange(): return lax.ppermute(value, axis, [(i, i ^ flip) for i in range(count)])  15.1 us
    pallas_call x1, Pallas kernels, advance(): pl.pallas_call(functools.partial(step_kernel, slabs), out_shape=[jax.Shap...  4.71 us
    pallas_call x3, Pallas kernels, x_filter(): pl.pallas_call(functools.partial(x_kernel, cores), out_shape=[jax.ShapeDt...  3.05 us
    pallas_call x1, Pallas kernels, fast_body(): pl.pallas_call(z_last_kernel, out_shape=jax.ShapeDtypeStruct((len(PRODUCT...  2.7 us
    select_n x2, other arithmetic, advance(): halos.append(jnp.where(low, after, before))  2.54 us
    unnamed x4, local copies, waits for them, and re-layouts  2.19 us
    convert_element_type x1, local copies, waits for them, and re-layouts, advance(): lax.dynamic_slice_in_dim(v, rows * (q ^ flip), rows, 1).astype(WIRE)  2 us
  transfers between devices with their start and end apart: 23, of which 12 were waited for; matrix products, arithmetic and copies ran while one was open for 8% of the time, Pallas kernels for 8%

profile of v3, /device:TPU:0, one launch (start us, length us, event | category | flops | bytes accessed | tf_op | source)
XLA Modules:
  0.0 72.6 jit_solution(567247764270631325)
XLA Ops:
  0.0 2.0 %fusion.2 = (bf16[3,32,1024]{2,1,0:T(8,128)(2,1)S(1)}, bf16[3,32,1024]{2,1,0:T(8,128)(2,1)S(1)}, bf16[3,32,1024]{2,1,0:T(8,128)(2,1)}) fusion(f32[3,1,128,1024]{3,2,0,1:T(8,128)} %bitcast.62, s32[]{:T(128)S(6)} %select_n.100, s32[]{:T(128)S(6)} %select_n.99, s32[]{:T(128)S(6)} %select_n.98), kind=kLoop, calls=%fused_computation.9 | loop fusion | bytes 1179660 | tf_op jit(solution)/shard_map/convert_element_type | solution.py:187
  2.0 5.0 %collective-permute-start.4 = (bf16[3,32,1024]{2,1,0:T(8,128)(2,1)S(1)}, bf16[3,32,1024]{2,1,0:T(8,128)(2,1)S(1)}, u32[]{:S(2)}, u32[]{:S(2)}) collective-permute-start(bf16[3,32,1024]{2,1,0:T(8,128)(2,1)S(1)} %get-tuple-element.88), channel_id=1, source_target_pairs={{0,3},{1,2},{2,1},{3,0},{4,7},{5,6},{6,5},{7,4},{8,11},{9,10},{10,... | collective-permute-start | bytes 589832 | tf_op jit(solution)/shard_map/ppermute | solution.py:35
  7.0 0.0 collective-permute-start.3
  7.1 0.0 copy-start.1
  7.1 0.6 collective-permute-start.2
  7.6 1.6 %convert_bitcast_fusion = bf16[3,128,1024]{2,1,0:T(8,128)(2,1)S(1)} fusion(f32[3,1,128,1024]{3,2,1,0:T(8,128)} %param.4), kind=kLoop, calls=%fused_computation | loop fusion | flops 393216 | bytes 2359296 | tf_op jit(solution)/shard_map/convert.1 | solution.py:449
  9.2 0.6 fusion.23
  9.9 1.7 %collective-permute-start.1 = (bf16[3,8,1024]{2,1,0:T(8,128)(2,1)}, bf16[3,8,1024]{2,1,0:T(8,128)(2,1)S(1)}, u32[]{:S(2)}, u32[]{:S(2)}) collective-permute-start(bf16[3,8,1024]{2,1,0:T(8,128)(2,1)} %get-tuple-element.91), channel_id=1, source_target_pairs={{0,4},{4,8},{8,12},{12,16},{16,20},{20,24},{24,28},{28,0},{1,5},{5... | collective-permute-start | bytes 147464 | tf_op jit(solution)/shard_map/ppermute | solution.py:183
  11.5 1.0 %collective-permute-start = (bf16[3,8,1024]{2,1,0:T(8,128)(2,1)}, bf16[3,8,1024]{2,1,0:T(8,128)(2,1)}, u32[]{:S(2)}, u32[]{:S(2)}) collective-permute-start(bf16[3,8,1024]{2,1,0:T(8,128)(2,1)} %get-tuple-element.92), channel_id=1, source_target_pairs={{4,0},{8,4},{12,8},{16,12},{20,16},{24,20},{28,24},{0,28},{5,1},{9... | collective-permute-start | bytes 147464 | tf_op jit(solution)/shard_map/ppermute | solution.py:184
  12.5 1.0 %dynamic-slice_bitcast_fusion.refs_0_ = f32[3,32,1024]{2,1,0:T(8,128)S(1)} fusion(f32[3,1,128,1024]{3,2,1,0:T(8,128)} %param.4, s32[]{:T(128)S(6)} %select_n.91), kind=kLoop, calls=%fused_computation.5 | loop fusion | bytes 786436 | tf_op jit(solution)/shard_map/dynamic_slice | solution.py:185
  14.2 0.3 collective-permute-done.1
  14.5 1.4 %collective-permute-done = bf16[3,8,1024]{2,1,0:T(8,128)(2,1)} collective-permute-done((bf16[3,8,1024]{2,1,0:T(8,128)(2,1)}, bf16[3,8,1024]{2,1,0:T(8,128)(2,1)}, u32[]{:S(2)}, u32[]{:S(2)}) %collective-permute-start) | collective-permute-done | bytes 49184 | tf_op jit(solution)/shard_map/ppermute | solution.py:184
  15.9 1.4 %fusion.20 = (bf16[3,8,1024]{2,1,0:T(8,128)(2,1)S(1)}, bf16[3,8,1024]{2,1,0:T(8,128)(2,1)S(1)}, bf16[3,8,1024]{2,1,0:T(8,128)(2,1)S(1)}) fusion(bf16[3,8,1024]{2,1,0:T(8,128)(2,1)} %collective-permute-done, f32[3,1,128,1024]{3,2,0,1:T(8,128)} %bitcast.63, s32[]{:T(128)S(6)} %select_n.114, bf16[3,8,1024]{2,1,0:T(8,128)(2,1)S(1)} %collective-permute-done.1, ...), kind=kLoop, calls=%fused_computation.35 | loop fusion | flops 221184 | bytes 540710 | tf_op jit(solution)/shard_map/jit(_where)/select_n | solution.py:196
  17.4 3.7 %collective-permute-start.7 = (bf16[3,8,1024]{2,1,0:T(8,128)(2,1)S(1)}, bf16[3,8,1024]{2,1,0:T(8,128)(2,1)S(1)}, u32[]{:S(2)}, u32[]{:S(2)}) collective-permute-start(bf16[3,8,1024]{2,1,0:T(8,128)(2,1)S(1)} %get-tuple-element.85), channel_id=1, source_target_pairs={{0,3},{1,2},{2,1},{3,0},{4,7},{5,6},{6,5},{7,4},{8,11},{9,10},{10,... | collective-permute-start | bytes 147464 | tf_op jit(solution)/shard_map/ppermute | solution.py:35
  21.1 0.0 collective-permute-start.6
  21.1 1.1 %fusion.5 = bf16[3,8,1024]{2,1,0:T(8,128)(2,1)S(1)} fusion(bf16[3,8,1024]{2,1,0:T(8,128)(2,1)} %collective-permute-done, f32[3,1,128,1024]{3,2,0,1:T(8,128)} %bitcast.64, s32[]{:T(128)S(6)} %select_n.93, bf16[3,8,1024]{2,1,0:T(8,128)(2,1)S(1)} %collective-permute-done.1, s32[]{:T(128)S(6)} %max.12, pred[8]{0:T(512)(128)(4,1)S(1)} %iota_compare_fusion, ...), kind=kLoop, calls=%fused_computation.20 | loop fusion | flops 73728 | bytes 245778 | tf_op jit(solution)/shard_map/jit(_where)/select_n | solution.py:196
  22.2 0.0 collective-permute-done.2.refs_1_
  22.2 0.8 %collective-permute-start.5 = (bf16[3,8,1024]{2,1,0:T(8,128)(2,1)S(1)}, bf16[3,8,1024]{2,1,0:T(8,128)(2,1)S(1)}, u32[]{:S(2)}, u32[]{:S(2)}) collective-permute-start(bf16[3,8,1024]{2,1,0:T(8,128)(2,1)S(1)} %fusion.5), channel_id=1, source_target_pairs={{0,1},{1,0},{2,3},{3,2},{4,5},{5,4},{6,7},{7,6},{8,9},{9,8},{10,11... | collective-permute-start | bytes 147464 | tf_op jit(solution)/shard_map/ppermute | solution.py:35
  23.0 0.1 pad_add_fusion.place_ref
  23.1 0.0 copy-done.1
  23.1 2.2 %copy-done = bf16[2,1024,1024]{2,1,0:T(8,128)(2,1)S(1)} copy-done((bf16[2,1024,1024]{2,1,0:T(8,128)(2,1)S(1)}, bf16[2,1024,1024]{2,1,0:T(8,128)(2,1)}, u32[]{:S(2)}) %copy-start) | copy-done | bytes 4194328
  25.3 1.5 %prepare.1 = (bf16[1024,1024]{1,0:T(8,128)(2,1)S(1)}, bf16[256,1024]{1,0:T(8,128)(2,1)S(1)}, bf16[512,1024]{1,0:T(8,128)(2,1)S(1)}, bf16[256,1024]{1,0:T(8,128)(2,1)S(1)}) custom-call(s32[3]{0:T(128)S(1)} %pad_add_fusion.place_ref, bf16[2,1024,1024]{2,1,0:T(8,128)(2,1)S(1)} %copy-done, bf16[1024,1024]{1,0:T(8,128)(2,1)S(1)} %copy-done.1), custom_call_target="tpu_custom_call" | custom-call | bytes 11100000 | tf_op jit(solution)/shard_map/prepare/pallas_call | solution.py:289
  26.8 0.0 collective-permute-done.7.refs_7_
  26.8 1.2 %collective-permute-done.6.refs_6_ = bf16[3,8,1024]{2,1,0:T(8,128)(2,1)S(1)} collective-permute-done((bf16[3,8,1024]{2,1,0:T(8,128)(2,1)S(1)}, bf16[3,8,1024]{2,1,0:T(8,128)(2,1)S(1)}, u32[]{:S(2)}, u32[]{:S(2)}) %collective-permute-start.6) | collective-permute-done | bytes 49184 | tf_op jit(solution)/shard_map/ppermute | solution.py:35
  28.0 0.0 collective-permute-done.4.refs_3_
  28.0 0.0 collective-permute-done.3.refs_2_
  28.0 0.0 collective-permute-done.5.refs_5_
  28.0 4.7 %advance.1 = (bf16[3,32,1024]{2,1,0:T(8,128)(2,1)S(1)}, bf16[3,32,1024]{2,1,0:T(8,128)(2,1)S(1)}, bf16[3,32,1024]{2,1,0:T(8,128)(2,1)S(1)}, bf16[3,32,1024]{2,1,0:T(8,128)(2,1)S(1)}) custom-call(s32[1]{0:T(128)} %bitcast.14.q_ref, f32[3,32,1024]{2,1,0:T(8,128)S(1)} %dynamic-slice_bitcast_fusion.refs_0_, ...), custom_call_target="tpu_custom_call" | custom-call | bytes 18500000 | tf_op jit(solution)/shard_map/advance/pallas_call | solution.py:203
  32.7 0.2 collective-permute-start.12
  32.9 2.9 %collective-permute-start.13 = (bf16[3,32,1024]{2,1,0:T(8,128)(2,1)S(1)}, bf16[3,32,1024]{2,1,0:T(8,128)(2,1)S(1)}, u32[]{:S(2)}, u32[]{:S(2)}) collective-permute-start(bf16[3,32,1024]{2,1,0:T(8,128)(2,1)S(1)} %get-tuple-element.68), channel_id=1, source_target_pairs={{0,2},{1,3},{2,0},{3,1},{4,6},{5,7},{6,4},{7,5},{8,10},{9,11},{10,... | collective-permute-start | bytes 589832 | tf_op jit(solution)/shard_map/ppermute | solution.py:35
  35.8 0.8 %x_filter_0.1 = (bf16[2,9,32,128]{3,2,1,0:T(8,128)(2,1)S(1)}, bf16[2,9,32,128]{3,2,1,0:T(8,128)(2,1)S(1)}, bf16[2,9,32,128]{3,2,1,0:T(8,128)(2,1)S(1)}, bf16[2,9,32,128]{3,2,1,0:T(8,128)(2,1)S(1)}) custom-call(bf16[1024,1024]{1,0:T(8,128)(2,1)S(1)} %get-tuple-element.53.matrix, bf16[3,32,1024]{2,1,0:T(8,128)(2,1)S(1)} %get-tuple-element.62.refs_0_), custom_call_target="tpu_custom_call" | custom-call | bytes 370000 | tf_op jit(solution)/shard_map/x_filter_0/pallas_call | solution.py:306
  36.6 1.5 %collective-permute-start.8 = (bf16[2,9,32,128]{3,2,1,0:T(8,128)(2,1)S(1)}, bf16[2,9,32,128]{3,2,1,0:T(8,128)(2,1)S(1)}, u32[]{:S(2)}, u32[]{:S(2)}) collective-permute-start(bf16[2,9,32,128]{3,2,1,0:T(8,128)(2,1)S(1)} %get-tuple-element.64), channel_id=1, source_target_pairs={{0,4},{4,0},{8,12},{12,8},{16,20},{20,16},{24,28},{28,24},{1,5},{5... | collective-permute-start | bytes 442376 | tf_op jit(solution)/shard_map/ppermute | solution.py:35
  38.2 1.5 %collective-permute-start.9 = (bf16[2,9,32,128]{3,2,1,0:T(8,128)(2,1)S(1)}, bf16[2,9,32,128]{3,2,1,0:T(8,128)(2,1)S(1)}, u32[]{:S(2)}, u32[]{:S(2)}) collective-permute-start(bf16[2,9,32,128]{3,2,1,0:T(8,128)(2,1)S(1)} %get-tuple-element.65), channel_id=1, source_target_pairs={{0,16},{4,20},{8,24},{12,28},{16,0},{20,4},{24,8},{28,12},{1,17},{... | collective-permute-start | bytes 442376 | tf_op jit(solution)/shard_map/ppermute | solution.py:35
  39.7 0.5 collective-permute-start.10
  40.2 3.2 %collective-permute-done.8.refs_3_ = bf16[2,9,32,128]{3,2,1,0:T(8,128)(2,1)S(1)} collective-permute-done((bf16[2,9,32,128]{3,2,1,0:T(8,128)(2,1)S(1)}, bf16[2,9,32,128]{3,2,1,0:T(8,128)(2,1)S(1)}, u32[]{:S(2)}, u32[]{:S(2)}) %collective-permute-start.8) | collective-permute-done | bytes 147488 | tf_op jit(solution)/shard_map/ppermute | solution.py:35
  43.4 0.3 collective-permute-start.17
  43.7 0.5 collective-permute-done.9.refs_4_
  44.2 1.5 %collective-permute-done.10.refs_5_ = bf16[2,9,32,128]{3,2,1,0:T(8,128)(2,1)S(1)} collective-permute-done((bf16[2,9,32,128]{3,2,1,0:T(8,128)(2,1)S(1)}, bf16[2,9,32,128]{3,2,1,0:T(8,128)(2,1)S(1)}, u32[]{:S(2)}, u32[]{:S(2)}) %collective-permute-start.10) | collective-permute-done | bytes 147488 | tf_op jit(solution)/shard_map/ppermute | solution.py:35
  45.8 0.0 collective-permute-done.12.refs_0_
  45.8 0.0 collective-permute-done.13.refs_1_
  45.8 1.4 %x_filter_1.1 = (bf16[2,9,64,128]{3,2,1,0:T(8,128)(2,1)S(1)}, bf16[2,9,64,128]{3,2,1,0:T(8,128)(2,1)S(1)}, bf16[2,9,64,128]{3,2,1,0:T(8,128)(2,1)S(1)}, bf16[2,9,64,128]{3,2,1,0:T(8,128)(2,1)S(1)}) custom-call(bf16[1024,1024]{1,0:T(8,128)(2,1)S(1)} %get-tuple-element.53.matrix, bf16[3,32,1024]{2,1,0:T(8,128)(2,1)S(1)} %collective-permute-done.12.refs_0_, ...), custom_call_target="tpu_custom_call" | custom-call | bytes 370000 | tf_op jit(solution)/shard_map/x_filter_1/pallas_call | solution.py:306
  47.2 2.4 %collective-permute-start.14 = (bf16[2,9,64,128]{3,2,1,0:T(8,128)(2,1)S(1)}, bf16[2,9,64,128]{3,2,1,0:T(8,128)(2,1)S(1)}, u32[]{:S(2)}, u32[]{:S(2)}) collective-permute-start(bf16[2,9,64,128]{3,2,1,0:T(8,128)(2,1)S(1)} %get-tuple-element.74), channel_id=1, source_target_pairs={{0,4},{4,0},{8,12},{12,8},{16,20},{20,16},{24,28},{28,24},{1,5},{5... | collective-permute-start | bytes 884744 | tf_op jit(solution)/shard_map/ppermute | solution.py:35
  49.7 2.0 %collective-permute-start.15 = (bf16[2,9,64,128]{3,2,1,0:T(8,128)(2,1)S(1)}, bf16[2,9,64,128]{3,2,1,0:T(8,128)(2,1)S(1)}, u32[]{:S(2)}, u32[]{:S(2)}) collective-permute-start(bf16[2,9,64,128]{3,2,1,0:T(8,128)(2,1)S(1)} %get-tuple-element.75), channel_id=1, source_target_pairs={{0,16},{4,20},{8,24},{12,28},{16,0},{20,4},{24,8},{28,12},{1,17},{... | collective-permute-start | bytes 884744 | tf_op jit(solution)/shard_map/ppermute | solution.py:35
  51.6 0.0 collective-permute-start.16
  51.7 0.1 collective-permute-start.11
  51.8 0.0 collective-permute-done.17.refs_0_
  51.8 0.5 collective-permute-start.18
  52.3 1.3 %collective-permute-done.18.refs_1_ = bf16[3,32,1024]{2,1,0:T(8,128)(2,1)S(1)} collective-permute-done((bf16[3,32,1024]{2,1,0:T(8,128)(2,1)S(1)}, bf16[3,32,1024]{2,1,0:T(8,128)(2,1)S(1)}, u32[]{:S(2)}, u32[]{:S(2)}) %collective-permute-start.18) | collective-permute-done | bytes 196640 | tf_op jit(solution)/shard_map/ppermute | solution.py:35
  53.6 0.8 %x_filter_2.1 = (bf16[1,9,64,128]{3,2,1,0:T(8,128)(2,1)S(1)}, bf16[1,9,64,128]{3,2,1,0:T(8,128)(2,1)S(1)}, bf16[1,9,64,128]{3,2,1,0:T(8,128)(2,1)S(1)}, bf16[1,9,64,128]{3,2,1,0:T(8,128)(2,1)S(1)}) custom-call(bf16[1024,1024]{1,0:T(8,128)(2,1)S(1)} %get-tuple-element.53.matrix, bf16[3,32,1024]{2,1,0:T(8,128)(2,1)S(1)} %collective-permute-done.17.refs_0_, ...), custom_call_target="tpu_custom_call" | custom-call | bytes 370000 | tf_op jit(solution)/shard_map/x_filter_2/pallas_call | solution.py:306
  54.4 1.6 %collective-permute-start.19 = (bf16[1,9,64,128]{3,2,1,0:T(8,128)(2,1)S(1)}, bf16[1,9,64,128]{3,2,1,0:T(8,128)(2,1)S(1)}, u32[]{:S(2)}, u32[]{:S(2)}) collective-permute-start(bf16[1,9,64,128]{3,2,1,0:T(8,128)(2,1)S(1)} %get-tuple-element.79), channel_id=1, source_target_pairs={{0,4},{4,0},{8,12},{12,8},{16,20},{20,16},{24,28},{28,24},{1,5},{5... | collective-permute-start | bytes 442376 | tf_op jit(solution)/shard_map/ppermute | solution.py:35
  56.0 1.7 %collective-permute-done.14.refs_8_ = bf16[2,9,64,128]{3,2,1,0:T(8,128)(2,1)S(1)} collective-permute-done((bf16[2,9,64,128]{3,2,1,0:T(8,128)(2,1)S(1)}, bf16[2,9,64,128]{3,2,1,0:T(8,128)(2,1)S(1)}, u32[]{:S(2)}, u32[]{:S(2)}) %collective-permute-start.14) | collective-permute-done | bytes 294944 | tf_op jit(solution)/shard_map/ppermute | solution.py:35
  57.7 1.6 %collective-permute-start.20 = (bf16[1,9,64,128]{3,2,1,0:T(8,128)(2,1)S(1)}, bf16[1,9,64,128]{3,2,1,0:T(8,128)(2,1)S(1)}, u32[]{:S(2)}, u32[]{:S(2)}) collective-permute-start(bf16[1,9,64,128]{3,2,1,0:T(8,128)(2,1)S(1)} %get-tuple-element.80), channel_id=1, source_target_pairs={{0,16},{4,20},{8,24},{12,28},{16,0},{20,4},{24,8},{28,12},{1,17},{... | collective-permute-start | bytes 442376 | tf_op jit(solution)/shard_map/ppermute | solution.py:35
  59.2 0.0 collective-permute-done.15.refs_9_
  59.2 3.3 %collective-permute-start.21 = (bf16[1,9,64,128]{3,2,1,0:T(8,128)(2,1)S(1)}, bf16[1,9,64,128]{3,2,1,0:T(8,128)(2,1)S(1)}, u32[]{:S(2)}, u32[]{:S(2)}) collective-permute-start(bf16[1,9,64,128]{3,2,1,0:T(8,128)(2,1)S(1)} %get-tuple-element.82), channel_id=1, source_target_pairs={{0,20},{4,16},{8,28},{12,24},{16,4},{20,0},{24,12},{28,8},{1,21},{... | collective-permute-start | bytes 442376 | tf_op jit(solution)/shard_map/ppermute | solution.py:35
  62.6 1.9 %collective-permute-done.16.refs_10_ = bf16[2,9,64,128]{3,2,1,0:T(8,128)(2,1)S(1)} collective-permute-done((bf16[2,9,64,128]{3,2,1,0:T(8,128)(2,1)S(1)}, bf16[2,9,64,128]{3,2,1,0:T(8,128)(2,1)S(1)}, u32[]{:S(2)}, u32[]{:S(2)}) %collective-permute-start.16) | collective-permute-done | bytes 294944 | tf_op jit(solution)/shard_map/ppermute | solution.py:35
  64.6 0.0 collective-permute-done.11.refs_6_
  64.6 1.4 %z_filter_first.1.passed = f32[9,128,1024]{2,1,0:T(8,128)S(1)} custom-call(bf16[256,1024]{1,0:T(8,128)(2,1)S(1)} %get-tuple-element.51.refs_0_, bf16[512,1024]{1,0:T(8,128)(2,1)S(1)} %get-tuple-element.52.refs_1_.line_second, bf16[2,9,32,128]{3,2,1,0:T(8,128)(2,1)S(1)} %get-tuple-element.63.refs_2_, ...), custom_call_target="tpu_custom_call" | custom-call | bytes 370000 | tf_op jit(solution)/shard_map/z_filter_first/pallas_call | solution.py:334
  66.0 0.1 pad_maximum_fusion
  66.1 0.0 collective-permute-done.19.refs_1_
  66.1 0.2 collective-permute-done.20.refs_2_
  66.3 1.6 %collective-permute-done.21.refs_3_ = bf16[1,9,64,128]{3,2,1,0:T(8,128)(2,1)S(1)} collective-permute-done((bf16[1,9,64,128]{3,2,1,0:T(8,128)(2,1)S(1)}, bf16[1,9,64,128]{3,2,1,0:T(8,128)(2,1)S(1)}, u32[]{:S(2)}, u32[]{:S(2)}) %collective-permute-start.21) | collective-permute-done | bytes 147488 | tf_op jit(solution)/shard_map/ppermute | solution.py:35
  67.9 0.0 collective-permute-start.22
  67.9 2.0 %collective-permute-done.22.others = bf16[4,9,64,128]{3,2,1,0:T(8,128)(2,1)S(1)} collective-permute-done((bf16[4,9,64,128]{3,2,1,0:T(8,128)(2,1)S(1)}, bf16[4,9,64,128]{3,2,1,0:T(8,128)(2,1)S(1)}, u32[]{:S(2)}, u32[]{:S(2)}) %collective-permute-start.22) | collective-permute-done | bytes 589856 | tf_op jit(solution)/shard_map/ppermute | solution.py:35
  69.9 2.7 %z_filter_last.1 = f32[6,1,128,1024]{3,2,1,0:T(8,128)} custom-call(f32[9,128,1024]{2,1,0:T(8,128)S(1)} %z_filter_first.1.passed, bf16[512,1024]{1,0:T(8,128)(2,1)S(1)} %get-tuple-element.52.refs_1_.line_second, bf16[256,1024]{1,0:T(8,128)(2,1)S(1)} %get-tuple-element.77.line_last, bf16[4,9,64,128]{3,2,1,0:T(8,128)(2,1)S(1)} %collective-permute-done.22.others, ...), custom_call_target="tpu_custom_call" | custom-call | bytes 370000 | tf_op jit(solution)/shard_map/z_filter_last/pallas_call | solution.py:344
  (11 shorter events, 0.1 us)
Async XLA Ops:
  2.0 26.0 %collective-permute-start.4 = (bf16[3,32,1024]{2,1,0:T(8,128)(2,1)S(1)}, bf16[3,32,1024]{2,1,0:T(8,128)(2,1)S(1)}, u32[]{:S(2)}, u32[]{:S(2)}) collective-permute-start(bf16[3,32,1024]{2,1,0:T(8,128)(2,1)S(1)} %get-tuple-element.88), channel_id=1, source_target_pairs={{0,3},{1,2},{2,1},{3,0},{4,7},{5,6},{6,5},{7,4},{8,11},{9,10},{10,... | collective-permute-start | bytes 589832 | tf_op jit(solution)/shard_map/ppermute | solution.py:35
  7.0 20.9 %collective-permute-start.3 = (bf16[3,32,1024]{2,1,0:T(8,128)(2,1)S(1)}, bf16[3,32,1024]{2,1,0:T(8,128)(2,1)S(1)}, u32[]{:S(2)}, u32[]{:S(2)}) collective-permute-start(bf16[3,32,1024]{2,1,0:T(8,128)(2,1)S(1)} %get-tuple-element.89), channel_id=1, source_target_pairs={{0,2},{1,3},{2,0},{3,1},{4,6},{5,7},{6,4},{7,5},{8,10},{9,11},{10,... | collective-permute-start | bytes 589832 | tf_op jit(solution)/shard_map/ppermute | solution.py:35
  7.1 16.0 %copy-start.1 = (bf16[1024,1024]{1,0:T(8,128)(2,1)S(1)}, bf16[1024,1024]{1,0:T(8,128)(2,1)}, u32[]{:S(2)}) copy-start(bf16[1024,1024]{1,0:T(8,128)(2,1)} %z_filter.1) | copy-start | bytes 6291460
  7.1 15.1 %collective-permute-start.2 = (bf16[3,32,1024]{2,1,0:T(8,128)(2,1)}, bf16[3,32,1024]{2,1,0:T(8,128)(2,1)S(1)}, u32[]{:S(2)}, u32[]{:S(2)}) collective-permute-start(bf16[3,32,1024]{2,1,0:T(8,128)(2,1)} %get-tuple-element.90), channel_id=1, source_target_pairs={{0,1},{1,0},{2,3},{3,2},{4,5},{5,4},{6,7},{7,6},{8,9},{9,8},{10,11... | collective-permute-start | bytes 589832 | tf_op jit(solution)/shard_map/ppermute | solution.py:35
  9.9 4.7 %collective-permute-start.1 = (bf16[3,8,1024]{2,1,0:T(8,128)(2,1)}, bf16[3,8,1024]{2,1,0:T(8,128)(2,1)S(1)}, u32[]{:S(2)}, u32[]{:S(2)}) collective-permute-start(bf16[3,8,1024]{2,1,0:T(8,128)(2,1)} %get-tuple-element.91), channel_id=1, source_target_pairs={{0,4},{4,8},{8,12},{12,16},{16,20},{20,24},{24,28},{28,0},{1,5},{5... | collective-permute-start | bytes 147464 | tf_op jit(solution)/shard_map/ppermute | solution.py:183
  11.5 4.4 %collective-permute-start = (bf16[3,8,1024]{2,1,0:T(8,128)(2,1)}, bf16[3,8,1024]{2,1,0:T(8,128)(2,1)}, u32[]{:S(2)}, u32[]{:S(2)}) collective-permute-start(bf16[3,8,1024]{2,1,0:T(8,128)(2,1)} %get-tuple-element.92), channel_id=1, source_target_pairs={{4,0},{8,4},{12,8},{16,12},{20,16},{24,20},{28,24},{0,28},{5,1},{9... | collective-permute-start | bytes 147464 | tf_op jit(solution)/shard_map/ppermute | solution.py:184
  17.4 9.4 %collective-permute-start.7 = (bf16[3,8,1024]{2,1,0:T(8,128)(2,1)S(1)}, bf16[3,8,1024]{2,1,0:T(8,128)(2,1)S(1)}, u32[]{:S(2)}, u32[]{:S(2)}) collective-permute-start(bf16[3,8,1024]{2,1,0:T(8,128)(2,1)S(1)} %get-tuple-element.85), channel_id=1, source_target_pairs={{0,3},{1,2},{2,1},{3,0},{4,7},{5,6},{6,5},{7,4},{8,11},{9,10},{10,... | collective-permute-start | bytes 147464 | tf_op jit(solution)/shard_map/ppermute | solution.py:35
  21.1 6.9 %collective-permute-start.6 = (bf16[3,8,1024]{2,1,0:T(8,128)(2,1)S(1)}, bf16[3,8,1024]{2,1,0:T(8,128)(2,1)S(1)}, u32[]{:S(2)}, u32[]{:S(2)}) collective-permute-start(bf16[3,8,1024]{2,1,0:T(8,128)(2,1)S(1)} %get-tuple-element.86), channel_id=1, source_target_pairs={{0,2},{1,3},{2,0},{3,1},{4,6},{5,7},{6,4},{7,5},{8,10},{9,11},{10,... | collective-permute-start | bytes 147464 | tf_op jit(solution)/shard_map/ppermute | solution.py:35
  22.2 5.8 %collective-permute-start.5 = (bf16[3,8,1024]{2,1,0:T(8,128)(2,1)S(1)}, bf16[3,8,1024]{2,1,0:T(8,128)(2,1)S(1)}, u32[]{:S(2)}, u32[]{:S(2)}) collective-permute-start(bf16[3,8,1024]{2,1,0:T(8,128)(2,1)S(1)} %fusion.5), channel_id=1, source_target_pairs={{0,1},{1,0},{2,3},{3,2},{4,5},{5,4},{6,7},{7,6},{8,9},{9,8},{10,11... | collective-permute-start | bytes 147464 | tf_op jit(solution)/shard_map/ppermute | solution.py:35
  23.1 2.2 %copy-start = (bf16[2,1024,1024]{2,1,0:T(8,128)(2,1)S(1)}, bf16[2,1024,1024]{2,1,0:T(8,128)(2,1)}, u32[]{:S(2)}) copy-start(bf16[2,1024,1024]{2,1,0:T(8,128)(2,1)} %x_filters.1) | copy-start | bytes 12582916
  32.7 13.1 %collective-permute-start.12 = (bf16[3,32,1024]{2,1,0:T(8,128)(2,1)S(1)}, bf16[3,32,1024]{2,1,0:T(8,128)(2,1)S(1)}, u32[]{:S(2)}, u32[]{:S(2)}) collective-permute-start(bf16[3,32,1024]{2,1,0:T(8,128)(2,1)S(1)} %get-tuple-element.67), channel_id=1, source_target_pairs={{0,1},{1,0},{2,3},{3,2},{4,5},{5,4},{6,7},{7,6},{8,9},{9,8},{10,11... | collective-permute-start | bytes 589832 | tf_op jit(solution)/shard_map/ppermute | solution.py:35
  32.9 12.9 %collective-permute-start.13 = (bf16[3,32,1024]{2,1,0:T(8,128)(2,1)S(1)}, bf16[3,32,1024]{2,1,0:T(8,128)(2,1)S(1)}, u32[]{:S(2)}, u32[]{:S(2)}) collective-permute-start(bf16[3,32,1024]{2,1,0:T(8,128)(2,1)S(1)} %get-tuple-element.68), channel_id=1, source_target_pairs={{0,2},{1,3},{2,0},{3,1},{4,6},{5,7},{6,4},{7,5},{8,10},{9,11},{10,... | collective-permute-start | bytes 589832 | tf_op jit(solution)/shard_map/ppermute | solution.py:35
  36.6 6.7 %collective-permute-start.8 = (bf16[2,9,32,128]{3,2,1,0:T(8,128)(2,1)S(1)}, bf16[2,9,32,128]{3,2,1,0:T(8,128)(2,1)S(1)}, u32[]{:S(2)}, u32[]{:S(2)}) collective-permute-start(bf16[2,9,32,128]{3,2,1,0:T(8,128)(2,1)S(1)} %get-tuple-element.64), channel_id=1, source_target_pairs={{0,4},{4,0},{8,12},{12,8},{16,20},{20,16},{24,28},{28,24},{1,5},{5... | collective-permute-start | bytes 442376 | tf_op jit(solution)/shard_map/ppermute | solution.py:35
  38.2 6.0 %collective-permute-start.9 = (bf16[2,9,32,128]{3,2,1,0:T(8,128)(2,1)S(1)}, bf16[2,9,32,128]{3,2,1,0:T(8,128)(2,1)S(1)}, u32[]{:S(2)}, u32[]{:S(2)}) collective-permute-start(bf16[2,9,32,128]{3,2,1,0:T(8,128)(2,1)S(1)} %get-tuple-element.65), channel_id=1, source_target_pairs={{0,16},{4,20},{8,24},{12,28},{16,0},{20,4},{24,8},{28,12},{1,17},{... | collective-permute-start | bytes 442376 | tf_op jit(solution)/shard_map/ppermute | solution.py:35
  39.7 6.1 %collective-permute-start.10 = (bf16[2,9,32,128]{3,2,1,0:T(8,128)(2,1)S(1)}, bf16[2,9,32,128]{3,2,1,0:T(8,128)(2,1)S(1)}, u32[]{:S(2)}, u32[]{:S(2)}) collective-permute-start(bf16[2,9,32,128]{3,2,1,0:T(8,128)(2,1)S(1)} %get-tuple-element.66), channel_id=1, source_target_pairs={{0,20},{4,16},{8,28},{12,24},{16,4},{20,0},{24,12},{28,8},{1,21},{... | collective-permute-start | bytes 442376 | tf_op jit(solution)/shard_map/ppermute | solution.py:35
  43.4 8.4 %collective-permute-start.17 = (bf16[3,32,1024]{2,1,0:T(8,128)(2,1)S(1)}, bf16[3,32,1024]{2,1,0:T(8,128)(2,1)S(1)}, u32[]{:S(2)}, u32[]{:S(2)}) collective-permute-start(bf16[3,32,1024]{2,1,0:T(8,128)(2,1)S(1)} %get-tuple-element.78), channel_id=1, source_target_pairs={{0,3},{1,2},{2,1},{3,0},{4,7},{5,6},{6,5},{7,4},{8,11},{9,10},{10,... | collective-permute-start | bytes 589832 | tf_op jit(solution)/shard_map/ppermute | solution.py:35
  47.2 10.4 %collective-permute-start.14 = (bf16[2,9,64,128]{3,2,1,0:T(8,128)(2,1)S(1)}, bf16[2,9,64,128]{3,2,1,0:T(8,128)(2,1)S(1)}, u32[]{:S(2)}, u32[]{:S(2)}) collective-permute-start(bf16[2,9,64,128]{3,2,1,0:T(8,128)(2,1)S(1)} %get-tuple-element.74), channel_id=1, source_target_pairs={{0,4},{4,0},{8,12},{12,8},{16,20},{20,16},{24,28},{28,24},{1,5},{5... | collective-permute-start | bytes 884744 | tf_op jit(solution)/shard_map/ppermute | solution.py:35
  49.7 9.6 %collective-permute-start.15 = (bf16[2,9,64,128]{3,2,1,0:T(8,128)(2,1)S(1)}, bf16[2,9,64,128]{3,2,1,0:T(8,128)(2,1)S(1)}, u32[]{:S(2)}, u32[]{:S(2)}) collective-permute-start(bf16[2,9,64,128]{3,2,1,0:T(8,128)(2,1)S(1)} %get-tuple-element.75), channel_id=1, source_target_pairs={{0,16},{4,20},{8,24},{12,28},{16,0},{20,4},{24,8},{28,12},{1,17},{... | collective-permute-start | bytes 884744 | tf_op jit(solution)/shard_map/ppermute | solution.py:35
  51.6 12.9 %collective-permute-start.16 = (bf16[2,9,64,128]{3,2,1,0:T(8,128)(2,1)S(1)}, bf16[2,9,64,128]{3,2,1,0:T(8,128)(2,1)S(1)}, u32[]{:S(2)}, u32[]{:S(2)}) collective-permute-start(bf16[2,9,64,128]{3,2,1,0:T(8,128)(2,1)S(1)} %get-tuple-element.76), channel_id=1, source_target_pairs={{0,20},{4,16},{8,28},{12,24},{16,4},{20,0},{24,12},{28,8},{1,21},{... | collective-permute-start | bytes 884744 | tf_op jit(solution)/shard_map/ppermute | solution.py:35
  51.7 12.9 %collective-permute-start.11 = (bf16[4,9,32,128]{3,2,1,0:T(8,128)(2,1)S(1)}, bf16[4,9,32,128]{3,2,1,0:T(8,128)(2,1)S(1)}, u32[]{:S(2)}, u32[]{:S(2)}) collective-permute-start(bf16[4,9,32,128]{3,2,1,0:T(8,128)(2,1)S(1)} %pad_maximum_fusion.1), channel_id=1, source_target_pairs={{0,8},{8,0},{16,24},{24,16},{1,9},{9,1},{17,25},{25,17},{2,10},{10... | collective-permute-start | bytes 884744 | tf_op jit(solution)/shard_map/ppermute | solution.py:35
  51.8 1.8 %collective-permute-start.18 = (bf16[3,32,1024]{2,1,0:T(8,128)(2,1)S(1)}, bf16[3,32,1024]{2,1,0:T(8,128)(2,1)S(1)}, u32[]{:S(2)}, u32[]{:S(2)}) collective-permute-start(bf16[3,32,1024]{2,1,0:T(8,128)(2,1)S(1)} %collective-permute-done.17.refs_0_), channel_id=1, source_target_pairs={{0,8},{8,0},{16,24},{24,16},{1,9},{9,1},{17,25},{25,17},{2,10},{10... | collective-permute-start | bytes 589832 | tf_op jit(solution)/shard_map/ppermute | solution.py:35
  54.4 11.7 %collective-permute-start.19 = (bf16[1,9,64,128]{3,2,1,0:T(8,128)(2,1)S(1)}, bf16[1,9,64,128]{3,2,1,0:T(8,128)(2,1)S(1)}, u32[]{:S(2)}, u32[]{:S(2)}) collective-permute-start(bf16[1,9,64,128]{3,2,1,0:T(8,128)(2,1)S(1)} %get-tuple-element.79), channel_id=1, source_target_pairs={{0,4},{4,0},{8,12},{12,8},{16,20},{20,16},{24,28},{28,24},{1,5},{5... | collective-permute-start | bytes 442376 | tf_op jit(solution)/shard_map/ppermute | solution.py:35
  57.7 8.6 %collective-permute-start.20 = (bf16[1,9,64,128]{3,2,1,0:T(8,128)(2,1)S(1)}, bf16[1,9,64,128]{3,2,1,0:T(8,128)(2,1)S(1)}, u32[]{:S(2)}, u32[]{:S(2)}) collective-permute-start(bf16[1,9,64,128]{3,2,1,0:T(8,128)(2,1)S(1)} %get-tuple-element.80), channel_id=1, source_target_pairs={{0,16},{4,20},{8,24},{12,28},{16,0},{20,4},{24,8},{28,12},{1,17},{... | collective-permute-start | bytes 442376 | tf_op jit(solution)/shard_map/ppermute | solution.py:35
  59.2 8.6 %collective-permute-start.21 = (bf16[1,9,64,128]{3,2,1,0:T(8,128)(2,1)S(1)}, bf16[1,9,64,128]{3,2,1,0:T(8,128)(2,1)S(1)}, u32[]{:S(2)}, u32[]{:S(2)}) collective-permute-start(bf16[1,9,64,128]{3,2,1,0:T(8,128)(2,1)S(1)} %get-tuple-element.82), channel_id=1, source_target_pairs={{0,20},{4,16},{8,28},{12,24},{16,4},{20,0},{24,12},{28,8},{1,21},{... | collective-permute-start | bytes 442376 | tf_op jit(solution)/shard_map/ppermute | solution.py:35
  67.9 2.0 %collective-permute-start.22 = (bf16[4,9,64,128]{3,2,1,0:T(8,128)(2,1)S(1)}, bf16[4,9,64,128]{3,2,1,0:T(8,128)(2,1)S(1)}, u32[]{:S(2)}, u32[]{:S(2)}) collective-permute-start(bf16[4,9,64,128]{3,2,1,0:T(8,128)(2,1)S(1)} %pad_maximum_fusion), channel_id=1, source_target_pairs={{0,8},{8,0},{16,24},{24,16},{1,9},{9,1},{17,25},{25,17},{2,10},{10... | collective-permute-start | bytes 1769480 | tf_op jit(solution)/shard_map/ppermute | solution.py:35

commit v4 on v3

--- a/solution.py
+++ b/solution.py
@@ -43,20 +43,25 @@
     return pl.BlockSpec(memory_space=memory)
 
 
-def prepare_kernel(slabs, place_ref, x_filters, z_filter, rows_out, *refs):
-    lines_out, (sem,) = refs[: len(CHUNKS)], refs[len(CHUNKS) :]
-    q, me, prof = place_ref[0], place_ref[1], place_ref[2]
+def x_rows_kernel(place_ref, x_filters, rows_out, sem):
+    me, prof = place_ref[1], place_ref[2]
     copies = []
     for core in range(2):
         for slot, flip in enumerate(CHIPS):
+            number = core * len(CHIPS) + slot
             at = pl.multiple_of((me ^ flip ^ (2 * core)) * 128, 128)
-            to = (core * len(CHIPS) + slot) * 128
             copies.append(
                 pltpu.make_async_copy(
-                    x_filters.at[prof, pl.ds(at, 128)], rows_out.at[pl.ds(to, 128)], sem.at[core * len(CHIPS) + slot]
+                    x_filters.at[prof, pl.ds(at, 128)], rows_out.at[pl.ds(number * 128, 128)], sem.at[number]
                 )
             )
             copies[-1].start()
+    for copy in copies:
+        copy.wait()
+
+
+def z_lines_kernel(slabs, place_ref, z_filter, *lines_out):
+    q, me = place_ref[0], place_ref[1]
     rows = 128 // slabs
     target = lax.broadcasted_iota(jnp.int32, (128, 128), 0)
     source = lax.broadcasted_iota(jnp.int32, (128, 128), 1)
@@ -73,8 +78,35 @@
                 else:
                     at = (slot * 2 + core) * cells
                 lines_out[number][at : at + cells] = part
+
+
+def edge_kernel(slabs, q_ref, velocity, own, tail, head, *refs):
+    halos, (cells, line, sem) = refs[:slabs], refs[slabs:]
+    q = q_ref[0]
+    block, width = cells.shape[1:]
+    rows = block // slabs
+    copies = [pltpu.make_async_copy(velocity.at[comp, 0], cells.at[comp], sem.at[comp]) for comp in range(3)]
     for copy in copies:
-        copy.wait()
+        copy.start()
+
+    def lay(comp, before, after):
+        last = cells[comp, pl.ds(pl.multiple_of(before, HALO), HALO)][HALO - REACH :]
+        first = cells[comp, pl.ds(pl.multiple_of(after, HALO), HALO)][:REACH]
+        for part in range(8):
+            lanes = slice(width // 8 * part, width // 8 * (part + 1))
+            line[pl.ds(part, REACH, stride=8)] = last[:, lanes]
+            line[pl.ds(8 * REACH + part, REACH, stride=8)] = first[:, lanes]
+
+    for comp in range(3):
+        copies[comp].wait()
+        own[comp] = cells[comp, pl.ds(pl.multiple_of(rows * q, rows), rows)]
+        lay(comp, block - HALO, 0)
+        tail[comp] = line[: 8 * REACH].astype(WIRE)
+        head[comp] = line[8 * REACH :].astype(WIRE)
+        for flip in range(slabs):
+            at = rows * (q ^ flip)
+            lay(comp, jnp.maximum(at - HALO, 0), jnp.minimum(at + rows, block - HALO))
+            halos[flip][comp] = line[...].astype(WIRE)
 
 
 def step_kernel(slabs, q_ref, *refs):
@@ -98,10 +130,8 @@
                             8 * half : 8 * half + 8, 128 * part : 128 * part + 128
                         ]
             halo = halos[flip][comp].astype(jnp.float32)
-            for part in range(parts):
-                lanes = halo[:, 128 * part : 128 * part + 128]
-                start[y, comp, pl.ds((REACH + rows) * 8 + part, REACH, stride=8)] = lanes[:REACH]
-                start[y, comp, pl.ds(part, REACH, stride=8)] = lanes[HALO - REACH :]
+            start[y, comp, : 8 * REACH] = halo[: 8 * REACH]
+            start[y, comp, 8 * (REACH + rows) :] = halo[8 * REACH :]
 
     lane = lax.broadcasted_iota(jnp.int32, (8, 128), 1)
     at_end, at_start = lane == 127, lane == 0
@@ -180,20 +210,32 @@
     v = velocity[:, 0]
     block, width = v.shape[1:]
     rows = block // slabs
-    tail = lax.ppermute(v[:, block - HALO :].astype(WIRE), PLANE, [(j, (j + 1) % plane) for j in range(plane)])
-    head = lax.ppermute(v[:, :HALO].astype(WIRE), PLANE, [((j + 1) % plane, j) for j in range(plane)])
-    mains = [lax.dynamic_slice_in_dim(v, rows * q, rows, 1)]
-    for flip in range(1, slabs):
-        mains.append(exchange(lax.dynamic_slice_in_dim(v, rows * (q ^ flip), rows, 1).astype(WIRE), "col", flip))
-    low = lax.broadcasted_iota(jnp.int32, (3, HALO, width), 1) < HALO // 2
-    halos = []
+    slabs_sent = [lax.dynamic_slice_in_dim(v, rows * (q ^ flip), rows, 1).astype(WIRE) for flip in range(1, slabs)]
+    edge = jax.ShapeDtypeStruct((3, 8 * REACH, width // 8), WIRE)
+    around = jax.ShapeDtypeStruct((3, 16 * REACH, width // 8), WIRE)
+    own, tail, head, *halos = pl.pallas_call(
+        functools.partial(edge_kernel, slabs),
+        out_shape=[jax.ShapeDtypeStruct((3, rows, width), v.dtype), edge, edge] + [around] * slabs,
+        in_specs=[whole(pltpu.SMEM), whole(pl.ANY)],
+        out_specs=[whole()] * (3 + slabs),
+        scratch_shapes=[
+            pltpu.VMEM((3, block, width), v.dtype),
+            pltpu.VMEM((16 * REACH, width // 8), v.dtype),
+            pltpu.SemaphoreType.DMA((3,)),
+        ],
+        compiler_params=pltpu.CompilerParams(vmem_limit_bytes=VMEM_BYTES),
+        cost_estimate=cost("prepare"),
+        name="edges",
+    )(delayed(q.reshape(1), *slabs_sent), velocity)
+    tail = lax.ppermute(tail, PLANE, [(j, (j + 1) % plane) for j in range(plane)])
+    head = lax.ppermute(head, PLANE, [((j + 1) % plane, j) for j in range(plane)])
+    mains = [own] + [exchange(slabs_sent[flip - 1], "col", flip) for flip in range(1, slabs)]
+    outer = jnp.concatenate([tail, head], axis=1)
+    before = lax.broadcasted_iota(jnp.int32, around.shape, 1) < 8 * REACH
     for flip in range(slabs):
         at = rows * (q ^ flip)
-        before = lax.dynamic_slice_in_dim(v, jnp.maximum(at - HALO, 0), HALO, 1).astype(WIRE)
-        after = lax.dynamic_slice_in_dim(v, jnp.minimum(at + rows, block - HALO), HALO, 1).astype(WIRE)
-        before = jnp.where(at == 0, tail, before)
-        after = jnp.where(at == block - rows, head, after)
-        halos.append(jnp.where(low, after, before))
+        outside = jnp.logical_or(jnp.logical_and(before, at == 0), jnp.logical_and(~before, at == block - rows))
+        halos[flip] = jnp.where(outside, outer, halos[flip])
     halos[1], mains[1] = lax.optimization_barrier((halos[1], mains[1]))
     for flip in (3, 2, 1):
         halos[flip] = exchange(halos[flip], "col", flip)
@@ -286,19 +328,29 @@
     place = jnp.stack([q, me, profile[0]])
     params = pltpu.CompilerParams(vmem_limit_bytes=VMEM_BYTES)
     sizes = [len(flips) * 128 // slabs for flips in CHUNKS]
-    matrix, *lines = pl.pallas_call(
-        functools.partial(prepare_kernel, slabs),
-        out_shape=[jax.ShapeDtypeStruct((256 * len(CHIPS), width), jnp.bfloat16)]
-        + [jax.ShapeDtypeStruct((2 * len(CHIPS) * cells, z_filter.shape[0]), jnp.bfloat16) for cells in sizes],
-        in_specs=[whole(pltpu.SMEM), whole(pl.ANY), whole()],
-        out_specs=[whole()] * (1 + len(CHUNKS)),
+    matrix = pl.pallas_call(
+        x_rows_kernel,
+        out_shape=jax.ShapeDtypeStruct((256 * len(CHIPS), width), jnp.bfloat16),
+        in_specs=[whole(pltpu.SMEM), whole(pl.ANY)],
+        out_specs=whole(),
         scratch_shapes=[pltpu.SemaphoreType.DMA((2 * len(CHIPS),))],
         compiler_params=params,
         cost_estimate=cost("prepare"),
-        name="prepare",
-    )(place, x_filters, z_filter)
-
-    pieces, (matrix, *lines) = advance(velocity, (matrix, *lines))
+        name="x_rows",
+    )(place, x_filters)
+    lines = pl.pallas_call(
+        functools.partial(z_lines_kernel, slabs),
+        out_shape=[
+            jax.ShapeDtypeStruct((2 * len(CHIPS) * cells, z_filter.shape[0]), jnp.bfloat16) for cells in sizes
+        ],
+        in_specs=[whole(pltpu.SMEM), whole()],
+        out_specs=[whole()] * len(CHUNKS),
+        compiler_params=params,
+        cost_estimate=cost("prepare"),
+        name="z_lines",
+    )(place, z_filter)
+
+    pieces, matrix = advance(velocity, matrix)
 
     def x_filter(number, cores, inputs):
         cells = sum(piece.shape[1] for piece in inputs)

time: 72.8 us -> 71.2 us (0.978)
  waiting for transfers between devices: 16.8 us -> 22.5 us
  other arithmetic: 4.32 us -> 0.32 us
  starting transfers between devices: 31.3 us -> 28.1 us
  local copies, waits for them, and re-layouts: 5.92 us -> 5 us
  Pallas kernels: 13.4 us -> 14.2 us
    ppermute x21, waiting for transfers between devices: 15.1 us -> 20.4 us  [exchange(): return lax.ppermute(value, axis, [(i, i ^ flip) for i in range(count)])]
    ppermute x21, starting transfers between devices: 28.6 us -> 25.4 us  [exchange(): return lax.ppermute(value, axis, [(i, i ^ flip) for i in range(count)])]
    select_n x2 -> x1, other arithmetic: 2.54 us -> 0.09 us  [advance(): halos[flip] = jnp.where(outside, outer, halos[flip])]
    another operation x1 -> x0, other arithmetic: 1.58 us -> none  [run(): jax.shard_map(fast_body if suits else body, mesh=mesh, in_specs=placed, o...]
    unnamed x4 -> x7, local copies, waits for them, and re-layouts: 2.19 us -> 3.61 us
    dynamic_slice x1 -> x0, local copies, waits for them, and re-layouts: 1.02 us -> none  [advance(): mains = [lax.dynamic_slice_in_dim(v, rows * q, rows, 1)]]
    pallas_call x1 -> x3, Pallas kernels: 1.51 us -> 2.38 us  [the longest x1 1.27 us: fast_body(): pl.pallas_call(functools.partial(z_lines_kernel, slabs), out_shape=[jax.S...]
  transfers between devices with their start and end apart: 23 -> 23, of which waited for: 12 -> 13; matrix products, arithmetic and copies ran while one was open for 8% -> 1% of each run, Pallas kernels for 8% -> 10%
where the time goes in v4:
time: 71.2 us; the launch traced here: 71 us
  starting transfers between devices  28.1 us (39%)
  waiting for transfers between devices  22.5 us (32%)
  Pallas kernels  14.2 us (20%)
  local copies, waits for them, and re-layouts  5 us (7%)
  between operations  0.86 us (1%)
    ppermute x21, starting transfers between devices, exchange(): return lax.ppermute(value, axis, [(i, i ^ flip) for i in range(count)])  25.4 us
    ppermute x21, waiting for transfers between devices, exchange(): return lax.ppermute(value, axis, [(i, i ^ flip) for i in range(count)])  20.4 us
    pallas_call x1, Pallas kernels, advance(): pl.pallas_call(functools.partial(step_kernel, slabs), out_shape=[jax.Shap...  4.66 us
    unnamed x7, local copies, waits for them, and re-layouts  3.61 us
    pallas_call x3, Pallas kernels, x_filter(): pl.pallas_call(functools.partial(x_kernel, cores), out_shape=[jax.ShapeDt...  3.05 us
    pallas_call x1, Pallas kernels, fast_body(): pl.pallas_call(z_last_kernel, out_shape=jax.ShapeDtypeStruct((len(PRODUCT...  2.71 us
    ppermute x1, starting transfers between devices, advance(): lax.ppermute(tail, PLANE, [(j, (j + 1) % plane) for j in range(plane)])  1.72 us
    pallas_call x1, Pallas kernels, fast_body(): pl.pallas_call(z_first_kernel, out_shape=jax.ShapeDtypeStruct((FIELDS, 12...  1.42 us
  transfers between devices with their start and end apart: 23, of which 13 were waited for; matrix products, arithmetic and copies ran while one was open for 1% of the time, Pallas kernels for 10%

profile of v4, /device:TPU:0, one launch (start us, length us, event | category | flops | bytes accessed | tf_op | source)
XLA Modules:
  0.0 71.0 jit_solution(9243651597804427047)
XLA Ops:
  0.0 1.3 %fusion.2 = (bf16[3,32,1024]{2,1,0:T(8,128)(2,1)S(1)}, bf16[3,32,1024]{2,1,0:T(8,128)(2,1)S(1)}, bf16[3,32,1024]{2,1,0:T(8,128)(2,1)S(1)}) fusion(f32[3,1,128,1024]{3,2,0,1:T(8,128)} %bitcast.9, s32[]{:T(128)S(6)} %select_n.24, s32[]{:T(128)S(6)} %select_n.23, s32[]{:T(128)S(6)} %select_n.22), kind=kLoop, calls=%fused_computation.7 | loop fusion | bytes 1179660 | tf_op jit(solution)/shard_map/convert_element_type | solution.py:213
  1.3 5.1 %collective-permute-start.4 = (bf16[3,32,1024]{2,1,0:T(8,128)(2,1)S(1)}, bf16[3,32,1024]{2,1,0:T(8,128)(2,1)S(1)}, u32[]{:S(2)}, u32[]{:S(2)}) collective-permute-start(bf16[3,32,1024]{2,1,0:T(8,128)(2,1)S(1)} %get-tuple-element.93), channel_id=1, source_target_pairs={{0,3},{1,2},{2,1},{3,0},{4,7},{5,6},{6,5},{7,4},{8,11},{9,10},{10,... | collective-permute-start | bytes 589832 | tf_op jit(solution)/shard_map/ppermute | solution.py:35
  6.4 0.0 collective-permute-start.3
  6.4 0.6 collective-permute-start.2
  7.1 0.0 copy-start.1
  7.1 1.4 %copy-done.1 = f32[3,1,128,1024]{3,2,1,0:T(8,128)S(1)} copy-done((f32[3,1,128,1024]{3,2,1,0:T(8,128)S(1)}, f32[3,1,128,1024]{3,2,1,0:T(8,128)}, u32[]{:S(2)}) %copy-start.1) | copy-done | bytes 1572888
  8.5 0.3 edges.1
  8.8 1.7 %collective-permute-start = (bf16[3,24,128]{2,1,0:T(8,128)(2,1)S(1)}, bf16[3,24,128]{2,1,0:T(8,128)(2,1)S(1)}, u32[]{:S(2)}, u32[]{:S(2)}) collective-permute-start(bf16[3,24,128]{2,1,0:T(8,128)(2,1)S(1)} %get-tuple-element.53), channel_id=1, source_target_pairs={{0,4},{4,8},{8,12},{12,16},{16,20},{20,24},{24,28},{28,0},{1,5},{5... | collective-permute-start | bytes 55304 | tf_op jit(solution)/shard_map/ppermute | solution.py:230
  10.5 1.0 %collective-permute-start.1 = (bf16[3,24,128]{2,1,0:T(8,128)(2,1)S(1)}, bf16[3,24,128]{2,1,0:T(8,128)(2,1)S(1)}, u32[]{:S(2)}, u32[]{:S(2)}) collective-permute-start(bf16[3,24,128]{2,1,0:T(8,128)(2,1)S(1)} %get-tuple-element.54), channel_id=1, source_target_pairs={{4,0},{8,4},{12,8},{16,12},{20,16},{24,20},{28,24},{0,28},{5,1},{9... | collective-permute-start | bytes 55304 | tf_op jit(solution)/shard_map/ppermute | solution.py:231
  12.2 0.8 %collective-permute-done = bf16[3,24,128]{2,1,0:T(8,128)(2,1)S(1)} collective-permute-done((bf16[3,24,128]{2,1,0:T(8,128)(2,1)S(1)}, bf16[3,24,128]{2,1,0:T(8,128)(2,1)S(1)}, u32[]{:S(2)}, u32[]{:S(2)}) %collective-permute-start) | collective-permute-done | bytes 18464 | tf_op jit(solution)/shard_map/ppermute | solution.py:230
  13.0 1.3 %collective-permute-done.1 = bf16[3,24,128]{2,1,0:T(8,128)(2,1)S(1)} collective-permute-done((bf16[3,24,128]{2,1,0:T(8,128)(2,1)S(1)}, bf16[3,24,128]{2,1,0:T(8,128)(2,1)S(1)}, u32[]{:S(2)}, u32[]{:S(2)}) %collective-permute-start.1) | collective-permute-done | bytes 18464 | tf_op jit(solution)/shard_map/ppermute | solution.py:231
  14.3 0.1 broadcast_select_fusion
  14.4 3.7 %collective-permute-start.7 = (bf16[3,48,128]{2,1,0:T(8,128)(2,1)S(1)}, bf16[3,48,128]{2,1,0:T(8,128)(2,1)S(1)}, u32[]{:S(2)}, u32[]{:S(2)}) collective-permute-start(bf16[3,48,128]{2,1,0:T(8,128)(2,1)S(1)} %get-tuple-element.96), channel_id=1, source_target_pairs={{0,3},{1,2},{2,1},{3,0},{4,7},{5,6},{6,5},{7,4},{8,11},{9,10},{10,... | collective-permute-start | bytes 110600 | tf_op jit(solution)/shard_map/ppermute | solution.py:35
  18.1 0.0 collective-permute-start.6
  18.1 1.8 %collective-permute-done.2.refs_1_ = bf16[3,32,1024]{2,1,0:T(8,128)(2,1)S(1)} collective-permute-done((bf16[3,32,1024]{2,1,0:T(8,128)(2,1)S(1)}, bf16[3,32,1024]{2,1,0:T(8,128)(2,1)S(1)}, u32[]{:S(2)}, u32[]{:S(2)}) %collective-permute-start.2) | collective-permute-done | bytes 196640 | tf_op jit(solution)/shard_map/ppermute | solution.py:35
  19.9 2.5 %collective-permute-start.5 = (bf16[3,48,128]{2,1,0:T(8,128)(2,1)S(1)}, bf16[3,48,128]{2,1,0:T(8,128)(2,1)S(1)}, u32[]{:S(2)}, u32[]{:S(2)}) collective-permute-start(bf16[3,48,128]{2,1,0:T(8,128)(2,1)S(1)} %get-tuple-element.58), channel_id=1, source_target_pairs={{0,1},{1,0},{2,3},{3,2},{4,5},{5,4},{6,7},{7,6},{8,9},{9,8},{10,11... | collective-permute-start | bytes 110600 | tf_op jit(solution)/shard_map/ppermute | solution.py:35
  22.4 0.1 pad_add_fusion.place_ref
  22.5 2.2 %copy-done = bf16[2,1024,1024]{2,1,0:T(8,128)(2,1)S(1)} copy-done((bf16[2,1024,1024]{2,1,0:T(8,128)(2,1)S(1)}, bf16[2,1024,1024]{2,1,0:T(8,128)(2,1)}, u32[]{:S(2)}) %copy-start) | copy-done | bytes 4194328
  24.7 0.8 %x_rows.1.matrix = bf16[1024,1024]{1,0:T(8,128)(2,1)S(1)} custom-call(s32[3]{0:T(128)S(1)} %pad_add_fusion.place_ref, bf16[2,1024,1024]{2,1,0:T(8,128)(2,1)S(1)} %copy-done), custom_call_target="tpu_custom_call" | custom-call | bytes 11100000 | tf_op jit(solution)/shard_map/x_rows/pallas_call | solution.py:331
  25.4 0.0 collective-permute-done.7.refs_7_
  25.5 0.9 %collective-permute-done.6.refs_6_ = bf16[3,48,128]{2,1,0:T(8,128)(2,1)S(1)} collective-permute-done((bf16[3,48,128]{2,1,0:T(8,128)(2,1)S(1)}, bf16[3,48,128]{2,1,0:T(8,128)(2,1)S(1)}, u32[]{:S(2)}, u32[]{:S(2)}) %collective-permute-start.6) | collective-permute-done | bytes 36896 | tf_op jit(solution)/shard_map/ppermute | solution.py:35
  26.3 0.0 collective-permute-done.4.refs_3_
  26.3 0.0 collective-permute-done.3.refs_2_
  26.3 0.0 collective-permute-done.5.refs_5_
  26.3 4.7 %advance.1 = (bf16[3,32,1024]{2,1,0:T(8,128)(2,1)S(1)}, bf16[3,32,1024]{2,1,0:T(8,128)(2,1)S(1)}, bf16[3,32,1024]{2,1,0:T(8,128)(2,1)S(1)}, bf16[3,32,1024]{2,1,0:T(8,128)(2,1)S(1)}) custom-call(s32[1]{0:T(128)} %bitcast.q_ref, f32[3,32,1024]{2,1,0:T(8,128)S(1)} %get-tuple-element.62.refs_0_, bf16[3,32,1024]{2,1,0:T(8,128)(2,1)S(1)} %collective-permute-done.2.refs_1_, ...), custom_call_target="tpu_custom_call" | custom-call | bytes 18500000 | tf_op jit(solution)/shard_map/advance/pallas_call | solution.py:245
  31.0 0.2 collective-permute-start.12
  31.3 2.8 %collective-permute-start.13 = (bf16[3,32,1024]{2,1,0:T(8,128)(2,1)S(1)}, bf16[3,32,1024]{2,1,0:T(8,128)(2,1)S(1)}, u32[]{:S(2)}, u32[]{:S(2)}) collective-permute-start(bf16[3,32,1024]{2,1,0:T(8,128)(2,1)S(1)} %get-tuple-element.76), channel_id=1, source_target_pairs={{0,2},{1,3},{2,0},{3,1},{4,6},{5,7},{6,4},{7,5},{8,10},{9,11},{10,... | collective-permute-start | bytes 589832 | tf_op jit(solution)/shard_map/ppermute | solution.py:35
  34.1 0.8 %x_filter_0.1 = (bf16[2,9,32,128]{3,2,1,0:T(8,128)(2,1)S(1)}, bf16[2,9,32,128]{3,2,1,0:T(8,128)(2,1)S(1)}, bf16[2,9,32,128]{3,2,1,0:T(8,128)(2,1)S(1)}, bf16[2,9,32,128]{3,2,1,0:T(8,128)(2,1)S(1)}) custom-call(bf16[1024,1024]{1,0:T(8,128)(2,1)S(1)} %x_rows.1.matrix, bf16[3,32,1024]{2,1,0:T(8,128)(2,1)S(1)} %get-tuple-element.70.refs_0_), custom_call_target="tpu_custom_call" | custom-call | bytes 370000 | tf_op jit(solution)/shard_map/x_filter_0/pallas_call | solution.py:358
  34.9 1.6 %collective-permute-start.8 = (bf16[2,9,32,128]{3,2,1,0:T(8,128)(2,1)S(1)}, bf16[2,9,32,128]{3,2,1,0:T(8,128)(2,1)S(1)}, u32[]{:S(2)}, u32[]{:S(2)}) collective-permute-start(bf16[2,9,32,128]{3,2,1,0:T(8,128)(2,1)S(1)} %get-tuple-element.72), channel_id=1, source_target_pairs={{0,4},{4,0},{8,12},{12,8},{16,20},{20,16},{24,28},{28,24},{1,5},{5... | collective-permute-start | bytes 442376 | tf_op jit(solution)/shard_map/ppermute | solution.py:35
  36.5 1.5 %collective-permute-start.9 = (bf16[2,9,32,128]{3,2,1,0:T(8,128)(2,1)S(1)}, bf16[2,9,32,128]{3,2,1,0:T(8,128)(2,1)S(1)}, u32[]{:S(2)}, u32[]{:S(2)}) collective-permute-start(bf16[2,9,32,128]{3,2,1,0:T(8,128)(2,1)S(1)} %get-tuple-element.73), channel_id=1, source_target_pairs={{0,16},{4,20},{8,24},{12,28},{16,0},{20,4},{24,8},{28,12},{1,17},{... | collective-permute-start | bytes 442376 | tf_op jit(solution)/shard_map/ppermute | solution.py:35
  38.0 0.5 collective-permute-start.10
  38.5 3.1 %collective-permute-done.8.refs_3_ = bf16[2,9,32,128]{3,2,1,0:T(8,128)(2,1)S(1)} collective-permute-done((bf16[2,9,32,128]{3,2,1,0:T(8,128)(2,1)S(1)}, bf16[2,9,32,128]{3,2,1,0:T(8,128)(2,1)S(1)}, u32[]{:S(2)}, u32[]{:S(2)}) %collective-permute-start.8) | collective-permute-done | bytes 147488 | tf_op jit(solution)/shard_map/ppermute | solution.py:35
  41.5 0.6 collective-permute-start.17
  42.2 0.0 collective-permute-done.9.refs_4_
  42.2 1.9 %collective-permute-done.10.refs_5_ = bf16[2,9,32,128]{3,2,1,0:T(8,128)(2,1)S(1)} collective-permute-done((bf16[2,9,32,128]{3,2,1,0:T(8,128)(2,1)S(1)}, bf16[2,9,32,128]{3,2,1,0:T(8,128)(2,1)S(1)}, u32[]{:S(2)}, u32[]{:S(2)}) %collective-permute-start.10) | collective-permute-done | bytes 147488 | tf_op jit(solution)/shard_map/ppermute | solution.py:35
  44.1 0.0 collective-permute-done.12.refs_0_
  44.1 1.1 %collective-permute-done.13.refs_1_ = bf16[3,32,1024]{2,1,0:T(8,128)(2,1)S(1)} collective-permute-done((bf16[3,32,1024]{2,1,0:T(8,128)(2,1)S(1)}, bf16[3,32,1024]{2,1,0:T(8,128)(2,1)S(1)}, u32[]{:S(2)}, u32[]{:S(2)}) %collective-permute-start.13) | collective-permute-done | bytes 196640 | tf_op jit(solution)/shard_map/ppermute | solution.py:35
  45.2 1.4 %x_filter_1.1 = (bf16[2,9,64,128]{3,2,1,0:T(8,128)(2,1)S(1)}, bf16[2,9,64,128]{3,2,1,0:T(8,128)(2,1)S(1)}, bf16[2,9,64,128]{3,2,1,0:T(8,128)(2,1)S(1)}, bf16[2,9,64,128]{3,2,1,0:T(8,128)(2,1)S(1)}) custom-call(bf16[1024,1024]{1,0:T(8,128)(2,1)S(1)} %x_rows.1.matrix, bf16[3,32,1024]{2,1,0:T(8,128)(2,1)S(1)} %collective-permute-done.12.refs_0_, ...), custom_call_target="tpu_custom_call" | custom-call | bytes 370000 | tf_op jit(solution)/shard_map/x_filter_1/pallas_call | solution.py:358
  46.6 0.0 copy-start.2
  46.6 1.6 %collective-permute-start.14 = (bf16[2,9,64,128]{3,2,1,0:T(8,128)(2,1)S(1)}, bf16[2,9,64,128]{3,2,1,0:T(8,128)(2,1)S(1)}, u32[]{:S(2)}, u32[]{:S(2)}) collective-permute-start(bf16[2,9,64,128]{3,2,1,0:T(8,128)(2,1)S(1)} %get-tuple-element.82), channel_id=1, source_target_pairs={{0,4},{4,0},{8,12},{12,8},{16,20},{20,16},{24,28},{28,24},{1,5},{5... | collective-permute-start | bytes 884744 | tf_op jit(solution)/shard_map/ppermute | solution.py:35
  48.3 1.5 %collective-permute-start.15 = (bf16[2,9,64,128]{3,2,1,0:T(8,128)(2,1)S(1)}, bf16[2,9,64,128]{3,2,1,0:T(8,128)(2,1)S(1)}, u32[]{:S(2)}, u32[]{:S(2)}) collective-permute-start(bf16[2,9,64,128]{3,2,1,0:T(8,128)(2,1)S(1)} %get-tuple-element.83), channel_id=1, source_target_pairs={{0,16},{4,20},{8,24},{12,28},{16,0},{20,4},{24,8},{28,12},{1,17},{... | collective-permute-start | bytes 884744 | tf_op jit(solution)/shard_map/ppermute | solution.py:35
  49.7 0.5 collective-permute-start.16
  50.2 0.1 collective-permute-start.11
  50.3 0.0 collective-permute-done.17.refs_0_
  50.3 0.5 collective-permute-start.18
  50.8 1.3 %collective-permute-done.18.refs_1_ = bf16[3,32,1024]{2,1,0:T(8,128)(2,1)S(1)} collective-permute-done((bf16[3,32,1024]{2,1,0:T(8,128)(2,1)S(1)}, bf16[3,32,1024]{2,1,0:T(8,128)(2,1)S(1)}, u32[]{:S(2)}, u32[]{:S(2)}) %collective-permute-start.18) | collective-permute-done | bytes 196640 | tf_op jit(solution)/shard_map/ppermute | solution.py:35
  52.2 0.8 %x_filter_2.1 = (bf16[1,9,64,128]{3,2,1,0:T(8,128)(2,1)S(1)}, bf16[1,9,64,128]{3,2,1,0:T(8,128)(2,1)S(1)}, bf16[1,9,64,128]{3,2,1,0:T(8,128)(2,1)S(1)}, bf16[1,9,64,128]{3,2,1,0:T(8,128)(2,1)S(1)}) custom-call(bf16[1024,1024]{1,0:T(8,128)(2,1)S(1)} %x_rows.1.matrix, bf16[3,32,1024]{2,1,0:T(8,128)(2,1)S(1)} %collective-permute-done.17.refs_0_, ...), custom_call_target="tpu_custom_call" | custom-call | bytes 370000 | tf_op jit(solution)/shard_map/x_filter_2/pallas_call | solution.py:358
  53.0 1.6 %collective-permute-start.19 = (bf16[1,9,64,128]{3,2,1,0:T(8,128)(2,1)S(1)}, bf16[1,9,64,128]{3,2,1,0:T(8,128)(2,1)S(1)}, u32[]{:S(2)}, u32[]{:S(2)}) collective-permute-start(bf16[1,9,64,128]{3,2,1,0:T(8,128)(2,1)S(1)} %get-tuple-element.87), channel_id=1, source_target_pairs={{0,4},{4,0},{8,12},{12,8},{16,20},{20,16},{24,28},{28,24},{1,5},{5... | collective-permute-start | bytes 442376 | tf_op jit(solution)/shard_map/ppermute | solution.py:35
  54.6 3.5 %collective-permute-done.14.refs_8_ = bf16[2,9,64,128]{3,2,1,0:T(8,128)(2,1)S(1)} collective-permute-done((bf16[2,9,64,128]{3,2,1,0:T(8,128)(2,1)S(1)}, bf16[2,9,64,128]{3,2,1,0:T(8,128)(2,1)S(1)}, u32[]{:S(2)}, u32[]{:S(2)}) %collective-permute-start.14) | collective-permute-done | bytes 294944 | tf_op jit(solution)/shard_map/ppermute | solution.py:35
  58.1 0.0 collective-permute-start.20
  58.2 0.0 collective-permute-done.15.refs_9_
  58.2 0.5 collective-permute-start.21
  58.7 0.0 copy-done.2
  58.7 1.3 %z_lines.1 = (bf16[256,1024]{1,0:T(8,128)(2,1)S(1)}, bf16[512,1024]{1,0:T(8,128)(2,1)S(1)}, bf16[256,1024]{1,0:T(8,128)(2,1)S(1)}) custom-call(s32[3]{0:T(128)S(1)} %pad_add_fusion.place_ref, bf16[1024,1024]{1,0:T(8,128)(2,1)S(1)} %copy-done.2), custom_call_target="tpu_custom_call" | custom-call | bytes 11100000 | tf_op jit(solution)/shard_map/z_lines/pallas_call | solution.py:341
  60.0 2.9 %collective-permute-done.16.refs_10_ = bf16[2,9,64,128]{3,2,1,0:T(8,128)(2,1)S(1)} collective-permute-done((bf16[2,9,64,128]{3,2,1,0:T(8,128)(2,1)S(1)}, bf16[2,9,64,128]{3,2,1,0:T(8,128)(2,1)S(1)}, u32[]{:S(2)}, u32[]{:S(2)}) %collective-permute-start.16) | collective-permute-done | bytes 294944 | tf_op jit(solution)/shard_map/ppermute | solution.py:35
  62.9 0.0 collective-permute-done.11.refs_6_
  62.9 1.4 %z_filter_first.1.passed = f32[9,128,1024]{2,1,0:T(8,128)S(1)} custom-call(bf16[256,1024]{1,0:T(8,128)(2,1)S(1)} %get-tuple-element.49.refs_0_, bf16[512,1024]{1,0:T(8,128)(2,1)S(1)} %get-tuple-element.50.refs_1_.line_second, bf16[2,9,32,128]{3,2,1,0:T(8,128)(2,1)S(1)} %get-tuple-element.71.refs_2_, ...), custom_call_target="tpu_custom_call" | custom-call | bytes 370000 | tf_op jit(solution)/shard_map/z_filter_first/pallas_call | solution.py:386
  64.3 0.1 pad_maximum_fusion
  64.4 0.1 collective-permute-done.19.refs_1_
  64.5 0.0 collective-permute-done.20.refs_2_
  64.5 1.8 %collective-permute-done.21.refs_3_ = bf16[1,9,64,128]{3,2,1,0:T(8,128)(2,1)S(1)} collective-permute-done((bf16[1,9,64,128]{3,2,1,0:T(8,128)(2,1)S(1)}, bf16[1,9,64,128]{3,2,1,0:T(8,128)(2,1)S(1)}, u32[]{:S(2)}, u32[]{:S(2)}) %collective-permute-start.21) | collective-permute-done | bytes 147488 | tf_op jit(solution)/shard_map/ppermute | solution.py:35
  66.3 0.0 collective-permute-start.22
  66.3 2.0 %collective-permute-done.22.others = bf16[4,9,64,128]{3,2,1,0:T(8,128)(2,1)S(1)} collective-permute-done((bf16[4,9,64,128]{3,2,1,0:T(8,128)(2,1)S(1)}, bf16[4,9,64,128]{3,2,1,0:T(8,128)(2,1)S(1)}, u32[]{:S(2)}, u32[]{:S(2)}) %collective-permute-start.22) | collective-permute-done | bytes 589856 | tf_op jit(solution)/shard_map/ppermute | solution.py:35
  68.3 2.7 %z_filter_last.1 = f32[6,1,128,1024]{3,2,1,0:T(8,128)} custom-call(f32[9,128,1024]{2,1,0:T(8,128)S(1)} %z_filter_first.1.passed, bf16[512,1024]{1,0:T(8,128)(2,1)S(1)} %get-tuple-element.50.refs_1_.line_second, bf16[256,1024]{1,0:T(8,128)(2,1)S(1)} %get-tuple-element.85.line_last, bf16[4,9,64,128]{3,2,1,0:T(8,128)(2,1)S(1)} %collective-permute-done.22.others, ...), custom_call_target="tpu_custom_call" | custom-call | bytes 370000 | tf_op jit(solution)/shard_map/z_filter_last/pallas_call | solution.py:396
  (15 shorter events, 0.2 us)
Async XLA Ops:
  1.3 25.0 %collective-permute-start.4 = (bf16[3,32,1024]{2,1,0:T(8,128)(2,1)S(1)}, bf16[3,32,1024]{2,1,0:T(8,128)(2,1)S(1)}, u32[]{:S(2)}, u32[]{:S(2)}) collective-permute-start(bf16[3,32,1024]{2,1,0:T(8,128)(2,1)S(1)} %get-tuple-element.93), channel_id=1, source_target_pairs={{0,3},{1,2},{2,1},{3,0},{4,7},{5,6},{6,5},{7,4},{8,11},{9,10},{10,... | collective-permute-start | bytes 589832 | tf_op jit(solution)/shard_map/ppermute | solution.py:35
  6.4 19.9 %collective-permute-start.3 = (bf16[3,32,1024]{2,1,0:T(8,128)(2,1)S(1)}, bf16[3,32,1024]{2,1,0:T(8,128)(2,1)S(1)}, u32[]{:S(2)}, u32[]{:S(2)}) collective-permute-start(bf16[3,32,1024]{2,1,0:T(8,128)(2,1)S(1)} %get-tuple-element.94), channel_id=1, source_target_pairs={{0,2},{1,3},{2,0},{3,1},{4,6},{5,7},{6,4},{7,5},{8,10},{9,11},{10,... | collective-permute-start | bytes 589832 | tf_op jit(solution)/shard_map/ppermute | solution.py:35
  6.4 13.5 %collective-permute-start.2 = (bf16[3,32,1024]{2,1,0:T(8,128)(2,1)S(1)}, bf16[3,32,1024]{2,1,0:T(8,128)(2,1)S(1)}, u32[]{:S(2)}, u32[]{:S(2)}) collective-permute-start(bf16[3,32,1024]{2,1,0:T(8,128)(2,1)S(1)} %get-tuple-element.95), channel_id=1, source_target_pairs={{0,1},{1,0},{2,3},{3,2},{4,5},{5,4},{6,7},{7,6},{8,9},{9,8},{10,11... | collective-permute-start | bytes 589832 | tf_op jit(solution)/shard_map/ppermute | solution.py:35
  7.1 1.4 %copy-start.1 = (f32[3,1,128,1024]{3,2,1,0:T(8,128)S(1)}, f32[3,1,128,1024]{3,2,1,0:T(8,128)}, u32[]{:S(2)}) copy-start(f32[3,1,128,1024]{3,2,1,0:T(8,128)} %velocity.1) | copy-start | bytes 4718596
  8.8 4.1 %collective-permute-start = (bf16[3,24,128]{2,1,0:T(8,128)(2,1)S(1)}, bf16[3,24,128]{2,1,0:T(8,128)(2,1)S(1)}, u32[]{:S(2)}, u32[]{:S(2)}) collective-permute-start(bf16[3,24,128]{2,1,0:T(8,128)(2,1)S(1)} %get-tuple-element.53), channel_id=1, source_target_pairs={{0,4},{4,8},{8,12},{12,16},{16,20},{20,24},{24,28},{28,0},{1,5},{5... | collective-permute-start | bytes 55304 | tf_op jit(solution)/shard_map/ppermute | solution.py:230
  10.5 3.8 %collective-permute-start.1 = (bf16[3,24,128]{2,1,0:T(8,128)(2,1)S(1)}, bf16[3,24,128]{2,1,0:T(8,128)(2,1)S(1)}, u32[]{:S(2)}, u32[]{:S(2)}) collective-permute-start(bf16[3,24,128]{2,1,0:T(8,128)(2,1)S(1)} %get-tuple-element.54), channel_id=1, source_target_pairs={{4,0},{8,4},{12,8},{16,12},{20,16},{24,20},{28,24},{0,28},{5,1},{9... | collective-permute-start | bytes 55304 | tf_op jit(solution)/shard_map/ppermute | solution.py:231
  14.4 11.0 %collective-permute-start.7 = (bf16[3,48,128]{2,1,0:T(8,128)(2,1)S(1)}, bf16[3,48,128]{2,1,0:T(8,128)(2,1)S(1)}, u32[]{:S(2)}, u32[]{:S(2)}) collective-permute-start(bf16[3,48,128]{2,1,0:T(8,128)(2,1)S(1)} %get-tuple-element.96), channel_id=1, source_target_pairs={{0,3},{1,2},{2,1},{3,0},{4,7},{5,6},{6,5},{7,4},{8,11},{9,10},{10,... | collective-permute-start | bytes 110600 | tf_op jit(solution)/shard_map/ppermute | solution.py:35
  18.1 8.3 %collective-permute-start.6 = (bf16[3,48,128]{2,1,0:T(8,128)(2,1)S(1)}, bf16[3,48,128]{2,1,0:T(8,128)(2,1)S(1)}, u32[]{:S(2)}, u32[]{:S(2)}) collective-permute-start(bf16[3,48,128]{2,1,0:T(8,128)(2,1)S(1)} %get-tuple-element.97), channel_id=1, source_target_pairs={{0,2},{1,3},{2,0},{3,1},{4,6},{5,7},{6,4},{7,5},{8,10},{9,11},{10,... | collective-permute-start | bytes 110600 | tf_op jit(solution)/shard_map/ppermute | solution.py:35
  19.9 6.4 %collective-permute-start.5 = (bf16[3,48,128]{2,1,0:T(8,128)(2,1)S(1)}, bf16[3,48,128]{2,1,0:T(8,128)(2,1)S(1)}, u32[]{:S(2)}, u32[]{:S(2)}) collective-permute-start(bf16[3,48,128]{2,1,0:T(8,128)(2,1)S(1)} %get-tuple-element.58), channel_id=1, source_target_pairs={{0,1},{1,0},{2,3},{3,2},{4,5},{5,4},{6,7},{7,6},{8,9},{9,8},{10,11... | collective-permute-start | bytes 110600 | tf_op jit(solution)/shard_map/ppermute | solution.py:35
  22.5 2.2 %copy-start = (bf16[2,1024,1024]{2,1,0:T(8,128)(2,1)S(1)}, bf16[2,1024,1024]{2,1,0:T(8,128)(2,1)}, u32[]{:S(2)}) copy-start(bf16[2,1024,1024]{2,1,0:T(8,128)(2,1)} %x_filters.1) | copy-start | bytes 12582916
  31.0 13.0 %collective-permute-start.12 = (bf16[3,32,1024]{2,1,0:T(8,128)(2,1)S(1)}, bf16[3,32,1024]{2,1,0:T(8,128)(2,1)S(1)}, u32[]{:S(2)}, u32[]{:S(2)}) collective-permute-start(bf16[3,32,1024]{2,1,0:T(8,128)(2,1)S(1)} %get-tuple-element.75), channel_id=1, source_target_pairs={{0,1},{1,0},{2,3},{3,2},{4,5},{5,4},{6,7},{7,6},{8,9},{9,8},{10,11... | collective-permute-start | bytes 589832 | tf_op jit(solution)/shard_map/ppermute | solution.py:35
  31.3 13.9 %collective-permute-start.13 = (bf16[3,32,1024]{2,1,0:T(8,128)(2,1)S(1)}, bf16[3,32,1024]{2,1,0:T(8,128)(2,1)S(1)}, u32[]{:S(2)}, u32[]{:S(2)}) collective-permute-start(bf16[3,32,1024]{2,1,0:T(8,128)(2,1)S(1)} %get-tuple-element.76), channel_id=1, source_target_pairs={{0,2},{1,3},{2,0},{3,1},{4,6},{5,7},{6,4},{7,5},{8,10},{9,11},{10,... | collective-permute-start | bytes 589832 | tf_op jit(solution)/shard_map/ppermute | solution.py:35
  34.9 6.6 %collective-permute-start.8 = (bf16[2,9,32,128]{3,2,1,0:T(8,128)(2,1)S(1)}, bf16[2,9,32,128]{3,2,1,0:T(8,128)(2,1)S(1)}, u32[]{:S(2)}, u32[]{:S(2)}) collective-permute-start(bf16[2,9,32,128]{3,2,1,0:T(8,128)(2,1)S(1)} %get-tuple-element.72), channel_id=1, source_target_pairs={{0,4},{4,0},{8,12},{12,8},{16,20},{20,16},{24,28},{28,24},{1,5},{5... | collective-permute-start | bytes 442376 | tf_op jit(solution)/shard_map/ppermute | solution.py:35
  36.5 5.7 %collective-permute-start.9 = (bf16[2,9,32,128]{3,2,1,0:T(8,128)(2,1)S(1)}, bf16[2,9,32,128]{3,2,1,0:T(8,128)(2,1)S(1)}, u32[]{:S(2)}, u32[]{:S(2)}) collective-permute-start(bf16[2,9,32,128]{3,2,1,0:T(8,128)(2,1)S(1)} %get-tuple-element.73), channel_id=1, source_target_pairs={{0,16},{4,20},{8,24},{12,28},{16,0},{20,4},{24,8},{28,12},{1,17},{... | collective-permute-start | bytes 442376 | tf_op jit(solution)/shard_map/ppermute | solution.py:35
  38.0 6.1 %collective-permute-start.10 = (bf16[2,9,32,128]{3,2,1,0:T(8,128)(2,1)S(1)}, bf16[2,9,32,128]{3,2,1,0:T(8,128)(2,1)S(1)}, u32[]{:S(2)}, u32[]{:S(2)}) collective-permute-start(bf16[2,9,32,128]{3,2,1,0:T(8,128)(2,1)S(1)} %get-tuple-element.74), channel_id=1, source_target_pairs={{0,20},{4,16},{8,28},{12,24},{16,4},{20,0},{24,12},{28,8},{1,21},{... | collective-permute-start | bytes 442376 | tf_op jit(solution)/shard_map/ppermute | solution.py:35
  41.5 8.8 %collective-permute-start.17 = (bf16[3,32,1024]{2,1,0:T(8,128)(2,1)S(1)}, bf16[3,32,1024]{2,1,0:T(8,128)(2,1)S(1)}, u32[]{:S(2)}, u32[]{:S(2)}) collective-permute-start(bf16[3,32,1024]{2,1,0:T(8,128)(2,1)S(1)} %get-tuple-element.86), channel_id=1, source_target_pairs={{0,3},{1,2},{2,1},{3,0},{4,7},{5,6},{6,5},{7,4},{8,11},{9,10},{10,... | collective-permute-start | bytes 589832 | tf_op jit(solution)/shard_map/ppermute | solution.py:35
  46.6 12.0 %copy-start.2 = (bf16[1024,1024]{1,0:T(8,128)(2,1)S(1)}, bf16[1024,1024]{1,0:T(8,128)(2,1)}, u32[]{:S(2)}) copy-start(bf16[1024,1024]{1,0:T(8,128)(2,1)} %z_filter.1) | copy-start | bytes 6291460
  46.6 11.5 %collective-permute-start.14 = (bf16[2,9,64,128]{3,2,1,0:T(8,128)(2,1)S(1)}, bf16[2,9,64,128]{3,2,1,0:T(8,128)(2,1)S(1)}, u32[]{:S(2)}, u32[]{:S(2)}) collective-permute-start(bf16[2,9,64,128]{3,2,1,0:T(8,128)(2,1)S(1)} %get-tuple-element.82), channel_id=1, source_target_pairs={{0,4},{4,0},{8,12},{12,8},{16,20},{20,16},{24,28},{28,24},{1,5},{5... | collective-permute-start | bytes 884744 | tf_op jit(solution)/shard_map/ppermute | solution.py:35
  48.3 9.9 %collective-permute-start.15 = (bf16[2,9,64,128]{3,2,1,0:T(8,128)(2,1)S(1)}, bf16[2,9,64,128]{3,2,1,0:T(8,128)(2,1)S(1)}, u32[]{:S(2)}, u32[]{:S(2)}) collective-permute-start(bf16[2,9,64,128]{3,2,1,0:T(8,128)(2,1)S(1)} %get-tuple-element.83), channel_id=1, source_target_pairs={{0,16},{4,20},{8,24},{12,28},{16,0},{20,4},{24,8},{28,12},{1,17},{... | collective-permute-start | bytes 884744 | tf_op jit(solution)/shard_map/ppermute | solution.py:35
  49.7 13.1 %collective-permute-start.16 = (bf16[2,9,64,128]{3,2,1,0:T(8,128)(2,1)S(1)}, bf16[2,9,64,128]{3,2,1,0:T(8,128)(2,1)S(1)}, u32[]{:S(2)}, u32[]{:S(2)}) collective-permute-start(bf16[2,9,64,128]{3,2,1,0:T(8,128)(2,1)S(1)} %get-tuple-element.84), channel_id=1, source_target_pairs={{0,20},{4,16},{8,28},{12,24},{16,4},{20,0},{24,12},{28,8},{1,21},{... | collective-permute-start | bytes 884744 | tf_op jit(solution)/shard_map/ppermute | solution.py:35
  50.2 12.7 %collective-permute-start.11 = (bf16[4,9,32,128]{3,2,1,0:T(8,128)(2,1)S(1)}, bf16[4,9,32,128]{3,2,1,0:T(8,128)(2,1)S(1)}, u32[]{:S(2)}, u32[]{:S(2)}) collective-permute-start(bf16[4,9,32,128]{3,2,1,0:T(8,128)(2,1)S(1)} %pad_maximum_fusion.1), channel_id=1, source_target_pairs={{0,8},{8,0},{16,24},{24,16},{1,9},{9,1},{17,25},{25,17},{2,10},{10... | collective-permute-start | bytes 884744 | tf_op jit(solution)/shard_map/ppermute | solution.py:35
  50.3 1.8 %collective-permute-start.18 = (bf16[3,32,1024]{2,1,0:T(8,128)(2,1)S(1)}, bf16[3,32,1024]{2,1,0:T(8,128)(2,1)S(1)}, u32[]{:S(2)}, u32[]{:S(2)}) collective-permute-start(bf16[3,32,1024]{2,1,0:T(8,128)(2,1)S(1)} %collective-permute-done.17.refs_0_), channel_id=1, source_target_pairs={{0,8},{8,0},{16,24},{24,16},{1,9},{9,1},{17,25},{25,17},{2,10},{10... | collective-permute-start | bytes 589832 | tf_op jit(solution)/shard_map/ppermute | solution.py:35
  53.0 11.5 %collective-permute-start.19 = (bf16[1,9,64,128]{3,2,1,0:T(8,128)(2,1)S(1)}, bf16[1,9,64,128]{3,2,1,0:T(8,128)(2,1)S(1)}, u32[]{:S(2)}, u32[]{:S(2)}) collective-permute-start(bf16[1,9,64,128]{3,2,1,0:T(8,128)(2,1)S(1)} %get-tuple-element.87), channel_id=1, source_target_pairs={{0,4},{4,0},{8,12},{12,8},{16,20},{20,16},{24,28},{28,24},{1,5},{5... | collective-permute-start | bytes 442376 | tf_op jit(solution)/shard_map/ppermute | solution.py:35
  58.1 6.3 %collective-permute-start.20 = (bf16[1,9,64,128]{3,2,1,0:T(8,128)(2,1)S(1)}, bf16[1,9,64,128]{3,2,1,0:T(8,128)(2,1)S(1)}, u32[]{:S(2)}, u32[]{:S(2)}) collective-permute-start(bf16[1,9,64,128]{3,2,1,0:T(8,128)(2,1)S(1)} %get-tuple-element.88), channel_id=1, source_target_pairs={{0,16},{4,20},{8,24},{12,28},{16,0},{20,4},{24,8},{28,12},{1,17},{... | collective-permute-start | bytes 442376 | tf_op jit(solution)/shard_map/ppermute | solution.py:35
  58.2 8.1 %collective-permute-start.21 = (bf16[1,9,64,128]{3,2,1,0:T(8,128)(2,1)S(1)}, bf16[1,9,64,128]{3,2,1,0:T(8,128)(2,1)S(1)}, u32[]{:S(2)}, u32[]{:S(2)}) collective-permute-start(bf16[1,9,64,128]{3,2,1,0:T(8,128)(2,1)S(1)} %get-tuple-element.90), channel_id=1, source_target_pairs={{0,20},{4,16},{8,28},{12,24},{16,4},{20,0},{24,12},{28,8},{1,21},{... | collective-permute-start | bytes 442376 | tf_op jit(solution)/shard_map/ppermute | solution.py:35
  66.3 2.0 %collective-permute-start.22 = (bf16[4,9,64,128]{3,2,1,0:T(8,128)(2,1)S(1)}, bf16[4,9,64,128]{3,2,1,0:T(8,128)(2,1)S(1)}, u32[]{:S(2)}, u32[]{:S(2)}) collective-permute-start(bf16[4,9,64,128]{3,2,1,0:T(8,128)(2,1)S(1)} %pad_maximum_fusion), channel_id=1, source_target_pairs={{0,8},{8,0},{16,24},{24,16},{1,9},{9,1},{17,25},{25,17},{2,10},{10... | collective-permute-start | bytes 1769480 | tf_op jit(solution)/shard_map/ppermute | solution.py:35

commit v5 on v4

--- a/solution.py
+++ b/solution.py
@@ -102,11 +102,11 @@
         own[comp] = cells[comp, pl.ds(pl.multiple_of(rows * q, rows), rows)]
         lay(comp, block - HALO, 0)
         tail[comp] = line[: 8 * REACH].astype(WIRE)
-        head[comp] = line[8 * REACH :].astype(WIRE)
+        head[comp] = line[8 * REACH : 16 * REACH].astype(WIRE)
         for flip in range(slabs):
             at = rows * (q ^ flip)
             lay(comp, jnp.maximum(at - HALO, 0), jnp.minimum(at + rows, block - HALO))
-            halos[flip][comp] = line[...].astype(WIRE)
+            halos[flip][comp] = line[: 16 * REACH].astype(WIRE)
 
 
 def step_kernel(slabs, q_ref, *refs):
@@ -220,7 +220,7 @@
         out_specs=[whole()] * (3 + slabs),
         scratch_shapes=[
             pltpu.VMEM((3, block, width), v.dtype),
-            pltpu.VMEM((16 * REACH, width // 8), v.dtype),
+            pltpu.VMEM((16 * REACH + 64, width // 8), v.dtype),
             pltpu.SemaphoreType.DMA((3,)),
         ],
         compiler_params=pltpu.CompilerParams(vmem_limit_bytes=VMEM_BYTES),

time: 71.2 us -> 71.2 us (level)
  no operation moved by 1% of the time
where the time goes in v5:
time: 71.2 us; the launch traced here: 71 us
  starting transfers between devices  28.1 us (39%)
  waiting for transfers between devices  22.5 us (32%)
  Pallas kernels  14.2 us (20%)
  local copies, waits for them, and re-layouts  5 us (7%)
  between operations  0.86 us (1%)
    ppermute x21, starting transfers between devices, exchange(): return lax.ppermute(value, axis, [(i, i ^ flip) for i in range(count)])  25.4 us
    ppermute x21, waiting for transfers between devices, exchange(): return lax.ppermute(value, axis, [(i, i ^ flip) for i in range(count)])  20.4 us
    pallas_call x1, Pallas kernels, advance(): pl.pallas_call(functools.partial(step_kernel, slabs), out_shape=[jax.Shap...  4.66 us
    unnamed x7, local copies, waits for them, and re-layouts  3.61 us
    pallas_call x3, Pallas kernels, x_filter(): pl.pallas_call(functools.partial(x_kernel, cores), out_shape=[jax.ShapeDt...  3.05 us
    pallas_call x1, Pallas kernels, fast_body(): pl.pallas_call(z_last_kernel, out_shape=jax.ShapeDtypeStruct((len(PRODUCT...  2.71 us
    ppermute x1, starting transfers between devices, advance(): lax.ppermute(tail, PLANE, [(j, (j + 1) % plane) for j in range(plane)])  1.72 us
    pallas_call x1, Pallas kernels, fast_body(): pl.pallas_call(z_first_kernel, out_shape=jax.ShapeDtypeStruct((FIELDS, 12...  1.42 us
  transfers between devices with their start and end apart: 23, of which 13 were waited for; matrix products, arithmetic and copies ran while one was open for 1% of the time, Pallas kernels for 10%

profile of v5, /device:TPU:0, one launch (start us, length us, event | category | flops | bytes accessed | tf_op | source)
XLA Modules:
  0.0 71.0 jit_solution(9243651597804427047)
XLA Ops:
  0.0 1.3 %fusion.2 = (bf16[3,32,1024]{2,1,0:T(8,128)(2,1)S(1)}, bf16[3,32,1024]{2,1,0:T(8,128)(2,1)S(1)}, bf16[3,32,1024]{2,1,0:T(8,128)(2,1)S(1)}) fusion(f32[3,1,128,1024]{3,2,0,1:T(8,128)} %bitcast.9, s32[]{:T(128)S(6)} %select_n.24, s32[]{:T(128)S(6)} %select_n.23, s32[]{:T(128)S(6)} %select_n.22), kind=kLoop, calls=%fused_computation.7 | loop fusion | bytes 1179660 | tf_op jit(solution)/shard_map/convert_element_type | solution.py:213
  1.3 5.1 %collective-permute-start.4 = (bf16[3,32,1024]{2,1,0:T(8,128)(2,1)S(1)}, bf16[3,32,1024]{2,1,0:T(8,128)(2,1)S(1)}, u32[]{:S(2)}, u32[]{:S(2)}) collective-permute-start(bf16[3,32,1024]{2,1,0:T(8,128)(2,1)S(1)} %get-tuple-element.93), channel_id=1, source_target_pairs={{0,3},{1,2},{2,1},{3,0},{4,7},{5,6},{6,5},{7,4},{8,11},{9,10},{10,... | collective-permute-start | bytes 589832 | tf_op jit(solution)/shard_map/ppermute | solution.py:35
  6.4 0.0 collective-permute-start.3
  6.4 0.6 collective-permute-start.2
  7.1 0.0 copy-start.1
  7.1 1.4 %copy-done.1 = f32[3,1,128,1024]{3,2,1,0:T(8,128)S(1)} copy-done((f32[3,1,128,1024]{3,2,1,0:T(8,128)S(1)}, f32[3,1,128,1024]{3,2,1,0:T(8,128)}, u32[]{:S(2)}) %copy-start.1) | copy-done | bytes 1572888
  8.5 0.3 edges.1
  8.8 1.7 %collective-permute-start = (bf16[3,24,128]{2,1,0:T(8,128)(2,1)S(1)}, bf16[3,24,128]{2,1,0:T(8,128)(2,1)S(1)}, u32[]{:S(2)}, u32[]{:S(2)}) collective-permute-start(bf16[3,24,128]{2,1,0:T(8,128)(2,1)S(1)} %get-tuple-element.53), channel_id=1, source_target_pairs={{0,4},{4,8},{8,12},{12,16},{16,20},{20,24},{24,28},{28,0},{1,5},{5... | collective-permute-start | bytes 55304 | tf_op jit(solution)/shard_map/ppermute | solution.py:230
  10.5 1.0 %collective-permute-start.1 = (bf16[3,24,128]{2,1,0:T(8,128)(2,1)S(1)}, bf16[3,24,128]{2,1,0:T(8,128)(2,1)S(1)}, u32[]{:S(2)}, u32[]{:S(2)}) collective-permute-start(bf16[3,24,128]{2,1,0:T(8,128)(2,1)S(1)} %get-tuple-element.54), channel_id=1, source_target_pairs={{4,0},{8,4},{12,8},{16,12},{20,16},{24,20},{28,24},{0,28},{5,1},{9... | collective-permute-start | bytes 55304 | tf_op jit(solution)/shard_map/ppermute | solution.py:231
  12.2 0.8 %collective-permute-done = bf16[3,24,128]{2,1,0:T(8,128)(2,1)S(1)} collective-permute-done((bf16[3,24,128]{2,1,0:T(8,128)(2,1)S(1)}, bf16[3,24,128]{2,1,0:T(8,128)(2,1)S(1)}, u32[]{:S(2)}, u32[]{:S(2)}) %collective-permute-start) | collective-permute-done | bytes 18464 | tf_op jit(solution)/shard_map/ppermute | solution.py:230
  13.0 1.3 %collective-permute-done.1 = bf16[3,24,128]{2,1,0:T(8,128)(2,1)S(1)} collective-permute-done((bf16[3,24,128]{2,1,0:T(8,128)(2,1)S(1)}, bf16[3,24,128]{2,1,0:T(8,128)(2,1)S(1)}, u32[]{:S(2)}, u32[]{:S(2)}) %collective-permute-start.1) | collective-permute-done | bytes 18464 | tf_op jit(solution)/shard_map/ppermute | solution.py:231
  14.3 0.1 broadcast_select_fusion
  14.4 3.7 %collective-permute-start.7 = (bf16[3,48,128]{2,1,0:T(8,128)(2,1)S(1)}, bf16[3,48,128]{2,1,0:T(8,128)(2,1)S(1)}, u32[]{:S(2)}, u32[]{:S(2)}) collective-permute-start(bf16[3,48,128]{2,1,0:T(8,128)(2,1)S(1)} %get-tuple-element.96), channel_id=1, source_target_pairs={{0,3},{1,2},{2,1},{3,0},{4,7},{5,6},{6,5},{7,4},{8,11},{9,10},{10,... | collective-permute-start | bytes 110600 | tf_op jit(solution)/shard_map/ppermute | solution.py:35
  18.1 0.0 collective-permute-start.6
  18.1 1.8 %collective-permute-done.2.refs_1_ = bf16[3,32,1024]{2,1,0:T(8,128)(2,1)S(1)} collective-permute-done((bf16[3,32,1024]{2,1,0:T(8,128)(2,1)S(1)}, bf16[3,32,1024]{2,1,0:T(8,128)(2,1)S(1)}, u32[]{:S(2)}, u32[]{:S(2)}) %collective-permute-start.2) | collective-permute-done | bytes 196640 | tf_op jit(solution)/shard_map/ppermute | solution.py:35
  19.9 2.5 %collective-permute-start.5 = (bf16[3,48,128]{2,1,0:T(8,128)(2,1)S(1)}, bf16[3,48,128]{2,1,0:T(8,128)(2,1)S(1)}, u32[]{:S(2)}, u32[]{:S(2)}) collective-permute-start(bf16[3,48,128]{2,1,0:T(8,128)(2,1)S(1)} %get-tuple-element.58), channel_id=1, source_target_pairs={{0,1},{1,0},{2,3},{3,2},{4,5},{5,4},{6,7},{7,6},{8,9},{9,8},{10,11... | collective-permute-start | bytes 110600 | tf_op jit(solution)/shard_map/ppermute | solution.py:35
  22.4 0.1 pad_add_fusion.place_ref
  22.5 2.2 %copy-done = bf16[2,1024,1024]{2,1,0:T(8,128)(2,1)S(1)} copy-done((bf16[2,1024,1024]{2,1,0:T(8,128)(2,1)S(1)}, bf16[2,1024,1024]{2,1,0:T(8,128)(2,1)}, u32[]{:S(2)}) %copy-start) | copy-done | bytes 4194328
  24.7 0.8 %x_rows.1.matrix = bf16[1024,1024]{1,0:T(8,128)(2,1)S(1)} custom-call(s32[3]{0:T(128)S(1)} %pad_add_fusion.place_ref, bf16[2,1024,1024]{2,1,0:T(8,128)(2,1)S(1)} %copy-done), custom_call_target="tpu_custom_call" | custom-call | bytes 11100000 | tf_op jit(solution)/shard_map/x_rows/pallas_call | solution.py:331
  25.4 0.0 collective-permute-done.7.refs_7_
  25.5 0.9 %collective-permute-done.6.refs_6_ = bf16[3,48,128]{2,1,0:T(8,128)(2,1)S(1)} collective-permute-done((bf16[3,48,128]{2,1,0:T(8,128)(2,1)S(1)}, bf16[3,48,128]{2,1,0:T(8,128)(2,1)S(1)}, u32[]{:S(2)}, u32[]{:S(2)}) %collective-permute-start.6) | collective-permute-done | bytes 36896 | tf_op jit(solution)/shard_map/ppermute | solution.py:35
  26.3 0.0 collective-permute-done.4.refs_3_
  26.3 0.0 collective-permute-done.3.refs_2_
  26.3 0.0 collective-permute-done.5.refs_5_
  26.3 4.7 %advance.1 = (bf16[3,32,1024]{2,1,0:T(8,128)(2,1)S(1)}, bf16[3,32,1024]{2,1,0:T(8,128)(2,1)S(1)}, bf16[3,32,1024]{2,1,0:T(8,128)(2,1)S(1)}, bf16[3,32,1024]{2,1,0:T(8,128)(2,1)S(1)}) custom-call(s32[1]{0:T(128)} %bitcast.q_ref, f32[3,32,1024]{2,1,0:T(8,128)S(1)} %get-tuple-element.62.refs_0_, bf16[3,32,1024]{2,1,0:T(8,128)(2,1)S(1)} %collective-permute-done.2.refs_1_, ...), custom_call_target="tpu_custom_call" | custom-call | bytes 18500000 | tf_op jit(solution)/shard_map/advance/pallas_call | solution.py:245
  31.0 0.2 collective-permute-start.12
  31.3 2.8 %collective-permute-start.13 = (bf16[3,32,1024]{2,1,0:T(8,128)(2,1)S(1)}, bf16[3,32,1024]{2,1,0:T(8,128)(2,1)S(1)}, u32[]{:S(2)}, u32[]{:S(2)}) collective-permute-start(bf16[3,32,1024]{2,1,0:T(8,128)(2,1)S(1)} %get-tuple-element.76), channel_id=1, source_target_pairs={{0,2},{1,3},{2,0},{3,1},{4,6},{5,7},{6,4},{7,5},{8,10},{9,11},{10,... | collective-permute-start | bytes 589832 | tf_op jit(solution)/shard_map/ppermute | solution.py:35
  34.1 0.8 %x_filter_0.1 = (bf16[2,9,32,128]{3,2,1,0:T(8,128)(2,1)S(1)}, bf16[2,9,32,128]{3,2,1,0:T(8,128)(2,1)S(1)}, bf16[2,9,32,128]{3,2,1,0:T(8,128)(2,1)S(1)}, bf16[2,9,32,128]{3,2,1,0:T(8,128)(2,1)S(1)}) custom-call(bf16[1024,1024]{1,0:T(8,128)(2,1)S(1)} %x_rows.1.matrix, bf16[3,32,1024]{2,1,0:T(8,128)(2,1)S(1)} %get-tuple-element.70.refs_0_), custom_call_target="tpu_custom_call" | custom-call | bytes 370000 | tf_op jit(solution)/shard_map/x_filter_0/pallas_call | solution.py:358
  34.9 1.6 %collective-permute-start.8 = (bf16[2,9,32,128]{3,2,1,0:T(8,128)(2,1)S(1)}, bf16[2,9,32,128]{3,2,1,0:T(8,128)(2,1)S(1)}, u32[]{:S(2)}, u32[]{:S(2)}) collective-permute-start(bf16[2,9,32,128]{3,2,1,0:T(8,128)(2,1)S(1)} %get-tuple-element.72), channel_id=1, source_target_pairs={{0,4},{4,0},{8,12},{12,8},{16,20},{20,16},{24,28},{28,24},{1,5},{5... | collective-permute-start | bytes 442376 | tf_op jit(solution)/shard_map/ppermute | solution.py:35
  36.5 1.5 %collective-permute-start.9 = (bf16[2,9,32,128]{3,2,1,0:T(8,128)(2,1)S(1)}, bf16[2,9,32,128]{3,2,1,0:T(8,128)(2,1)S(1)}, u32[]{:S(2)}, u32[]{:S(2)}) collective-permute-start(bf16[2,9,32,128]{3,2,1,0:T(8,128)(2,1)S(1)} %get-tuple-element.73), channel_id=1, source_target_pairs={{0,16},{4,20},{8,24},{12,28},{16,0},{20,4},{24,8},{28,12},{1,17},{... | collective-permute-start | bytes 442376 | tf_op jit(solution)/shard_map/ppermute | solution.py:35
  38.0 0.5 collective-permute-start.10
  38.5 3.1 %collective-permute-done.8.refs_3_ = bf16[2,9,32,128]{3,2,1,0:T(8,128)(2,1)S(1)} collective-permute-done((bf16[2,9,32,128]{3,2,1,0:T(8,128)(2,1)S(1)}, bf16[2,9,32,128]{3,2,1,0:T(8,128)(2,1)S(1)}, u32[]{:S(2)}, u32[]{:S(2)}) %collective-permute-start.8) | collective-permute-done | bytes 147488 | tf_op jit(solution)/shard_map/ppermute | solution.py:35
  41.5 0.6 collective-permute-start.17
  42.2 0.0 collective-permute-done.9.refs_4_
  42.2 1.9 %collective-permute-done.10.refs_5_ = bf16[2,9,32,128]{3,2,1,0:T(8,128)(2,1)S(1)} collective-permute-done((bf16[2,9,32,128]{3,2,1,0:T(8,128)(2,1)S(1)}, bf16[2,9,32,128]{3,2,1,0:T(8,128)(2,1)S(1)}, u32[]{:S(2)}, u32[]{:S(2)}) %collective-permute-start.10) | collective-permute-done | bytes 147488 | tf_op jit(solution)/shard_map/ppermute | solution.py:35
  44.1 0.0 collective-permute-done.12.refs_0_
  44.1 1.1 %collective-permute-done.13.refs_1_ = bf16[3,32,1024]{2,1,0:T(8,128)(2,1)S(1)} collective-permute-done((bf16[3,32,1024]{2,1,0:T(8,128)(2,1)S(1)}, bf16[3,32,1024]{2,1,0:T(8,128)(2,1)S(1)}, u32[]{:S(2)}, u32[]{:S(2)}) %collective-permute-start.13) | collective-permute-done | bytes 196640 | tf_op jit(solution)/shard_map/ppermute | solution.py:35
  45.2 1.4 %x_filter_1.1 = (bf16[2,9,64,128]{3,2,1,0:T(8,128)(2,1)S(1)}, bf16[2,9,64,128]{3,2,1,0:T(8,128)(2,1)S(1)}, bf16[2,9,64,128]{3,2,1,0:T(8,128)(2,1)S(1)}, bf16[2,9,64,128]{3,2,1,0:T(8,128)(2,1)S(1)}) custom-call(bf16[1024,1024]{1,0:T(8,128)(2,1)S(1)} %x_rows.1.matrix, bf16[3,32,1024]{2,1,0:T(8,128)(2,1)S(1)} %collective-permute-done.12.refs_0_, ...), custom_call_target="tpu_custom_call" | custom-call | bytes 370000 | tf_op jit(solution)/shard_map/x_filter_1/pallas_call | solution.py:358
  46.6 0.0 copy-start.2
  46.6 1.6 %collective-permute-start.14 = (bf16[2,9,64,128]{3,2,1,0:T(8,128)(2,1)S(1)}, bf16[2,9,64,128]{3,2,1,0:T(8,128)(2,1)S(1)}, u32[]{:S(2)}, u32[]{:S(2)}) collective-permute-start(bf16[2,9,64,128]{3,2,1,0:T(8,128)(2,1)S(1)} %get-tuple-element.82), channel_id=1, source_target_pairs={{0,4},{4,0},{8,12},{12,8},{16,20},{20,16},{24,28},{28,24},{1,5},{5... | collective-permute-start | bytes 884744 | tf_op jit(solution)/shard_map/ppermute | solution.py:35
  48.3 1.5 %collective-permute-start.15 = (bf16[2,9,64,128]{3,2,1,0:T(8,128)(2,1)S(1)}, bf16[2,9,64,128]{3,2,1,0:T(8,128)(2,1)S(1)}, u32[]{:S(2)}, u32[]{:S(2)}) collective-permute-start(bf16[2,9,64,128]{3,2,1,0:T(8,128)(2,1)S(1)} %get-tuple-element.83), channel_id=1, source_target_pairs={{0,16},{4,20},{8,24},{12,28},{16,0},{20,4},{24,8},{28,12},{1,17},{... | collective-permute-start | bytes 884744 | tf_op jit(solution)/shard_map/ppermute | solution.py:35
  49.7 0.5 collective-permute-start.16
  50.2 0.1 collective-permute-start.11
  50.3 0.0 collective-permute-done.17.refs_0_
  50.3 0.5 collective-permute-start.18
  50.8 1.3 %collective-permute-done.18.refs_1_ = bf16[3,32,1024]{2,1,0:T(8,128)(2,1)S(1)} collective-permute-done((bf16[3,32,1024]{2,1,0:T(8,128)(2,1)S(1)}, bf16[3,32,1024]{2,1,0:T(8,128)(2,1)S(1)}, u32[]{:S(2)}, u32[]{:S(2)}) %collective-permute-start.18) | collective-permute-done | bytes 196640 | tf_op jit(solution)/shard_map/ppermute | solution.py:35
  52.2 0.8 %x_filter_2.1 = (bf16[1,9,64,128]{3,2,1,0:T(8,128)(2,1)S(1)}, bf16[1,9,64,128]{3,2,1,0:T(8,128)(2,1)S(1)}, bf16[1,9,64,128]{3,2,1,0:T(8,128)(2,1)S(1)}, bf16[1,9,64,128]{3,2,1,0:T(8,128)(2,1)S(1)}) custom-call(bf16[1024,1024]{1,0:T(8,128)(2,1)S(1)} %x_rows.1.matrix, bf16[3,32,1024]{2,1,0:T(8,128)(2,1)S(1)} %collective-permute-done.17.refs_0_, ...), custom_call_target="tpu_custom_call" | custom-call | bytes 370000 | tf_op jit(solution)/shard_map/x_filter_2/pallas_call | solution.py:358
  53.0 1.6 %collective-permute-start.19 = (bf16[1,9,64,128]{3,2,1,0:T(8,128)(2,1)S(1)}, bf16[1,9,64,128]{3,2,1,0:T(8,128)(2,1)S(1)}, u32[]{:S(2)}, u32[]{:S(2)}) collective-permute-start(bf16[1,9,64,128]{3,2,1,0:T(8,128)(2,1)S(1)} %get-tuple-element.87), channel_id=1, source_target_pairs={{0,4},{4,0},{8,12},{12,8},{16,20},{20,16},{24,28},{28,24},{1,5},{5... | collective-permute-start | bytes 442376 | tf_op jit(solution)/shard_map/ppermute | solution.py:35
  54.6 3.5 %collective-permute-done.14.refs_8_ = bf16[2,9,64,128]{3,2,1,0:T(8,128)(2,1)S(1)} collective-permute-done((bf16[2,9,64,128]{3,2,1,0:T(8,128)(2,1)S(1)}, bf16[2,9,64,128]{3,2,1,0:T(8,128)(2,1)S(1)}, u32[]{:S(2)}, u32[]{:S(2)}) %collective-permute-start.14) | collective-permute-done | bytes 294944 | tf_op jit(solution)/shard_map/ppermute | solution.py:35
  58.1 0.0 collective-permute-start.20
  58.2 0.0 collective-permute-done.15.refs_9_
  58.2 0.5 collective-permute-start.21
  58.7 0.0 copy-done.2
  58.7 1.3 %z_lines.1 = (bf16[256,1024]{1,0:T(8,128)(2,1)S(1)}, bf16[512,1024]{1,0:T(8,128)(2,1)S(1)}, bf16[256,1024]{1,0:T(8,128)(2,1)S(1)}) custom-call(s32[3]{0:T(128)S(1)} %pad_add_fusion.place_ref, bf16[1024,1024]{1,0:T(8,128)(2,1)S(1)} %copy-done.2), custom_call_target="tpu_custom_call" | custom-call | bytes 11100000 | tf_op jit(solution)/shard_map/z_lines/pallas_call | solution.py:341
  60.0 2.9 %collective-permute-done.16.refs_10_ = bf16[2,9,64,128]{3,2,1,0:T(8,128)(2,1)S(1)} collective-permute-done((bf16[2,9,64,128]{3,2,1,0:T(8,128)(2,1)S(1)}, bf16[2,9,64,128]{3,2,1,0:T(8,128)(2,1)S(1)}, u32[]{:S(2)}, u32[]{:S(2)}) %collective-permute-start.16) | collective-permute-done | bytes 294944 | tf_op jit(solution)/shard_map/ppermute | solution.py:35
  62.9 0.0 collective-permute-done.11.refs_6_
  62.9 1.4 %z_filter_first.1.passed = f32[9,128,1024]{2,1,0:T(8,128)S(1)} custom-call(bf16[256,1024]{1,0:T(8,128)(2,1)S(1)} %get-tuple-element.49.refs_0_, bf16[512,1024]{1,0:T(8,128)(2,1)S(1)} %get-tuple-element.50.refs_1_.line_second, bf16[2,9,32,128]{3,2,1,0:T(8,128)(2,1)S(1)} %get-tuple-element.71.refs_2_, ...), custom_call_target="tpu_custom_call" | custom-call | bytes 370000 | tf_op jit(solution)/shard_map/z_filter_first/pallas_call | solution.py:386
  64.3 0.1 pad_maximum_fusion
  64.4 0.1 collective-permute-done.19.refs_1_
  64.5 0.0 collective-permute-done.20.refs_2_
  64.5 1.8 %collective-permute-done.21.refs_3_ = bf16[1,9,64,128]{3,2,1,0:T(8,128)(2,1)S(1)} collective-permute-done((bf16[1,9,64,128]{3,2,1,0:T(8,128)(2,1)S(1)}, bf16[1,9,64,128]{3,2,1,0:T(8,128)(2,1)S(1)}, u32[]{:S(2)}, u32[]{:S(2)}) %collective-permute-start.21) | collective-permute-done | bytes 147488 | tf_op jit(solution)/shard_map/ppermute | solution.py:35
  66.3 0.0 collective-permute-start.22
  66.3 2.0 %collective-permute-done.22.others = bf16[4,9,64,128]{3,2,1,0:T(8,128)(2,1)S(1)} collective-permute-done((bf16[4,9,64,128]{3,2,1,0:T(8,128)(2,1)S(1)}, bf16[4,9,64,128]{3,2,1,0:T(8,128)(2,1)S(1)}, u32[]{:S(2)}, u32[]{:S(2)}) %collective-permute-start.22) | collective-permute-done | bytes 589856 | tf_op jit(solution)/shard_map/ppermute | solution.py:35
  68.3 2.7 %z_filter_last.1 = f32[6,1,128,1024]{3,2,1,0:T(8,128)} custom-call(f32[9,128,1024]{2,1,0:T(8,128)S(1)} %z_filter_first.1.passed, bf16[512,1024]{1,0:T(8,128)(2,1)S(1)} %get-tuple-element.50.refs_1_.line_second, bf16[256,1024]{1,0:T(8,128)(2,1)S(1)} %get-tuple-element.85.line_last, bf16[4,9,64,128]{3,2,1,0:T(8,128)(2,1)S(1)} %collective-permute-done.22.others, ...), custom_call_target="tpu_custom_call" | custom-call | bytes 370000 | tf_op jit(solution)/shard_map/z_filter_last/pallas_call | solution.py:396
  (15 shorter events, 0.2 us)
Async XLA Ops:
  1.3 25.0 %collective-permute-start.4 = (bf16[3,32,1024]{2,1,0:T(8,128)(2,1)S(1)}, bf16[3,32,1024]{2,1,0:T(8,128)(2,1)S(1)}, u32[]{:S(2)}, u32[]{:S(2)}) collective-permute-start(bf16[3,32,1024]{2,1,0:T(8,128)(2,1)S(1)} %get-tuple-element.93), channel_id=1, source_target_pairs={{0,3},{1,2},{2,1},{3,0},{4,7},{5,6},{6,5},{7,4},{8,11},{9,10},{10,... | collective-permute-start | bytes 589832 | tf_op jit(solution)/shard_map/ppermute | solution.py:35
  6.4 19.9 %collective-permute-start.3 = (bf16[3,32,1024]{2,1,0:T(8,128)(2,1)S(1)}, bf16[3,32,1024]{2,1,0:T(8,128)(2,1)S(1)}, u32[]{:S(2)}, u32[]{:S(2)}) collective-permute-start(bf16[3,32,1024]{2,1,0:T(8,128)(2,1)S(1)} %get-tuple-element.94), channel_id=1, source_target_pairs={{0,2},{1,3},{2,0},{3,1},{4,6},{5,7},{6,4},{7,5},{8,10},{9,11},{10,... | collective-permute-start | bytes 589832 | tf_op jit(solution)/shard_map/ppermute | solution.py:35
  6.4 13.5 %collective-permute-start.2 = (bf16[3,32,1024]{2,1,0:T(8,128)(2,1)S(1)}, bf16[3,32,1024]{2,1,0:T(8,128)(2,1)S(1)}, u32[]{:S(2)}, u32[]{:S(2)}) collective-permute-start(bf16[3,32,1024]{2,1,0:T(8,128)(2,1)S(1)} %get-tuple-element.95), channel_id=1, source_target_pairs={{0,1},{1,0},{2,3},{3,2},{4,5},{5,4},{6,7},{7,6},{8,9},{9,8},{10,11... | collective-permute-start | bytes 589832 | tf_op jit(solution)/shard_map/ppermute | solution.py:35
  7.1 1.4 %copy-start.1 = (f32[3,1,128,1024]{3,2,1,0:T(8,128)S(1)}, f32[3,1,128,1024]{3,2,1,0:T(8,128)}, u32[]{:S(2)}) copy-start(f32[3,1,128,1024]{3,2,1,0:T(8,128)} %velocity.1) | copy-start | bytes 4718596
  8.8 4.1 %collective-permute-start = (bf16[3,24,128]{2,1,0:T(8,128)(2,1)S(1)}, bf16[3,24,128]{2,1,0:T(8,128)(2,1)S(1)}, u32[]{:S(2)}, u32[]{:S(2)}) collective-permute-start(bf16[3,24,128]{2,1,0:T(8,128)(2,1)S(1)} %get-tuple-element.53), channel_id=1, source_target_pairs={{0,4},{4,8},{8,12},{12,16},{16,20},{20,24},{24,28},{28,0},{1,5},{5... | collective-permute-start | bytes 55304 | tf_op jit(solution)/shard_map/ppermute | solution.py:230
  10.5 3.8 %collective-permute-start.1 = (bf16[3,24,128]{2,1,0:T(8,128)(2,1)S(1)}, bf16[3,24,128]{2,1,0:T(8,128)(2,1)S(1)}, u32[]{:S(2)}, u32[]{:S(2)}) collective-permute-start(bf16[3,24,128]{2,1,0:T(8,128)(2,1)S(1)} %get-tuple-element.54), channel_id=1, source_target_pairs={{4,0},{8,4},{12,8},{16,12},{20,16},{24,20},{28,24},{0,28},{5,1},{9... | collective-permute-start | bytes 55304 | tf_op jit(solution)/shard_map/ppermute | solution.py:231
  14.4 11.0 %collective-permute-start.7 = (bf16[3,48,128]{2,1,0:T(8,128)(2,1)S(1)}, bf16[3,48,128]{2,1,0:T(8,128)(2,1)S(1)}, u32[]{:S(2)}, u32[]{:S(2)}) collective-permute-start(bf16[3,48,128]{2,1,0:T(8,128)(2,1)S(1)} %get-tuple-element.96), channel_id=1, source_target_pairs={{0,3},{1,2},{2,1},{3,0},{4,7},{5,6},{6,5},{7,4},{8,11},{9,10},{10,... | collective-permute-start | bytes 110600 | tf_op jit(solution)/shard_map/ppermute | solution.py:35
  18.1 8.3 %collective-permute-start.6 = (bf16[3,48,128]{2,1,0:T(8,128)(2,1)S(1)}, bf16[3,48,128]{2,1,0:T(8,128)(2,1)S(1)}, u32[]{:S(2)}, u32[]{:S(2)}) collective-permute-start(bf16[3,48,128]{2,1,0:T(8,128)(2,1)S(1)} %get-tuple-element.97), channel_id=1, source_target_pairs={{0,2},{1,3},{2,0},{3,1},{4,6},{5,7},{6,4},{7,5},{8,10},{9,11},{10,... | collective-permute-start | bytes 110600 | tf_op jit(solution)/shard_map/ppermute | solution.py:35
  19.9 6.4 %collective-permute-start.5 = (bf16[3,48,128]{2,1,0:T(8,128)(2,1)S(1)}, bf16[3,48,128]{2,1,0:T(8,128)(2,1)S(1)}, u32[]{:S(2)}, u32[]{:S(2)}) collective-permute-start(bf16[3,48,128]{2,1,0:T(8,128)(2,1)S(1)} %get-tuple-element.58), channel_id=1, source_target_pairs={{0,1},{1,0},{2,3},{3,2},{4,5},{5,4},{6,7},{7,6},{8,9},{9,8},{10,11... | collective-permute-start | bytes 110600 | tf_op jit(solution)/shard_map/ppermute | solution.py:35
  22.5 2.2 %copy-start = (bf16[2,1024,1024]{2,1,0:T(8,128)(2,1)S(1)}, bf16[2,1024,1024]{2,1,0:T(8,128)(2,1)}, u32[]{:S(2)}) copy-start(bf16[2,1024,1024]{2,1,0:T(8,128)(2,1)} %x_filters.1) | copy-start | bytes 12582916
  31.0 13.0 %collective-permute-start.12 = (bf16[3,32,1024]{2,1,0:T(8,128)(2,1)S(1)}, bf16[3,32,1024]{2,1,0:T(8,128)(2,1)S(1)}, u32[]{:S(2)}, u32[]{:S(2)}) collective-permute-start(bf16[3,32,1024]{2,1,0:T(8,128)(2,1)S(1)} %get-tuple-element.75), channel_id=1, source_target_pairs={{0,1},{1,0},{2,3},{3,2},{4,5},{5,4},{6,7},{7,6},{8,9},{9,8},{10,11... | collective-permute-start | bytes 589832 | tf_op jit(solution)/shard_map/ppermute | solution.py:35
  31.3 13.9 %collective-permute-start.13 = (bf16[3,32,1024]{2,1,0:T(8,128)(2,1)S(1)}, bf16[3,32,1024]{2,1,0:T(8,128)(2,1)S(1)}, u32[]{:S(2)}, u32[]{:S(2)}) collective-permute-start(bf16[3,32,1024]{2,1,0:T(8,128)(2,1)S(1)} %get-tuple-element.76), channel_id=1, source_target_pairs={{0,2},{1,3},{2,0},{3,1},{4,6},{5,7},{6,4},{7,5},{8,10},{9,11},{10,... | collective-permute-start | bytes 589832 | tf_op jit(solution)/shard_map/ppermute | solution.py:35
  34.9 6.6 %collective-permute-start.8 = (bf16[2,9,32,128]{3,2,1,0:T(8,128)(2,1)S(1)}, bf16[2,9,32,128]{3,2,1,0:T(8,128)(2,1)S(1)}, u32[]{:S(2)}, u32[]{:S(2)}) collective-permute-start(bf16[2,9,32,128]{3,2,1,0:T(8,128)(2,1)S(1)} %get-tuple-element.72), channel_id=1, source_target_pairs={{0,4},{4,0},{8,12},{12,8},{16,20},{20,16},{24,28},{28,24},{1,5},{5... | collective-permute-start | bytes 442376 | tf_op jit(solution)/shard_map/ppermute | solution.py:35
  36.5 5.7 %collective-permute-start.9 = (bf16[2,9,32,128]{3,2,1,0:T(8,128)(2,1)S(1)}, bf16[2,9,32,128]{3,2,1,0:T(8,128)(2,1)S(1)}, u32[]{:S(2)}, u32[]{:S(2)}) collective-permute-start(bf16[2,9,32,128]{3,2,1,0:T(8,128)(2,1)S(1)} %get-tuple-element.73), channel_id=1, source_target_pairs={{0,16},{4,20},{8,24},{12,28},{16,0},{20,4},{24,8},{28,12},{1,17},{... | collective-permute-start | bytes 442376 | tf_op jit(solution)/shard_map/ppermute | solution.py:35
  38.0 6.1 %collective-permute-start.10 = (bf16[2,9,32,128]{3,2,1,0:T(8,128)(2,1)S(1)}, bf16[2,9,32,128]{3,2,1,0:T(8,128)(2,1)S(1)}, u32[]{:S(2)}, u32[]{:S(2)}) collective-permute-start(bf16[2,9,32,128]{3,2,1,0:T(8,128)(2,1)S(1)} %get-tuple-element.74), channel_id=1, source_target_pairs={{0,20},{4,16},{8,28},{12,24},{16,4},{20,0},{24,12},{28,8},{1,21},{... | collective-permute-start | bytes 442376 | tf_op jit(solution)/shard_map/ppermute | solution.py:35
  41.5 8.8 %collective-permute-start.17 = (bf16[3,32,1024]{2,1,0:T(8,128)(2,1)S(1)}, bf16[3,32,1024]{2,1,0:T(8,128)(2,1)S(1)}, u32[]{:S(2)}, u32[]{:S(2)}) collective-permute-start(bf16[3,32,1024]{2,1,0:T(8,128)(2,1)S(1)} %get-tuple-element.86), channel_id=1, source_target_pairs={{0,3},{1,2},{2,1},{3,0},{4,7},{5,6},{6,5},{7,4},{8,11},{9,10},{10,... | collective-permute-start | bytes 589832 | tf_op jit(solution)/shard_map/ppermute | solution.py:35
  46.6 12.0 %copy-start.2 = (bf16[1024,1024]{1,0:T(8,128)(2,1)S(1)}, bf16[1024,1024]{1,0:T(8,128)(2,1)}, u32[]{:S(2)}) copy-start(bf16[1024,1024]{1,0:T(8,128)(2,1)} %z_filter.1) | copy-start | bytes 6291460
  46.6 11.5 %collective-permute-start.14 = (bf16[2,9,64,128]{3,2,1,0:T(8,128)(2,1)S(1)}, bf16[2,9,64,128]{3,2,1,0:T(8,128)(2,1)S(1)}, u32[]{:S(2)}, u32[]{:S(2)}) collective-permute-start(bf16[2,9,64,128]{3,2,1,0:T(8,128)(2,1)S(1)} %get-tuple-element.82), channel_id=1, source_target_pairs={{0,4},{4,0},{8,12},{12,8},{16,20},{20,16},{24,28},{28,24},{1,5},{5... | collective-permute-start | bytes 884744 | tf_op jit(solution)/shard_map/ppermute | solution.py:35
  48.3 9.9 %collective-permute-start.15 = (bf16[2,9,64,128]{3,2,1,0:T(8,128)(2,1)S(1)}, bf16[2,9,64,128]{3,2,1,0:T(8,128)(2,1)S(1)}, u32[]{:S(2)}, u32[]{:S(2)}) collective-permute-start(bf16[2,9,64,128]{3,2,1,0:T(8,128)(2,1)S(1)} %get-tuple-element.83), channel_id=1, source_target_pairs={{0,16},{4,20},{8,24},{12,28},{16,0},{20,4},{24,8},{28,12},{1,17},{... | collective-permute-start | bytes 884744 | tf_op jit(solution)/shard_map/ppermute | solution.py:35
  49.7 13.1 %collective-permute-start.16 = (bf16[2,9,64,128]{3,2,1,0:T(8,128)(2,1)S(1)}, bf16[2,9,64,128]{3,2,1,0:T(8,128)(2,1)S(1)}, u32[]{:S(2)}, u32[]{:S(2)}) collective-permute-start(bf16[2,9,64,128]{3,2,1,0:T(8,128)(2,1)S(1)} %get-tuple-element.84), channel_id=1, source_target_pairs={{0,20},{4,16},{8,28},{12,24},{16,4},{20,0},{24,12},{28,8},{1,21},{... | collective-permute-start | bytes 884744 | tf_op jit(solution)/shard_map/ppermute | solution.py:35
  50.2 12.7 %collective-permute-start.11 = (bf16[4,9,32,128]{3,2,1,0:T(8,128)(2,1)S(1)}, bf16[4,9,32,128]{3,2,1,0:T(8,128)(2,1)S(1)}, u32[]{:S(2)}, u32[]{:S(2)}) collective-permute-start(bf16[4,9,32,128]{3,2,1,0:T(8,128)(2,1)S(1)} %pad_maximum_fusion.1), channel_id=1, source_target_pairs={{0,8},{8,0},{16,24},{24,16},{1,9},{9,1},{17,25},{25,17},{2,10},{10... | collective-permute-start | bytes 884744 | tf_op jit(solution)/shard_map/ppermute | solution.py:35
  50.3 1.8 %collective-permute-start.18 = (bf16[3,32,1024]{2,1,0:T(8,128)(2,1)S(1)}, bf16[3,32,1024]{2,1,0:T(8,128)(2,1)S(1)}, u32[]{:S(2)}, u32[]{:S(2)}) collective-permute-start(bf16[3,32,1024]{2,1,0:T(8,128)(2,1)S(1)} %collective-permute-done.17.refs_0_), channel_id=1, source_target_pairs={{0,8},{8,0},{16,24},{24,16},{1,9},{9,1},{17,25},{25,17},{2,10},{10... | collective-permute-start | bytes 589832 | tf_op jit(solution)/shard_map/ppermute | solution.py:35
  53.0 11.5 %collective-permute-start.19 = (bf16[1,9,64,128]{3,2,1,0:T(8,128)(2,1)S(1)}, bf16[1,9,64,128]{3,2,1,0:T(8,128)(2,1)S(1)}, u32[]{:S(2)}, u32[]{:S(2)}) collective-permute-start(bf16[1,9,64,128]{3,2,1,0:T(8,128)(2,1)S(1)} %get-tuple-element.87), channel_id=1, source_target_pairs={{0,4},{4,0},{8,12},{12,8},{16,20},{20,16},{24,28},{28,24},{1,5},{5... | collective-permute-start | bytes 442376 | tf_op jit(solution)/shard_map/ppermute | solution.py:35
  58.1 6.3 %collective-permute-start.20 = (bf16[1,9,64,128]{3,2,1,0:T(8,128)(2,1)S(1)}, bf16[1,9,64,128]{3,2,1,0:T(8,128)(2,1)S(1)}, u32[]{:S(2)}, u32[]{:S(2)}) collective-permute-start(bf16[1,9,64,128]{3,2,1,0:T(8,128)(2,1)S(1)} %get-tuple-element.88), channel_id=1, source_target_pairs={{0,16},{4,20},{8,24},{12,28},{16,0},{20,4},{24,8},{28,12},{1,17},{... | collective-permute-start | bytes 442376 | tf_op jit(solution)/shard_map/ppermute | solution.py:35
  58.2 8.1 %collective-permute-start.21 = (bf16[1,9,64,128]{3,2,1,0:T(8,128)(2,1)S(1)}, bf16[1,9,64,128]{3,2,1,0:T(8,128)(2,1)S(1)}, u32[]{:S(2)}, u32[]{:S(2)}) collective-permute-start(bf16[1,9,64,128]{3,2,1,0:T(8,128)(2,1)S(1)} %get-tuple-element.90), channel_id=1, source_target_pairs={{0,20},{4,16},{8,28},{12,24},{16,4},{20,0},{24,12},{28,8},{1,21},{... | collective-permute-start | bytes 442376 | tf_op jit(solution)/shard_map/ppermute | solution.py:35
  66.3 2.0 %collective-permute-start.22 = (bf16[4,9,64,128]{3,2,1,0:T(8,128)(2,1)S(1)}, bf16[4,9,64,128]{3,2,1,0:T(8,128)(2,1)S(1)}, u32[]{:S(2)}, u32[]{:S(2)}) collective-permute-start(bf16[4,9,64,128]{3,2,1,0:T(8,128)(2,1)S(1)} %pad_maximum_fusion), channel_id=1, source_target_pairs={{0,8},{8,0},{16,24},{24,16},{1,9},{9,1},{17,25},{25,17},{2,10},{10... | collective-permute-start | bytes 1769480 | tf_op jit(solution)/shard_map/ppermute | solution.py:35
